TPU v7x, 256 devices: a whole 4x4x8 slice. The times are simulated.
256 devices in a mesh: rows: 256 (over x, z, y, core).
Axes of the slice: x: 4, y: 4, z: 8, core: 2. Of those that a mesh axis runs over, the one named last changes fastest.
Arguments:
- x_states: bfloat16 [131072, 2048], P('rows'), may hold values from -6 to 6
- h_blocks: bfloat16 [1024, 12, 128, 128], P('rows'), may hold values from -0.15625 to 0.15625
- col_blocks: int32 [1024, 12], P('rows'), may hold values from 0 to 1023, as said below
- send_list: int32 [256, 4, 4], replicated, may hold values from 0 to 4, as said below
- center: float32 [1], replicated, may hold values from 0.2 to 0.6
- half_width: float32 [1], replicated, may hold values from 1 to 1.5
- rotation: bfloat16 [2048, 2048], P('rows'), may hold values from -0.125 to 0.125
Outputs:
- rotated: bfloat16 [131072, 2048], P('rows')
Inputs may be any that keep to these rules, and one draw needn't show every extreme that they name: `col_blocks`: row block b names 12 distinct column blocks (b + t) modulo 1024 with -(6) <= t <= 6, among them those with t = 0, 1, -1, 4, -4, 5 and -5. send_list[o, j] lists in ascending order each p for which block o * 4 + p is named by some row block of the device at offset 1, 2, -1, -2 (j = 0, 1, 2, 3) from device o, modulo the number of devices, and 4 in the remaining places; the lists for offsets 1 and -1 are always full, those for offsets 2 and -2 hold at most 2 blocks, and some device's hold 2.
All inputs are finite; a program needn't handle non-finite values.
Results may differ from a plain program's by a relative error of at most 0.0056.
Values may be sent and summed in bfloat16 or wider, within the bound.
No kernel may reach another device: no remote copies, remote signals or barrier semaphores. Data moves between devices by JAX's collectives and lax.ppermute only.
A program may use at most 128 MiB of HBM per device.

v0:
```python
import jax
import jax.numpy as jnp
from jax import lax
from jax.sharding import PartitionSpec as P


def shifted(block, axis, distance):
    devices = range(lax.axis_size(axis))
    route = [((i - distance) % len(devices), i) for i in devices]
    return lax.ppermute(block, axis, route)


def local(x_states, h_blocks, col_blocks, send_list, center, half_width, rotation):
    axis_count = lax.axis_size("rows")
    device = lax.axis_index("rows")
    row_count, block_count = col_blocks.shape
    block_size = h_blocks.shape[2]
    width = x_states.shape[1]
    owner_device = col_blocks // row_count
    local_index = col_blocks - owner_device * row_count
    offset = jnp.mod(device - owner_device + 2, axis_count) - 2
    list_slot = jnp.clip(jnp.where(offset > 0, offset - 1, 1 - offset), 0, 3)
    listed = send_list[owner_device, list_slot]
    matches = listed == local_index[..., None]
    available = jnp.any(matches, axis=-1) | (offset == 0)
    masked = h_blocks * available[..., None, None].astype(h_blocks.dtype)
    h_rows = masked.transpose(0, 2, 1, 3).reshape(row_count, block_size, block_count * block_size)
    bases = jnp.array([row_count, 2 * row_count, 3 * row_count, 4 * row_count], jnp.int32)
    sources = jnp.where(offset == 0, local_index, bases[list_slot] + local_index)

    def neighbours(blocks):
        received = []
        for shift_by in (1, 2, -1, -2):
            received.append(shifted(blocks, "rows", shift_by))
        return received

    def product(blocks):
        block_pool = jnp.concatenate([blocks] + neighbours(blocks), 0)

        def one_row(operands):
            row_blocks, row_sources = operands
            picked = block_pool[row_sources].reshape(block_count * block_size, width)
            return jnp.dot(row_blocks, picked, preferred_element_type=jnp.float32)

        return lax.map(one_row, (h_rows, sources))

    center_value = center[0]
    half_value = half_width[0]
    x_blocks = x_states.reshape(row_count, block_size, width)
    x_wide = x_blocks.astype(jnp.float32)
    first_pass = ((product(x_blocks) - center_value * x_wide) / half_value).astype(jnp.bfloat16)
    second_term = product(first_pass) - center_value * first_pass.astype(jnp.float32)
    second_pass = (2.0 * second_term / half_value - x_wide).astype(jnp.bfloat16)
    flattened = second_pass.reshape(row_count * block_size, width)
    rotated = jnp.dot(
        flattened,
        lax.all_gather(rotation, "rows", axis=0, tiled=True),
        preferred_element_type=jnp.float32,
    )
    return rotated.astype(jnp.bfloat16)


def solution(mesh):
    placed = (
        P("rows", None),
        P("rows", None, None, None),
        P("rows", None),
        P(),
        P(),
        P(),
        P("rows", None),
    )
    return jax.shard_map(
        local, mesh=mesh, in_specs=placed, out_specs=P("rows", None), check_vma=False
    )
```

profile of v0, /device:TPU:1, one launch (start us, length us, event | category | flops | bytes accessed | tf_op | source)
XLA Modules:
  0.0 308.0 jit_solution(10346603999486924348)
XLA Ops:
  6.5 0.7 all-gather.2.cloned.1.call-update
  7.3 2.8 collective-permute-start
  10.0 1.3 collective-permute-start.1
  11.3 7.9 %collective-permute-start.3 = (bf16[4,128,2048]{2,1,0:T(8,128)(2,1)}, bf16[4,128,2048]{2,1,0:T(8,128)(2,1)}, u32[]{:S(2)}, u32[]{:S(2)}) collective-permute-start(bf16[4,128,2048]{2,1,0:T(8,128)(2,1)} %bitcast.78), channel_id=1, source_target_pairs={{2,0},{3,1},{4,2},{5,3},{6,4},{7,5},{8,6},{9,7},{10,8},{11,9},{12,... | collective-permute-start | bytes 6291464 | tf_op jit(solution)/shard_map/ppermute | solution.py:10
  19.2 0.7 compare_select_fusion.2
  20.0 1.4 gather_fusion.3
  21.6 0.7 add_select_fusion
  22.4 1.0 copy.11
  23.3 0.9 gather_fusion.2
  24.4 1.9 copy.13
  26.4 0.2 broadcast_multiply_fusion
  26.5 0.7 copy.15
  28.6 1.7 constant_dynamic-update-slice_fusion.4
  30.3 25.0 %collective-permute-done = bf16[4,128,2048]{2,1,0:T(8,128)(2,1)} collective-permute-done((bf16[4,128,2048]{2,1,0:T(8,128)(2,1)}, bf16[4,128,2048]{2,1,0:T(8,128)(2,1)}, u32[]{:S(2)}, u32[]{:S(2)}) %collective-permute-start) | collective-permute-done | bytes 2097184 | tf_op jit(solution)/shard_map/ppermute | solution.py:10
  55.3 1.7 constant_dynamic-update-slice_fusion.3
  57.1 32.6 %collective-permute-done.1 = bf16[4,128,2048]{2,1,0:T(8,128)(2,1)} collective-permute-done((bf16[4,128,2048]{2,1,0:T(8,128)(2,1)}, bf16[4,128,2048]{2,1,0:T(8,128)(2,1)}, u32[]{:S(2)}, u32[]{:S(2)}) %collective-permute-start.1) | collective-permute-done | bytes 2097184 | tf_op jit(solution)/shard_map/ppermute | solution.py:10
  89.7 1.7 constant_dynamic-update-slice_fusion.2
  91.5 1.7 constant_dynamic-update-slice_fusion.1
  93.2 1.7 constant_dynamic-update-slice_fusion
  94.9 2.8 broadcast.67.clone
  97.7 2.5 copy-done.1
  100.2 53.0 %while.20 = (s32[]{:T(128)}, f32[4,128,2048]{2,1,0:T(8,128)}, bf16[4,128,1536]{2,1,0:T(8,128)(2,1)S(1)}, s32[4,12]{1,0:T(4,128)S(1)}, bf16[20,128,2048]{2,1,0:T(8,128)(2,1)}, /*index=5*/s32[]{:T(128)}) while((s32[]{:T(128)}, f32[4,128,2048]{2,1,0:T(8,128)}, bf16[4,128,1536]{2,1,0:T(8,128)(2,1)S(1)}, s32[4,12]{1,0:T(4,128)S(1)}, ...), condition=%wide.region_2.3_spmd, body=%wide.region_1.2_spmd.sunk | while | flops 805307456 | bytes 20321544 | solution.py:45
  100.3 8.1 %gather_fusion = bf16[12,128,2048]{2,1,0:T(8,128)(2,1)} fusion(bf16[20,128,2048]{2,1,0:T(8,128)(2,1)} %get-tuple-element.177, s32[1024]{0:T(1024)S(1)} %pad_clamp_fusion.5), kind=kCustom, calls=%fused_computation.clone.1 | custom fusion | bytes 12582960 | tf_op jit(solution)/shard_map/while/body/eval_jaxpr/gather | solution.py:42
  108.4 5.0 %fusion.38 = f32[4,128,2048]{2,1,0:T(8,128)} fusion(f32[4,128,2048]{2,1,0:T(8,128)} %get-tuple-element.168, s32[]{:T(128)} %get-tuple-element.167, bf16[1536,2048]{1,0:T(8,128)(2,1)} %bitcast.73, bf16[4,128,1536]{2,1,0:T(8,128)(2,1)S(1)} %get-tuple-element.175), kind=kOutput, calls=%fused_computation.5.clone.1 | convolution fusion | flops 805306368 | bytes 7734272 | tf_op jit(solution)/shard_map/while/body/eval_jaxpr/dot_general | solution.py:43
  113.4 8.5 %gather_fusion = bf16[12,128,2048]{2,1,0:T(8,128)(2,1)} fusion(bf16[20,128,2048]{2,1,0:T(8,128)(2,1)} %get-tuple-element.177, s32[1024]{0:T(1024)S(1)} %pad_clamp_fusion.5), kind=kCustom, calls=%fused_computation.clone.1 | custom fusion | bytes 12582960 | tf_op jit(solution)/shard_map/while/body/eval_jaxpr/gather | solution.py:42
  121.9 5.1 %fusion.38 = f32[4,128,2048]{2,1,0:T(8,128)} fusion(f32[4,128,2048]{2,1,0:T(8,128)} %get-tuple-element.168, s32[]{:T(128)} %get-tuple-element.167, bf16[1536,2048]{1,0:T(8,128)(2,1)} %bitcast.73, bf16[4,128,1536]{2,1,0:T(8,128)(2,1)S(1)} %get-tuple-element.175), kind=kOutput, calls=%fused_computation.5.clone.1 | convolution fusion | flops 805306368 | bytes 7734272 | tf_op jit(solution)/shard_map/while/body/eval_jaxpr/dot_general | solution.py:43
  127.0 8.3 %gather_fusion = bf16[12,128,2048]{2,1,0:T(8,128)(2,1)} fusion(bf16[20,128,2048]{2,1,0:T(8,128)(2,1)} %get-tuple-element.177, s32[1024]{0:T(1024)S(1)} %pad_clamp_fusion.5), kind=kCustom, calls=%fused_computation.clone.1 | custom fusion | bytes 12582960 | tf_op jit(solution)/shard_map/while/body/eval_jaxpr/gather | solution.py:42
  135.3 5.0 %fusion.38 = f32[4,128,2048]{2,1,0:T(8,128)} fusion(f32[4,128,2048]{2,1,0:T(8,128)} %get-tuple-element.168, s32[]{:T(128)} %get-tuple-element.167, bf16[1536,2048]{1,0:T(8,128)(2,1)} %bitcast.73, bf16[4,128,1536]{2,1,0:T(8,128)(2,1)S(1)} %get-tuple-element.175), kind=kOutput, calls=%fused_computation.5.clone.1 | convolution fusion | flops 805306368 | bytes 7734272 | tf_op jit(solution)/shard_map/while/body/eval_jaxpr/dot_general | solution.py:43
  140.3 8.1 %gather_fusion = bf16[12,128,2048]{2,1,0:T(8,128)(2,1)} fusion(bf16[20,128,2048]{2,1,0:T(8,128)(2,1)} %get-tuple-element.177, s32[1024]{0:T(1024)S(1)} %pad_clamp_fusion.5), kind=kCustom, calls=%fused_computation.clone.1 | custom fusion | bytes 12582960 | tf_op jit(solution)/shard_map/while/body/eval_jaxpr/gather | solution.py:42
  148.4 4.8 %fusion.38 = f32[4,128,2048]{2,1,0:T(8,128)} fusion(f32[4,128,2048]{2,1,0:T(8,128)} %get-tuple-element.168, s32[]{:T(128)} %get-tuple-element.167, bf16[1536,2048]{1,0:T(8,128)(2,1)} %bitcast.73, bf16[4,128,1536]{2,1,0:T(8,128)(2,1)S(1)} %get-tuple-element.175), kind=kOutput, calls=%fused_computation.5.clone.1 | convolution fusion | flops 805306368 | bytes 7734272 | tf_op jit(solution)/shard_map/while/body/eval_jaxpr/dot_general | solution.py:43
  153.2 3.8 %constant_dynamic-update-slice_fusion.9 = (bf16[20,128,2048]{2,1,0:T(8,128)(2,1)S(1)}, bf16[4,128,2048]{2,1,0:T(8,128)(2,1)S(1)}) fusion(f32[]{:T(128)} %bitcast.71, f32[4,128,2048]{2,1,0:T(8,128)} %get-tuple-element.59, bf16[4,128,2048]{2,1,0:T(8,128)(2,1)} %bitcast.80, f32[]{:T(128)} %bitcast.69), kind=kLoop, calls=%fused_computation.41 | loop fusion | flops 5242879 | bytes 10485768
  157.2 0.4 collective-permute-start.6
  157.6 7.2 %collective-permute-start.7 = (bf16[4,128,2048]{2,1,0:T(8,128)(2,1)S(1)}, bf16[4,128,2048]{2,1,0:T(8,128)(2,1)S(1)}, u32[]{:S(2)}, u32[]{:S(2)}) collective-permute-start(bf16[4,128,2048]{2,1,0:T(8,128)(2,1)S(1)} %get-tuple-element.92), channel_id=1, source_target_pairs={{2,0},{3,1},{4,2},{5,3},{6,4},{7,5},{8,6},{9,7},{10,8},{11,9},{12,... | collective-permute-start | bytes 6291464 | tf_op jit(solution)/shard_map/ppermute | solution.py:10
  164.8 37.1 %collective-permute-done.4 = bf16[4,128,2048]{2,1,0:T(8,128)(2,1)S(1)} collective-permute-done((bf16[4,128,2048]{2,1,0:T(8,128)(2,1)S(1)}, bf16[4,128,2048]{2,1,0:T(8,128)(2,1)S(1)}, u32[]{:S(2)}, u32[]{:S(2)}) %collective-permute-start.4) | collective-permute-done | bytes 2097184 | tf_op jit(solution)/shard_map/ppermute | solution.py:10
  202.0 28.0 %collective-permute-done.5 = bf16[4,128,2048]{2,1,0:T(8,128)(2,1)S(1)} collective-permute-done((bf16[4,128,2048]{2,1,0:T(8,128)(2,1)S(1)}, bf16[4,128,2048]{2,1,0:T(8,128)(2,1)S(1)}, u32[]{:S(2)}, u32[]{:S(2)}) %collective-permute-start.5) | collective-permute-done | bytes 2097184 | tf_op jit(solution)/shard_map/ppermute | solution.py:10
  230.5 2.8 broadcast.67
  233.3 2.5 copy-done
  235.8 51.7 %while.21 = (s32[]{:T(128)}, f32[4,128,2048]{2,1,0:T(8,128)}, bf16[4,128,1536]{2,1,0:T(8,128)(2,1)S(1)}, s32[4,12]{1,0:T(4,128)S(1)}, bf16[20,128,2048]{2,1,0:T(8,128)(2,1)}, /*index=5*/s32[]{:T(128)}) while((s32[]{:T(128)}, f32[4,128,2048]{2,1,0:T(8,128)}, bf16[4,128,1536]{2,1,0:T(8,128)(2,1)S(1)}, s32[4,12]{1,0:T(4,128)S(1)}, ...), condition=%wide.region_4.5_spmd, body=%wide.region_3.4_spmd.sunk | while | flops 805307456 | bytes 20321544 | solution.py:45
  235.8 8.1 %gather_fusion.1 = bf16[12,128,2048]{2,1,0:T(8,128)(2,1)} fusion(bf16[20,128,2048]{2,1,0:T(8,128)(2,1)} %get-tuple-element.195, s32[1024]{0:T(1024)S(1)} %pad_clamp_fusion.6), kind=kCustom, calls=%fused_computation.1.clone.1 | custom fusion | bytes 12582960 | tf_op jit(solution)/shard_map/while/body/eval_jaxpr/gather | solution.py:42
  244.0 4.8 %fusion.42 = f32[4,128,2048]{2,1,0:T(8,128)} fusion(f32[4,128,2048]{2,1,0:T(8,128)} %get-tuple-element.186, s32[]{:T(128)} %get-tuple-element.185, bf16[1536,2048]{1,0:T(8,128)(2,1)} %bitcast.74, bf16[4,128,1536]{2,1,0:T(8,128)(2,1)S(1)} %get-tuple-element.193), kind=kOutput, calls=%fused_computation.15.clone.1 | convolution fusion | flops 805306368 | bytes 7734272 | tf_op jit(solution)/shard_map/while/body/eval_jaxpr/dot_general | solution.py:43
  248.8 8.1 %gather_fusion.1 = bf16[12,128,2048]{2,1,0:T(8,128)(2,1)} fusion(bf16[20,128,2048]{2,1,0:T(8,128)(2,1)} %get-tuple-element.195, s32[1024]{0:T(1024)S(1)} %pad_clamp_fusion.6), kind=kCustom, calls=%fused_computation.1.clone.1 | custom fusion | bytes 12582960 | tf_op jit(solution)/shard_map/while/body/eval_jaxpr/gather | solution.py:42
  256.9 4.8 %fusion.42 = f32[4,128,2048]{2,1,0:T(8,128)} fusion(f32[4,128,2048]{2,1,0:T(8,128)} %get-tuple-element.186, s32[]{:T(128)} %get-tuple-element.185, bf16[1536,2048]{1,0:T(8,128)(2,1)} %bitcast.74, bf16[4,128,1536]{2,1,0:T(8,128)(2,1)S(1)} %get-tuple-element.193), kind=kOutput, calls=%fused_computation.15.clone.1 | convolution fusion | flops 805306368 | bytes 7734272 | tf_op jit(solution)/shard_map/while/body/eval_jaxpr/dot_general | solution.py:43
  261.7 8.1 %gather_fusion.1 = bf16[12,128,2048]{2,1,0:T(8,128)(2,1)} fusion(bf16[20,128,2048]{2,1,0:T(8,128)(2,1)} %get-tuple-element.195, s32[1024]{0:T(1024)S(1)} %pad_clamp_fusion.6), kind=kCustom, calls=%fused_computation.1.clone.1 | custom fusion | bytes 12582960 | tf_op jit(solution)/shard_map/while/body/eval_jaxpr/gather | solution.py:42
  269.8 4.7 %fusion.42 = f32[4,128,2048]{2,1,0:T(8,128)} fusion(f32[4,128,2048]{2,1,0:T(8,128)} %get-tuple-element.186, s32[]{:T(128)} %get-tuple-element.185, bf16[1536,2048]{1,0:T(8,128)(2,1)} %bitcast.74, bf16[4,128,1536]{2,1,0:T(8,128)(2,1)S(1)} %get-tuple-element.193), kind=kOutput, calls=%fused_computation.15.clone.1 | convolution fusion | flops 805306368 | bytes 7734272 | tf_op jit(solution)/shard_map/while/body/eval_jaxpr/dot_general | solution.py:43
  274.6 8.1 %gather_fusion.1 = bf16[12,128,2048]{2,1,0:T(8,128)(2,1)} fusion(bf16[20,128,2048]{2,1,0:T(8,128)(2,1)} %get-tuple-element.195, s32[1024]{0:T(1024)S(1)} %pad_clamp_fusion.6), kind=kCustom, calls=%fused_computation.1.clone.1 | custom fusion | bytes 12582960 | tf_op jit(solution)/shard_map/while/body/eval_jaxpr/gather | solution.py:42
  282.7 4.8 %fusion.42 = f32[4,128,2048]{2,1,0:T(8,128)} fusion(f32[4,128,2048]{2,1,0:T(8,128)} %get-tuple-element.186, s32[]{:T(128)} %get-tuple-element.185, bf16[1536,2048]{1,0:T(8,128)(2,1)} %bitcast.74, bf16[4,128,1536]{2,1,0:T(8,128)(2,1)S(1)} %get-tuple-element.193), kind=kOutput, calls=%fused_computation.15.clone.1 | convolution fusion | flops 805306368 | bytes 7734272 | tf_op jit(solution)/shard_map/while/body/eval_jaxpr/dot_general | solution.py:43
  287.5 4.6 %fusion.15 = bf16[4,128,2048]{2,1,0:T(8,128)(2,1)S(1)} fusion(bf16[4,128,2048]{2,1,0:T(8,128)(2,1)} %bitcast.81, f32[4,128,2048]{2,1,0:T(8,128)} %get-tuple-element.60, bf16[4,128,2048]{2,1,0:T(8,128)(2,1)} %copy-done.2, f32[]{:T(128)} %bitcast.72, f32[]{:T(128)} %bitcast.70), kind=kLoop, calls=%fused_computation.29 | loop fusion | flops 8388608 | bytes 10485768 | tf_op jit(solution)/shard_map/convert_element_type | solution.py:53
  292.2 9.0 %convolution_convert_fusion = bf16[512,2048]{1,0:T(8,128)(2,1)} fusion(bf16[512,2048]{1,0:T(8,128)(2,1)S(1)} %bitcast.83, bf16[2048,2048]{1,0:T(8,128)(2,1)} %all-gather.2.cloned.1.call-done), kind=kOutput, calls=%fused_computation.30 | convolution fusion | flops 4296015872 | bytes 12582912 | tf_op jit(solution)/shard_map/dot_general | solution.py:55
  (41 shorter events, 1.3 us)
Async XLA Ops:
  6.5 285.6 %all-gather.2.cloned.1.call-start = ((), (), s32[]{:S(2)}) async-start(), calls=%async_computation | async-start | bytes 8421376 | tf_op jit(solution)/shard_map/all_gather | solution.py:57
  7.3 48.1 %collective-permute-start = (bf16[4,128,2048]{2,1,0:T(8,128)(2,1)}, bf16[4,128,2048]{2,1,0:T(8,128)(2,1)}, u32[]{:S(2)}, u32[]{:S(2)}) collective-permute-start(bf16[4,128,2048]{2,1,0:T(8,128)(2,1)} %bitcast.75), channel_id=1, source_target_pairs={{255,0},{0,1},{1,2},{2,3},{3,4},{4,5},{5,6},{6,7},{7,8},{8,9},{9,1... | collective-permute-start | bytes 6291464 | tf_op jit(solution)/shard_map/ppermute | solution.py:10
  10.0 79.7 %collective-permute-start.1 = (bf16[4,128,2048]{2,1,0:T(8,128)(2,1)}, bf16[4,128,2048]{2,1,0:T(8,128)(2,1)}, u32[]{:S(2)}, u32[]{:S(2)}) collective-permute-start(bf16[4,128,2048]{2,1,0:T(8,128)(2,1)} %bitcast.76), channel_id=1, source_target_pairs={{254,0},{255,1},{0,2},{1,3},{2,4},{3,5},{4,6},{5,7},{6,8},{7,9},{8... | collective-permute-start | bytes 6291464 | tf_op jit(solution)/shard_map/ppermute | solution.py:10
  11.3 80.1 %collective-permute-start.2 = (bf16[4,128,2048]{2,1,0:T(8,128)(2,1)}, bf16[4,128,2048]{2,1,0:T(8,128)(2,1)}, u32[]{:S(2)}, u32[]{:S(2)}) collective-permute-start(bf16[4,128,2048]{2,1,0:T(8,128)(2,1)} %bitcast.77), channel_id=1, source_target_pairs={{1,0},{2,1},{3,2},{4,3},{5,4},{6,5},{7,6},{8,7},{9,8},{10,9},{11,1... | collective-permute-start | bytes 6291464 | tf_op jit(solution)/shard_map/ppermute | solution.py:10
  11.3 81.9 %collective-permute-start.3 = (bf16[4,128,2048]{2,1,0:T(8,128)(2,1)}, bf16[4,128,2048]{2,1,0:T(8,128)(2,1)}, u32[]{:S(2)}, u32[]{:S(2)}) collective-permute-start(bf16[4,128,2048]{2,1,0:T(8,128)(2,1)} %bitcast.78), channel_id=1, source_target_pairs={{2,0},{3,1},{4,2},{5,3},{6,4},{7,5},{8,6},{9,7},{10,8},{11,9},{12,... | collective-permute-start | bytes 6291464 | tf_op jit(solution)/shard_map/ppermute | solution.py:10
  94.9 5.3 %copy-start.1 = (bf16[20,128,2048]{2,1,0:T(8,128)(2,1)}, bf16[20,128,2048]{2,1,0:T(8,128)(2,1)S(1)}, u32[]{:S(2)}) copy-start(bf16[20,128,2048]{2,1,0:T(8,128)(2,1)S(1)} %constant_dynamic-update-slice_fusion) | copy-start | bytes 31457284
  157.0 73.2 %copy-start.2 = (bf16[4,128,2048]{2,1,0:T(8,128)(2,1)}, bf16[4,128,2048]{2,1,0:T(8,128)(2,1)S(1)}, u32[]{:S(2)}) copy-start(bf16[4,128,2048]{2,1,0:T(8,128)(2,1)S(1)} %get-tuple-element.92) | copy-start | bytes 6291460
  157.0 44.9 %collective-permute-start.4 = (bf16[4,128,2048]{2,1,0:T(8,128)(2,1)S(1)}, bf16[4,128,2048]{2,1,0:T(8,128)(2,1)S(1)}, u32[]{:S(2)}, u32[]{:S(2)}) collective-permute-start(bf16[4,128,2048]{2,1,0:T(8,128)(2,1)S(1)} %get-tuple-element.92), channel_id=1, source_target_pairs={{255,0},{0,1},{1,2},{2,3},{3,4},{4,5},{5,6},{6,7},{7,8},{8,9},{9,1... | collective-permute-start | bytes 6291464 | tf_op jit(solution)/shard_map/ppermute | solution.py:10
  157.1 73.0 %collective-permute-start.5 = (bf16[4,128,2048]{2,1,0:T(8,128)(2,1)S(1)}, bf16[4,128,2048]{2,1,0:T(8,128)(2,1)S(1)}, u32[]{:S(2)}, u32[]{:S(2)}) collective-permute-start(bf16[4,128,2048]{2,1,0:T(8,128)(2,1)S(1)} %get-tuple-element.92), channel_id=1, source_target_pairs={{254,0},{255,1},{0,2},{1,3},{2,4},{3,5},{4,6},{5,7},{6,8},{7,9},{8... | collective-permute-start | bytes 6291464 | tf_op jit(solution)/shard_map/ppermute | solution.py:10
  157.2 73.0 %collective-permute-start.6 = (bf16[4,128,2048]{2,1,0:T(8,128)(2,1)S(1)}, bf16[4,128,2048]{2,1,0:T(8,128)(2,1)S(1)}, u32[]{:S(2)}, u32[]{:S(2)}) collective-permute-start(bf16[4,128,2048]{2,1,0:T(8,128)(2,1)S(1)} %get-tuple-element.92), channel_id=1, source_target_pairs={{1,0},{2,1},{3,2},{4,3},{5,4},{6,5},{7,6},{8,7},{9,8},{10,9},{11,1... | collective-permute-start | bytes 6291464 | tf_op jit(solution)/shard_map/ppermute | solution.py:10
  157.6 72.8 %collective-permute-start.7 = (bf16[4,128,2048]{2,1,0:T(8,128)(2,1)S(1)}, bf16[4,128,2048]{2,1,0:T(8,128)(2,1)S(1)}, u32[]{:S(2)}, u32[]{:S(2)}) collective-permute-start(bf16[4,128,2048]{2,1,0:T(8,128)(2,1)S(1)} %get-tuple-element.92), channel_id=1, source_target_pairs={{2,0},{3,1},{4,2},{5,3},{6,4},{7,5},{8,6},{9,7},{10,8},{11,9},{12,... | collective-permute-start | bytes 6291464 | tf_op jit(solution)/shard_map/ppermute | solution.py:10
  230.5 5.3 %copy-start = (bf16[20,128,2048]{2,1,0:T(8,128)(2,1)}, bf16[20,128,2048]{2,1,0:T(8,128)(2,1)S(1)}, u32[]{:S(2)}) copy-start(bf16[20,128,2048]{2,1,0:T(8,128)(2,1)S(1)} %constant_dynamic-update-slice_fusion.5) | copy-start | bytes 31457284
Sparse Core Ops, SparseCore 0:
  11.1 131.8 all-gather.1
where the time goes:
time: 309 us; the launch traced here: 308 us
  waiting for transfers between devices  124 us (40%)
  local copies, waits for them, and re-layouts  91.7 us (30%)
  matrix products  48 us (16%)
  starting transfers between devices  19.7 us (6%)
  between operations  14.9 us (5%)
  other arithmetic  10.1 us (3%)
    ppermute x8, waiting for transfers between devices, shifted(): return lax.ppermute(block, axis, route)  123 us
    gather x8, local copies, waits for them, and re-layouts, one_row(): picked = block_pool[row_sources].reshape(block_count * block_size, width)  65.6 us
    dot_general x8, matrix products, one_row(): return jnp.dot(row_blocks, picked, preferred_element_type=jnp.float32)  39 us
    ppermute x8, starting transfers between devices, shifted(): return lax.ppermute(block, axis, route)  19.7 us
    unnamed x15, local copies, waits for them, and re-layouts  15.2 us
    dot_general x1, matrix products, local(): jnp.dot(flattened, lax.all_gather(rotation, 'rows', axis=0, tiled=True),...  9.05 us
  transfers between devices with their start and end apart: 9, of which 4 were waited for; matrix products, arithmetic and copies ran while one was open for 44% of the time, Pallas kernels for 0%

commit v1 on v0

v1 whole, which is shorter than its diff:
```python
import functools

import jax
import jax.numpy as jnp
from jax import lax
from jax.experimental import pallas as pl
from jax.experimental.pallas import tpu as pltpu
from jax.sharding import PartitionSpec as P

BLK = 128
PAIR = 2 * BLK
WINDOW = 14 * BLK
WORK = 20 * 1024 * WINDOW
CHUNKS = (768, 256)
ANY = pl.BlockSpec(memory_space=pl.ANY)
HBM = pl.BlockSpec(memory_space=pltpu.HBM)
SMEM = pl.BlockSpec(memory_space=pltpu.SMEM)
VMEM = pl.BlockSpec(memory_space=pltpu.VMEM)


def call(kernel, name, outs, ins, args, scratch=(), aliases=None, flops=0):
    shapes = [jax.ShapeDtypeStruct(shape, jnp.bfloat16) for shape, _ in outs]
    return pl.pallas_call(
        kernel,
        out_shape=shapes,
        in_specs=ins,
        out_specs=[spec for _, spec in outs],
        scratch_shapes=scratch,
        input_output_aliases=aliases or {},
        compiler_params=pltpu.CompilerParams(vmem_limit_bytes=16 * 1024 * 1024),
        cost_estimate=pl.CostEstimate(flops=flops, transcendentals=0, bytes_accessed=0),
        name=name,
    )(*args)


def core_index():
    return lax.axis_index("rows") & 1


def pack_kernel(*refs):
    pieces, (mine_ref, other_ref, wide) = refs[:4], refs[4:]
    device = lax.axis_index("rows")
    ring = lax.shift_right_logical(device, 1) & 3
    width = mine_ref.shape[1]
    for i, piece in enumerate(pieces):
        place = ((ring - i) & 3) * 8
        wide[pl.ds(pl.multiple_of(place, 8), 8), :] = piece[...].astype(jnp.float32)
    for half, out in ((device & 1, mine_ref), (1 - (device & 1), other_ref)):
        columns = pl.ds(pl.multiple_of(half * width, BLK), width)
        out[...] = wide[:, columns].astype(out.dtype)


def pack(pieces):
    width = pieces[0].shape[1]
    outs = [((32, width // 2), VMEM)] * 2
    scratch = [pltpu.VMEM((32, width), jnp.float32)]
    return call(pack_kernel, "pack", outs, [VMEM] * 4, pieces, scratch)


def slab_kernel(mine_ref, got_ref, after_ref, out_ref, wide):
    core = core_index()
    for ref, side in ((mine_ref, core), (got_ref, 1 - core)):
        rows = ref[...].astype(jnp.float32)
        for i in range(4):
            place = pl.multiple_of(i * 16 + side * 8, 8)
            wide[pl.ds(place, 8), :] = rows[i * 8 : (i + 1) * 8, :]
    out_ref[...] = wide[...].astype(out_ref.dtype)


def slab(mine, got, after):
    shape = (64, mine.shape[1])
    scratch = [pltpu.VMEM(shape, jnp.float32)]
    ins = [VMEM, VMEM, ANY]
    return call(slab_kernel, "slab", [(shape, VMEM)], ins, (mine, got, after), scratch)[0]


def split_kernel(x_ref, out_ref, sem):
    width = out_ref.shape[1]
    columns = pl.ds(pl.multiple_of((1 - core_index()) * width, BLK), width)
    copy = pltpu.make_async_copy(x_ref.at[:, columns], out_ref, sem)
    copy.start()
    copy.wait()


def split(x_states):
    shape = (x_states.shape[0], x_states.shape[1] // 2)
    scratch = [pltpu.SemaphoreType.DMA]
    return call(split_kernel, "split", [(shape, VMEM)], [HBM], (x_states,), scratch)[0]


def tie_kernel(*refs):
    pass


def tie(array, *after):
    ins = [ANY] * (1 + len(after))
    return call(tie_kernel, "tie", [(array.shape, ANY)], ins, (array, *after), (), {0: 0})[0]


def assemble_kernel(chunks, x_ref, partner_ref, after_ref, *rest):
    outs, sems = rest[:-1], rest[-1]
    core = core_index()
    width = sum(chunks)

    def fill(mine):
        copies, at = [], 0
        for i, n in enumerate(chunks):
            columns = pl.ds(pl.multiple_of(core * width + at, BLK), n)
            up, dn = outs[2 * i], outs[2 * i + 1]
            if mine == 0:
                targets = ((0, 512, dn, 0), (256, 256, up, 0))
            else:
                targets = ((0, 256, dn, 512), (0, 512, up, 256))
            for j, (source, rows, out, place) in enumerate(targets):
                copy = pltpu.make_async_copy(
                    x_ref.at[pl.ds(source, rows), columns],
                    out.at[pl.ds(place, rows)],
                    sems.at[2 * i + j],
                )
                copy.start()
                copies.append(copy)
            at += n
        at = 0
        for i, n in enumerate(chunks):
            up, dn = outs[2 * i], outs[2 * i + 1]
            if mine == 0:
                dn[512:768, :] = partner_ref[0:256, at : at + n]
                up[256:768, :] = partner_ref[:, at : at + n]
            else:
                dn[0:512, :] = partner_ref[:, at : at + n]
                up[0:256, :] = partner_ref[256:512, at : at + n]
            at += n
        for copy in copies:
            copy.wait()

    @pl.when(core == 0)
    def _():
        fill(0)

    @pl.when(core == 1)
    def _():
        fill(1)


def assemble(x_states, partner, after, chunks):
    outs = [((768, n), VMEM) for n in chunks for _ in range(2)]
    scratch = [pltpu.SemaphoreType.DMA((2 * len(chunks),))]
    kernel = functools.partial(assemble_kernel, chunks)
    return call(kernel, "assemble", outs, [HBM, VMEM, ANY], (x_states, partner, after), scratch)


def build_kernel(device_count, col_ref, send_ref, h_ref, after_ref, out_ref):
    device = lax.axis_index("rows")
    out_ref[...] = jnp.zeros_like(out_ref)
    block_count = device_count * 4
    for row in range(4):
        band, half = row // 2, row % 2
        for k in range(12):
            column = col_ref[row, k]
            owner = lax.shift_right_logical(column, 2)
            local = column & 3
            offset = ((device - owner + 2) & (device_count - 1)) - 2
            slot = jnp.clip(jnp.where(offset > 0, offset - 1, 1 - offset), 0, 3)
            counts = offset == 0
            for j in range(4):
                counts = counts | (send_ref[slot, j, owner] == local)
            shift = ((column - (device * 4 + row) + 6) & (block_count - 1)) + half
            place = pl.ds(pl.multiple_of(shift * BLK, BLK), BLK)

            @pl.when(counts)
            def _(band=band, half=half, row=row, k=k, place=place):
                out_ref[band, half * BLK : (half + 1) * BLK, place] = h_ref[row, k]


def build(h_blocks, col_blocks, send_list, after, device_count):
    kernel = functools.partial(build_kernel, device_count)
    args = (col_blocks, send_list.transpose(1, 2, 0), h_blocks, after)
    return call(
        kernel, "build_bands", [((2, PAIR, WINDOW), VMEM)], [SMEM, SMEM, VMEM, ANY], args
    )[0]


def merge_kernel(own_ref, partner_ref, out_ref):
    core = core_index()
    out_ref[pl.ds(core * 2, 2)] = own_ref[...]
    out_ref[pl.ds(2 - core * 2, 2)] = partner_ref[...]


def merge(own, partner):
    outs = [((4, PAIR, WINDOW), VMEM)]
    return call(merge_kernel, "merge_bands", outs, [VMEM] * 2, (own, partner))[0]


def times_bands(g, bands, left, dn, up, right):
    edge = 768 - g * PAIR

    def dot(start, stop, states):
        return jnp.dot(bands[g, :, start:stop], states, preferred_element_type=jnp.float32)

    total = dot(edge, edge + 768, dn[...]) + dot(edge + 768, edge + 1024, up[512:768, :])
    if g < 3:
        total += dot(0, edge, left[g * PAIR :, :])
    if g > 0:
        total += dot(edge + 1024, WINDOW, right[: g * PAIR, :])
    return total


def own_rows(g, dn, up):
    rows = dn[g * PAIR : (g + 1) * PAIR, :] if g < 3 else up[512:768, :]
    return rows.astype(jnp.float32)


def first_kernel(center, half, bands, left, dn, up, right, after, out_up, out_dn):
    for g in range(4):
        total = times_bands(g, bands, left, dn, up, right)
        value = (total - center[0] * own_rows(g, dn, up)) / half[0]
        value = value.astype(jnp.bfloat16)
        if g < 3:
            out_dn[g * PAIR : (g + 1) * PAIR, :] = value
        if g > 0:
            out_up[(g - 1) * PAIR : g * PAIR, :] = value


def second_kernel(
    center, half, bands, left, dn, up, right, after, xdn, xup, out_mine, out_other, outs
):
    for g in range(4):
        total = times_bands(g, bands, left, dn, up, right)
        value = 2.0 * (total - center[0] * own_rows(g, dn, up)) / half[0] - own_rows(g, xdn, xup)
        outs[g * PAIR : (g + 1) * PAIR, :] = value.astype(jnp.bfloat16)
    core = core_index()
    out_mine[...] = outs[pl.ds(core * 512, 512), :]
    out_other[...] = outs[pl.ds(512 - core * 512, 512), :]


def first_pass(*args):
    n = args[4].shape[1]
    outs = [((768, n), VMEM)] * 2
    ins = [SMEM] * 2 + [VMEM] * 5 + [ANY]
    return call(first_kernel, "first_pass", outs, ins, args, flops=WORK * n)


def second_pass(*args):
    n = args[4].shape[1]
    outs = [((512, n), VMEM)] * 2
    ins = [SMEM] * 2 + [VMEM] * 5 + [ANY] + [VMEM] * 2
    scratch = [pltpu.VMEM((1024, n), jnp.bfloat16)]
    return call(second_kernel, "second_pass", outs, ins, args, scratch, flops=WORK * n)


def rotate_kernel(chunks, own_half, *refs):
    count = len(chunks)
    own, got, rot = refs[:count], refs[count : 2 * count], refs[2 * count]
    out_ref, outs, sems = refs[-3:]
    core = core_index()
    width = sum(chunks)
    tile = 256
    half = core if own_half else 1 - core
    stores = []
    for j in range(width // tile):
        columns = slice(j * tile, (j + 1) * tile)
        total, at = 0.0, 0
        for i, n in enumerate(chunks):
            for piece, side in ((own[i], core), (got[i], 1 - core)):
                rows = pl.ds(pl.multiple_of(side * width + at, BLK), n)
                total += jnp.dot(piece[...], rot[rows, columns], preferred_element_type=jnp.float32)
            at += n
        outs[:, columns] = total.astype(jnp.bfloat16)
        target = pl.ds(pl.multiple_of(half * width + j * tile, BLK), tile)
        stores.append(
            pltpu.make_async_copy(outs.at[:, columns], out_ref.at[:, target], sems.at[j])
        )
        stores[-1].start()
    for store in stores:
        store.wait()


def rotate(own, got, rot, chunks, out=None):
    width = sum(chunks)
    kernel = functools.partial(rotate_kernel, chunks, out is None)
    args, ins = [*own, *got, rot], [VMEM] * (2 * len(chunks) + 1)
    aliases = None
    if out is not None:
        aliases = {len(args): 0}
        args.append(out)
        ins.append(HBM)
    scratch = [pltpu.VMEM((512, width), jnp.bfloat16), pltpu.SemaphoreType.DMA((width // 256,))]
    return call(kernel, "rotate", [((512, 2 * width), HBM)], ins, args, scratch, aliases)[0]


def local(x_states, h_blocks, col_blocks, send_list, center, half_width, rotation):
    count = lax.axis_size("rows")
    swap = [(i, i ^ 1) for i in range(count)]
    onward = [(i, (i + 2) % count) for i in range(count)]
    backward = [(i, (i - 2) % count) for i in range(count)]

    def move(array, route):
        return lax.ppermute(array, "rows", route)

    def ring(step):
        return [(8 * (i // 8) + (i + 2 * step) % 8, i) for i in range(count)]

    plane = [[g * 8 + i for g in range(count // 8)] for i in range(8)]
    partner = move(split(x_states), swap)
    mine, other = pack([rotation] + [move(rotation, ring(step)) for step in (-1, -2, -3)])
    pieces = assemble(x_states, partner, mine, CHUNKS)
    ups, dns = pieces[0::2], pieces[1::2]
    lefts = [move(up, onward) for up in ups]
    rights = [move(dn, backward) for dn in dns]
    rows = slab(mine, move(other, swap), pieces[0])
    rot_own = lax.all_gather(rows, "rows", axis=0, tiled=True, axis_index_groups=plane)

    bands = build(h_blocks, col_blocks, send_list, rows, count)
    bands = merge(bands, move(bands, swap))
    fixed = (center, half_width, bands)

    firsts, after = [], mine
    for left, dn, up, right in zip(lefts, dns, ups, rights):
        up, dn = first_pass(*fixed, left, dn, up, right, after)
        after = up
        firsts.append((move(up, onward), dn, up, move(dn, backward)))
    own, got = [], []
    for first, xdn, xup in zip(firsts, dns, ups):
        mine, other = second_pass(*fixed, *first, after, xdn, xup)
        own.append(mine)
        got.append(move(other, swap))
        after = mine
    rot_own = tie(rot_own, *got)
    rot_got = move(rot_own, swap)
    out = rotate(own, got, rot_own, CHUNKS)
    return rotate(own, got, rot_got, CHUNKS, out)


def solution(mesh):
    placed = (
        P("rows", None),
        P("rows", None, None, None),
        P("rows", None),
        P(),
        P(),
        P(),
        P("rows", None),
    )
    return jax.shard_map(
        local, mesh=mesh, in_specs=placed, out_specs=P("rows", None), check_vma=False
    )
```

time: 309 us -> 152 us (0.49)
  local copies, waits for them, and re-layouts: 91.7 us -> 3.57 us
  waiting for transfers between devices: 124 us -> 52.6 us
  matrix products: 48 us -> 0 us
  starting transfers between devices: 19.7 us -> 54.2 us
  Pallas kernels: 0 us -> 26.7 us
  other arithmetic: 10.1 us -> 0 us
    ppermute x8 -> x17, waiting for transfers between devices: 123 us -> 52.5 us  [move(): return lax.ppermute(array, 'rows', route)]
    gather x13 -> x0, local copies, waits for them, and re-layouts: 68.1 us -> none  [the longest x8 65.6 us: one_row(): picked = block_pool[row_sources].reshape(block_count * block_size, width)]
    dot_general x9 -> x0, matrix products: 48 us -> none  [the longest x8 39 us: one_row(): return jnp.dot(row_blocks, picked, preferred_element_type=jnp.float32)]
    ppermute x8 -> x17, starting transfers between devices: 19.7 us -> 54.1 us  [move(): return lax.ppermute(array, 'rows', route)]
    pallas_call x0 -> x13, Pallas kernels: none -> 26.7 us  [call(): pl.pallas_call(kernel, out_shape=shapes, in_specs=ins, out_specs=[spec fo...]
    unnamed x15 -> x24, local copies, waits for them, and re-layouts: 15.2 us -> 3.57 us
    another operation x2 -> x0, local copies, waits for them, and re-layouts: 5.57 us -> none
    convert_element_type x2 -> x0, other arithmetic: 4.61 us -> none  [the longest x1 4.6 us: local(): second_pass = (2.0 * second_term / half_value - x_wide).astype(jnp.bfloat16)]
  transfers between devices with their start and end apart: 9 -> 18, of which waited for: 4 -> 9; matrix products, arithmetic and copies ran while one was open for 44% -> 0% of each run, Pallas kernels for 0% -> 13%
where the time goes in v1:
time: 152 us
  starting transfers between devices  54.2 us (36%)
  waiting for transfers between devices  52.6 us (35%)
  Pallas kernels  26.7 us (18%)
  between operations  14.9 us (10%)
  local copies, waits for them, and re-layouts  3.57 us (2%)
    ppermute x17, starting transfers between devices, move(): return lax.ppermute(array, 'rows', route)  54.1 us
    ppermute x17, waiting for transfers between devices, move(): return lax.ppermute(array, 'rows', route)  52.5 us
    pallas_call x13, Pallas kernels, call(): pl.pallas_call(kernel, out_shape=shapes, in_specs=ins, out_specs=[spec fo...  26.7 us
    unnamed x24, local copies, waits for them, and re-layouts  3.57 us
  transfers between devices with their start and end apart: 18, of which 9 were waited for; matrix products, arithmetic and copies ran while one was open for 0% of the time, Pallas kernels for 13%

profile of v1, /device:TPU:1, one launch (start us, length us, event | category | flops | bytes accessed | tf_op | source)
XLA Modules:
  0.0 151.8 jit_solution(1562826398595230177)
XLA Ops:
  6.5 1.6 %copy-done = bf16[512,2048]{1,0:T(8,128)(2,1)S(1)} copy-done((bf16[512,2048]{1,0:T(8,128)(2,1)S(1)}, bf16[512,2048]{1,0:T(8,128)(2,1)}, u32[]{:S(2)}) %copy-start) | copy-done | bytes 2097176
  8.1 0.2 split.1
  8.3 3.3 %collective-permute-start.4 = (bf16[512,1024]{1,0:T(8,128)(2,1)S(1)}, bf16[512,1024]{1,0:T(8,128)(2,1)S(1)}, u32[]{:S(2)}, u32[]{:S(2)}) collective-permute-start(bf16[512,1024]{1,0:T(8,128)(2,1)S(1)} %split.1), channel_id=1, source_target_pairs={{0,1},{1,0},{2,3},{3,2},{4,5},{5,4},{6,7},{7,6},{8,9},{9,8},{10,11... | collective-permute-start | bytes 3145736 | tf_op jit(solution)/shard_map/ppermute | solution.py:298
  11.7 0.0 collective-permute-start
  11.7 2.2 %collective-permute-start.1 = (bf16[8,2048]{1,0:T(8,128)(2,1)S(1)}, bf16[8,2048]{1,0:T(8,128)(2,1)S(1)}, u32[]{:S(2)}, u32[]{:S(2)}) collective-permute-start(bf16[8,2048]{1,0:T(8,128)(2,1)S(1)} %copy-done.3), channel_id=1, source_target_pairs={{4,0},{5,1},{6,2},{7,3},{0,4},{1,5},{2,6},{3,7},{12,8},{13,9},{14,... | collective-permute-start | bytes 98312 | tf_op jit(solution)/shard_map/ppermute | solution.py:298
  13.9 1.1 collective-permute-start.2
  14.9 0.7 collective-permute-done.refs_1_
  15.7 0.5 collective-permute-done.1.refs_2_
  16.2 0.7 collective-permute-done.2.refs_3_
  17.0 2.0 %collective-permute-start.3 = (bf16[32,1024]{1,0:T(8,128)(2,1)S(1)}, bf16[32,1024]{1,0:T(8,128)(2,1)S(1)}, u32[]{:S(2)}, u32[]{:S(2)}) collective-permute-start(bf16[32,1024]{1,0:T(8,128)(2,1)S(1)} %get-tuple-element.20), channel_id=1, source_target_pairs={{0,1},{1,0},{2,3},{3,2},{4,5},{5,4},{6,7},{7,6},{8,9},{9,8},{10,11... | collective-permute-start | bytes 196616 | tf_op jit(solution)/shard_map/ppermute | solution.py:298
  18.9 0.0 collective-permute-done.4.partner_ref
  18.9 0.0 copy-start.5
  18.9 1.4 assemble.1
  20.3 1.0 copy-done.6
  21.4 0.0 collective-permute-done.3.got_ref
  21.4 0.8 copy-done.8
  22.1 0.1 copy-done.10
  22.3 0.7 slab.1.after_ref
  23.0 2.1 %build_bands.1.own_ref = bf16[2,256,1792]{2,1,0:T(8,128)(2,1)S(1)} custom-call(s32[4,12]{1,0:T(4,128)S(1)} %copy-done.5, s32[4,4,256]{2,1,0:T(4,128)S(1)} %bitcast.1, bf16[4,12,128,128]{3,2,1,0:T(8,128)(2,1)S(1)} %copy-done.2, bf16[64,1024]{1,0:T(8,128)(2,1)} %slab.1.after_ref), custom_call_target="tpu_custom_call" | custom-call | tf_op jit(solution)/shard_map/build_bands/pallas_call | solution.py:23
  25.1 0.1 collective-permute-start.5
  25.3 1.1 collective-permute-start.6
  26.4 8.8 %collective-permute-start.7 = (bf16[768,768]{1,0:T(8,128)(2,1)}, bf16[768,768]{1,0:T(8,128)(2,1)}, u32[]{:S(2)}, u32[]{:S(2)}) collective-permute-start(bf16[768,768]{1,0:T(8,128)(2,1)} %copy-done.6), channel_id=1, source_target_pairs={{0,254},{1,255},{2,0},{3,1},{4,2},{5,3},{6,4},{7,5},{8,6},{9,7},{1... | collective-permute-start | bytes 3538952 | tf_op jit(solution)/shard_map/ppermute | solution.py:298
  35.2 0.0 all-gather.2.cloned.1.call-update
  36.5 0.1 collective-permute-start.10
  36.6 6.9 %collective-permute-start.11 = (bf16[768,256]{1,0:T(8,128)(2,1)}, bf16[768,256]{1,0:T(8,128)(2,1)S(1)}, u32[]{:S(2)}, u32[]{:S(2)}) collective-permute-start(bf16[768,256]{1,0:T(8,128)(2,1)} %copy-done.10), channel_id=1, source_target_pairs={{0,254},{1,255},{2,0},{3,1},{4,2},{5,3},{6,4},{7,5},{8,6},{9,7},{1... | collective-permute-start | bytes 1179656 | tf_op jit(solution)/shard_map/ppermute | solution.py:298
  43.5 1.8 %merge_bands.1.bands = bf16[4,256,1792]{2,1,0:T(8,128)(2,1)S(1)} custom-call(bf16[2,256,1792]{2,1,0:T(8,128)(2,1)S(1)} %build_bands.1.own_ref, bf16[2,256,1792]{2,1,0:T(8,128)(2,1)} %collective-permute-done.5.partner_ref), custom_call_target="tpu_custom_call" | custom-call | tf_op jit(solution)/shard_map/merge_bands/pallas_call | solution.py:23
  45.3 18.7 %collective-permute-done.6.left = bf16[768,768]{1,0:T(8,128)(2,1)S(1)} collective-permute-done((bf16[768,768]{1,0:T(8,128)(2,1)}, bf16[768,768]{1,0:T(8,128)(2,1)S(1)}, u32[]{:S(2)}, u32[]{:S(2)}) %collective-permute-start.6) | collective-permute-done | bytes 1179680 | tf_op jit(solution)/shard_map/ppermute | solution.py:298
  64.0 0.3 collective-permute-done.7.right
  64.3 4.6 %first_pass.2 = (bf16[768,768]{1,0:T(8,128)(2,1)S(1)}, bf16[768,768]{1,0:T(8,128)(2,1)S(1)}) custom-call(f32[1]{0:T(128)S(6)} %copy.12.center, f32[1]{0:T(128)S(6)} %copy.13.half, bf16[4,256,1792]{2,1,0:T(8,128)(2,1)S(1)} %merge_bands.1.bands, bf16[768,768]{1,0:T(8,128)(2,1)S(1)} %collective-permute-done.6.left, bf16[768,768]{1,0:T(8,128)(2,1)S(1)} %copy-done.7, ...), custom_call_target="tpu_custom_call" | custom-call | flops 28185722880 | tf_op jit(solution)/shard_map/first_pass/pallas_call | solution.py:23
  68.9 0.3 collective-permute-start.8
  69.2 7.7 %collective-permute-start.9 = (bf16[768,768]{1,0:T(8,128)(2,1)S(1)}, bf16[768,768]{1,0:T(8,128)(2,1)S(1)}, u32[]{:S(2)}, u32[]{:S(2)}) collective-permute-start(bf16[768,768]{1,0:T(8,128)(2,1)S(1)} %get-tuple-element.24.dn), channel_id=1, source_target_pairs={{0,254},{1,255},{2,0},{3,1},{4,2},{5,3},{6,4},{7,5},{8,6},{9,7},{1... | collective-permute-start | bytes 3538952 | tf_op jit(solution)/shard_map/ppermute | solution.py:298
  76.9 0.0 collective-permute-done.10.left
  76.9 0.0 collective-permute-done.11.right
  76.9 1.1 first_pass.3
  78.1 0.1 collective-permute-start.12
  78.1 6.9 %collective-permute-start.13 = (bf16[768,256]{1,0:T(8,128)(2,1)S(1)}, bf16[768,256]{1,0:T(8,128)(2,1)S(1)}, u32[]{:S(2)}, u32[]{:S(2)}) collective-permute-start(bf16[768,256]{1,0:T(8,128)(2,1)S(1)} %get-tuple-element.29.dn), channel_id=1, source_target_pairs={{0,254},{1,255},{2,0},{3,1},{4,2},{5,3},{6,4},{7,5},{8,6},{9,7},{1... | collective-permute-start | bytes 1179656 | tf_op jit(solution)/shard_map/ppermute | solution.py:298
  85.0 26.7 %collective-permute-done.8.left = bf16[768,768]{1,0:T(8,128)(2,1)S(1)} collective-permute-done((bf16[768,768]{1,0:T(8,128)(2,1)S(1)}, bf16[768,768]{1,0:T(8,128)(2,1)S(1)}, u32[]{:S(2)}, u32[]{:S(2)}) %collective-permute-start.8) | collective-permute-done | bytes 1179680 | tf_op jit(solution)/shard_map/ppermute | solution.py:298
  111.7 2.1 %collective-permute-done.9.right = bf16[768,768]{1,0:T(8,128)(2,1)S(1)} collective-permute-done((bf16[768,768]{1,0:T(8,128)(2,1)S(1)}, bf16[768,768]{1,0:T(8,128)(2,1)S(1)}, u32[]{:S(2)}, u32[]{:S(2)}) %collective-permute-start.9) | collective-permute-done | bytes 1179680 | tf_op jit(solution)/shard_map/ppermute | solution.py:298
  113.8 4.8 %second_pass.2 = (bf16[512,768]{1,0:T(8,128)(2,1)S(1)}, bf16[512,768]{1,0:T(8,128)(2,1)S(1)}) custom-call(f32[1]{0:T(128)S(6)} %copy.12.center, f32[1]{0:T(128)S(6)} %copy.13.half, bf16[4,256,1792]{2,1,0:T(8,128)(2,1)S(1)} %merge_bands.1.bands, bf16[768,768]{1,0:T(8,128)(2,1)S(1)} %collective-permute-done.8.left, bf16[768,768]{1,0:T(8,128)(2,1)S(1)} %get-tuple-element.24.dn, ...), custom_call_target="tpu_custom_call" | custom-call | flops 28185722880 | tf_op jit(solution)/shard_map/second_pass/pallas_call | solution.py:23
  118.6 11.2 %collective-permute-start.14 = (bf16[512,768]{1,0:T(8,128)(2,1)S(1)}, bf16[512,768]{1,0:T(8,128)(2,1)S(1)}, u32[]{:S(2)}, u32[]{:S(2)}) collective-permute-start(bf16[512,768]{1,0:T(8,128)(2,1)S(1)} %get-tuple-element.31), channel_id=1, source_target_pairs={{0,1},{1,0},{2,3},{3,2},{4,5},{5,4},{6,7},{7,6},{8,9},{9,8},{10,11... | collective-permute-start | bytes 2359304 | tf_op jit(solution)/shard_map/ppermute | solution.py:298
  129.8 1.3 second_pass.3
  131.1 2.1 %collective-permute-start.15 = (bf16[512,256]{1,0:T(8,128)(2,1)S(1)}, bf16[512,256]{1,0:T(8,128)(2,1)S(1)}, u32[]{:S(2)}, u32[]{:S(2)}) collective-permute-start(bf16[512,256]{1,0:T(8,128)(2,1)S(1)} %get-tuple-element.32), channel_id=1, source_target_pairs={{0,1},{1,0},{2,3},{3,2},{4,5},{5,4},{6,7},{7,6},{8,9},{9,8},{10,11... | collective-permute-start | bytes 786440 | tf_op jit(solution)/shard_map/ppermute | solution.py:298
  133.2 1.2 collective-permute-done.15.refs_2_.refs_3_
  134.4 0.0 collective-permute-done.14.refs_1_.refs_2_
  134.4 0.4 collective-permute-start.16
  134.7 5.4 %rotate.2.refs_5_ = bf16[512,2048]{1,0:T(8,128)(2,1)} custom-call(bf16[512,768]{1,0:T(8,128)(2,1)S(1)} %get-tuple-element.28.after.refs_0_, bf16[512,256]{1,0:T(8,128)(2,1)S(1)} %get-tuple-element.30.refs_1_, bf16[512,768]{1,0:T(8,128)(2,1)S(1)} %collective-permute-done.14.refs_1_.refs_2_, bf16[512,256]{1,0:T(8,128)(2,1)S(1)} %collective-permute-done.15.refs_2_.refs_3_, ...), custom_call_target="tpu_custom_call" | custom-call | tf_op jit(solution)/shard_map/rotate/pallas_call | solution.py:23
  140.2 1.6 %collective-permute-done.16.refs_4_ = bf16[2048,1024]{1,0:T(8,128)(2,1)S(1)} collective-permute-done((bf16[2048,1024]{1,0:T(8,128)(2,1)}, bf16[2048,1024]{1,0:T(8,128)(2,1)S(1)}, u32[]{:S(2)}, u32[]{:S(2)}) %collective-permute-start.16) | collective-permute-done | bytes 4194336 | tf_op jit(solution)/shard_map/ppermute | solution.py:298
  141.7 3.2 %rotate.3 = bf16[512,2048]{1,0:T(8,128)(2,1)} custom-call(bf16[512,768]{1,0:T(8,128)(2,1)S(1)} %get-tuple-element.28.after.refs_0_, bf16[512,256]{1,0:T(8,128)(2,1)S(1)} %get-tuple-element.30.refs_1_, bf16[512,768]{1,0:T(8,128)(2,1)S(1)} %collective-permute-done.14.refs_1_.refs_2_, ...), custom_call_target="tpu_custom_call", output_to_operand_aliasing={{}: (5, {})} | custom-call | tf_op jit(solution)/shard_map/rotate/pallas_call | solution.py:23
  (26 shorter events, 0.1 us)
Async XLA Ops:
  6.5 127.8 %all-gather.2.cloned.1.call-start = ((), (), s32[]{:S(2)}) async-start(), calls=%async_computation | async-start | bytes 4325376 | tf_op jit(solution)/shard_map/all_gather | solution.py:311
  6.5 1.6 %copy-start = (bf16[512,2048]{1,0:T(8,128)(2,1)S(1)}, bf16[512,2048]{1,0:T(8,128)(2,1)}, u32[]{:S(2)}) copy-start(bf16[512,2048]{1,0:T(8,128)(2,1)} %x_ref.3) | copy-start | bytes 6291460
  8.1 3.5 %copy-start.3 = (bf16[8,2048]{1,0:T(8,128)(2,1)S(1)}, bf16[8,2048]{1,0:T(8,128)(2,1)}, u32[]{:S(2)}) copy-start(bf16[8,2048]{1,0:T(8,128)(2,1)} %refs_0_.1) | copy-start | bytes 98308
  8.1 10.8 %copy-start.1 = (bf16[512,2048]{1,0:T(8,128)(2,1)S(1)}, bf16[512,2048]{1,0:T(8,128)(2,1)}, u32[]{:S(2)}) copy-start(bf16[512,2048]{1,0:T(8,128)(2,1)} %x_ref.3) | copy-start | bytes 6291460
  8.3 10.6 %collective-permute-start.4 = (bf16[512,1024]{1,0:T(8,128)(2,1)S(1)}, bf16[512,1024]{1,0:T(8,128)(2,1)S(1)}, u32[]{:S(2)}, u32[]{:S(2)}) collective-permute-start(bf16[512,1024]{1,0:T(8,128)(2,1)S(1)} %split.1), channel_id=1, source_target_pairs={{0,1},{1,0},{2,3},{3,2},{4,5},{5,4},{6,7},{7,6},{8,9},{9,8},{10,11... | collective-permute-start | bytes 3145736 | tf_op jit(solution)/shard_map/ppermute | solution.py:298
  11.7 4.0 %collective-permute-start = (bf16[8,2048]{1,0:T(8,128)(2,1)S(1)}, bf16[8,2048]{1,0:T(8,128)(2,1)S(1)}, u32[]{:S(2)}, u32[]{:S(2)}) collective-permute-start(bf16[8,2048]{1,0:T(8,128)(2,1)S(1)} %copy-done.3), channel_id=1, source_target_pairs={{6,0},{7,1},{0,2},{1,3},{2,4},{3,5},{4,6},{5,7},{14,8},{15,9},{8,1... | collective-permute-start | bytes 98312 | tf_op jit(solution)/shard_map/ppermute | solution.py:298
  11.7 4.5 %collective-permute-start.1 = (bf16[8,2048]{1,0:T(8,128)(2,1)S(1)}, bf16[8,2048]{1,0:T(8,128)(2,1)S(1)}, u32[]{:S(2)}, u32[]{:S(2)}) collective-permute-start(bf16[8,2048]{1,0:T(8,128)(2,1)S(1)} %copy-done.3), channel_id=1, source_target_pairs={{4,0},{5,1},{6,2},{7,3},{0,4},{1,5},{2,6},{3,7},{12,8},{13,9},{14,... | collective-permute-start | bytes 98312 | tf_op jit(solution)/shard_map/ppermute | solution.py:298
  13.9 3.1 %collective-permute-start.2 = (bf16[8,2048]{1,0:T(8,128)(2,1)S(1)}, bf16[8,2048]{1,0:T(8,128)(2,1)S(1)}, u32[]{:S(2)}, u32[]{:S(2)}) collective-permute-start(bf16[8,2048]{1,0:T(8,128)(2,1)S(1)} %copy-done.3), channel_id=1, source_target_pairs={{2,0},{3,1},{4,2},{5,3},{6,4},{7,5},{0,6},{1,7},{10,8},{11,9},{12,... | collective-permute-start | bytes 98312 | tf_op jit(solution)/shard_map/ppermute | solution.py:298
  17.0 4.4 %collective-permute-start.3 = (bf16[32,1024]{1,0:T(8,128)(2,1)S(1)}, bf16[32,1024]{1,0:T(8,128)(2,1)S(1)}, u32[]{:S(2)}, u32[]{:S(2)}) collective-permute-start(bf16[32,1024]{1,0:T(8,128)(2,1)S(1)} %get-tuple-element.20), channel_id=1, source_target_pairs={{0,1},{1,0},{2,3},{3,2},{4,5},{5,4},{6,7},{7,6},{8,9},{9,8},{10,11... | collective-permute-start | bytes 196616 | tf_op jit(solution)/shard_map/ppermute | solution.py:298
  18.9 4.1 %copy-start.2 = (bf16[4,12,128,128]{3,2,1,0:T(8,128)(2,1)S(1)}, bf16[4,12,128,128]{3,2,1,0:T(8,128)(2,1)}, u32[]{:S(2)}) copy-start(bf16[4,12,128,128]{3,2,1,0:T(8,128)(2,1)} %h_ref.1) | copy-start | bytes 4718596
  18.9 4.1 %copy-start.4 = (s32[256,4,4]{0,2,1:T(4,128)S(1)}, s32[256,4,4]{0,2,1:T(4,128)}, u32[]{:S(2)}) copy-start(s32[256,4,4]{0,2,1:T(4,128)} %param.10) | copy-start | bytes 49156
  18.9 4.1 %copy-start.5 = (s32[4,12]{1,0:T(4,128)S(1)}, s32[4,12]{1,0:T(4,128)}, u32[]{:S(2)}) copy-start(s32[4,12]{1,0:T(4,128)} %col_ref.1) | copy-start | bytes 580
  20.3 1.0 copy-start.6
  21.4 0.8 copy-start.8
  21.4 0.9 copy-start.10
  25.1 18.3 %collective-permute-start.5 = (bf16[2,256,1792]{2,1,0:T(8,128)(2,1)S(1)}, bf16[2,256,1792]{2,1,0:T(8,128)(2,1)}, u32[]{:S(2)}, u32[]{:S(2)}) collective-permute-start(bf16[2,256,1792]{2,1,0:T(8,128)(2,1)S(1)} %build_bands.1.own_ref), channel_id=1, source_target_pairs={{0,1},{1,0},{2,3},{3,2},{4,5},{5,4},{6,7},{7,6},{8,9},{9,8},{10,11... | collective-permute-start | bytes 5505032 | tf_op jit(solution)/shard_map/ppermute | solution.py:298
  25.3 38.7 %collective-permute-start.6 = (bf16[768,768]{1,0:T(8,128)(2,1)}, bf16[768,768]{1,0:T(8,128)(2,1)S(1)}, u32[]{:S(2)}, u32[]{:S(2)}) collective-permute-start(bf16[768,768]{1,0:T(8,128)(2,1)} %get-tuple-element.21.after_ref.up.xup), channel_id=1, source_target_pairs={{0,2},{1,3},{2,4},{3,5},{4,6},{5,7},{6,8},{7,9},{8,10},{9,11},{10,... | collective-permute-start | bytes 3538952 | tf_op jit(solution)/shard_map/ppermute | solution.py:298
  26.4 37.9 %collective-permute-start.7 = (bf16[768,768]{1,0:T(8,128)(2,1)}, bf16[768,768]{1,0:T(8,128)(2,1)}, u32[]{:S(2)}, u32[]{:S(2)}) collective-permute-start(bf16[768,768]{1,0:T(8,128)(2,1)} %copy-done.6), channel_id=1, source_target_pairs={{0,254},{1,255},{2,0},{3,1},{4,2},{5,3},{6,4},{7,5},{8,6},{9,7},{1... | collective-permute-start | bytes 3538952 | tf_op jit(solution)/shard_map/ppermute | solution.py:298
  36.5 40.4 %collective-permute-start.10 = (bf16[768,256]{1,0:T(8,128)(2,1)}, bf16[768,256]{1,0:T(8,128)(2,1)S(1)}, u32[]{:S(2)}, u32[]{:S(2)}) collective-permute-start(bf16[768,256]{1,0:T(8,128)(2,1)} %copy-done.8), channel_id=1, source_target_pairs={{0,2},{1,3},{2,4},{3,5},{4,6},{5,7},{6,8},{7,9},{8,10},{9,11},{10,... | collective-permute-start | bytes 1179656 | tf_op jit(solution)/shard_map/ppermute | solution.py:298
  36.6 27.7 %copy-start.7 = (bf16[768,768]{1,0:T(8,128)(2,1)S(1)}, bf16[768,768]{1,0:T(8,128)(2,1)}, u32[]{:S(2)}) copy-start(bf16[768,768]{1,0:T(8,128)(2,1)} %copy-done.6) | copy-start | bytes 3538948
  36.6 40.3 %collective-permute-start.11 = (bf16[768,256]{1,0:T(8,128)(2,1)}, bf16[768,256]{1,0:T(8,128)(2,1)S(1)}, u32[]{:S(2)}, u32[]{:S(2)}) collective-permute-start(bf16[768,256]{1,0:T(8,128)(2,1)} %copy-done.10), channel_id=1, source_target_pairs={{0,254},{1,255},{2,0},{3,1},{4,2},{5,3},{6,4},{7,5},{8,6},{9,7},{1... | collective-permute-start | bytes 1179656 | tf_op jit(solution)/shard_map/ppermute | solution.py:298
  45.3 31.7 %copy-start.9 = (bf16[768,256]{1,0:T(8,128)(2,1)S(1)}, bf16[768,256]{1,0:T(8,128)(2,1)}, u32[]{:S(2)}) copy-start(bf16[768,256]{1,0:T(8,128)(2,1)} %copy-done.8) | copy-start | bytes 1179652
  45.3 31.6 %copy-start.11 = (bf16[768,256]{1,0:T(8,128)(2,1)S(1)}, bf16[768,256]{1,0:T(8,128)(2,1)}, u32[]{:S(2)}) copy-start(bf16[768,256]{1,0:T(8,128)(2,1)} %copy-done.10) | copy-start | bytes 1179652
  68.9 42.7 %collective-permute-start.8 = (bf16[768,768]{1,0:T(8,128)(2,1)S(1)}, bf16[768,768]{1,0:T(8,128)(2,1)S(1)}, u32[]{:S(2)}, u32[]{:S(2)}) collective-permute-start(bf16[768,768]{1,0:T(8,128)(2,1)S(1)} %get-tuple-element.23.after.up), channel_id=1, source_target_pairs={{0,2},{1,3},{2,4},{3,5},{4,6},{5,7},{6,8},{7,9},{8,10},{9,11},{10,... | collective-permute-start | bytes 3538952 | tf_op jit(solution)/shard_map/ppermute | solution.py:298
  69.2 44.6 %collective-permute-start.9 = (bf16[768,768]{1,0:T(8,128)(2,1)S(1)}, bf16[768,768]{1,0:T(8,128)(2,1)S(1)}, u32[]{:S(2)}, u32[]{:S(2)}) collective-permute-start(bf16[768,768]{1,0:T(8,128)(2,1)S(1)} %get-tuple-element.24.dn), channel_id=1, source_target_pairs={{0,254},{1,255},{2,0},{3,1},{4,2},{5,3},{6,4},{7,5},{8,6},{9,7},{1... | collective-permute-start | bytes 3538952 | tf_op jit(solution)/shard_map/ppermute | solution.py:298
  78.1 51.7 %collective-permute-start.12 = (bf16[768,256]{1,0:T(8,128)(2,1)S(1)}, bf16[768,256]{1,0:T(8,128)(2,1)S(1)}, u32[]{:S(2)}, u32[]{:S(2)}) collective-permute-start(bf16[768,256]{1,0:T(8,128)(2,1)S(1)} %get-tuple-element.27.after.up), channel_id=1, source_target_pairs={{0,2},{1,3},{2,4},{3,5},{4,6},{5,7},{6,8},{7,9},{8,10},{9,11},{10,... | collective-permute-start | bytes 1179656 | tf_op jit(solution)/shard_map/ppermute | solution.py:298
  78.1 51.7 %collective-permute-start.13 = (bf16[768,256]{1,0:T(8,128)(2,1)S(1)}, bf16[768,256]{1,0:T(8,128)(2,1)S(1)}, u32[]{:S(2)}, u32[]{:S(2)}) collective-permute-start(bf16[768,256]{1,0:T(8,128)(2,1)S(1)} %get-tuple-element.29.dn), channel_id=1, source_target_pairs={{0,254},{1,255},{2,0},{3,1},{4,2},{5,3},{6,4},{7,5},{8,6},{9,7},{1... | collective-permute-start | bytes 1179656 | tf_op jit(solution)/shard_map/ppermute | solution.py:298
  118.6 15.8 %collective-permute-start.14 = (bf16[512,768]{1,0:T(8,128)(2,1)S(1)}, bf16[512,768]{1,0:T(8,128)(2,1)S(1)}, u32[]{:S(2)}, u32[]{:S(2)}) collective-permute-start(bf16[512,768]{1,0:T(8,128)(2,1)S(1)} %get-tuple-element.31), channel_id=1, source_target_pairs={{0,1},{1,0},{2,3},{3,2},{4,5},{5,4},{6,7},{7,6},{8,9},{9,8},{10,11... | collective-permute-start | bytes 2359304 | tf_op jit(solution)/shard_map/ppermute | solution.py:298
  131.1 3.3 %collective-permute-start.15 = (bf16[512,256]{1,0:T(8,128)(2,1)S(1)}, bf16[512,256]{1,0:T(8,128)(2,1)S(1)}, u32[]{:S(2)}, u32[]{:S(2)}) collective-permute-start(bf16[512,256]{1,0:T(8,128)(2,1)S(1)} %get-tuple-element.32), channel_id=1, source_target_pairs={{0,1},{1,0},{2,3},{3,2},{4,5},{5,4},{6,7},{7,6},{8,9},{9,8},{10,11... | collective-permute-start | bytes 786440 | tf_op jit(solution)/shard_map/ppermute | solution.py:298
  134.4 7.4 %collective-permute-start.16 = (bf16[2048,1024]{1,0:T(8,128)(2,1)}, bf16[2048,1024]{1,0:T(8,128)(2,1)S(1)}, u32[]{:S(2)}, u32[]{:S(2)}) collective-permute-start(bf16[2048,1024]{1,0:T(8,128)(2,1)} %tie.1.refs_4_), channel_id=1, source_target_pairs={{0,1},{1,0},{2,3},{3,2},{4,5},{5,4},{6,7},{7,6},{8,9},{9,8},{10,11... | collective-permute-start | bytes 12582920 | tf_op jit(solution)/shard_map/ppermute | solution.py:298
Sparse Core Ops, SparseCore 0:
  35.3 93.9 all-gather.1

commit v2 on v1

v2 whole, which is shorter than its diff:
```python
import functools

import jax
import jax.numpy as jnp
from jax import lax
from jax.experimental import pallas as pl
from jax.experimental.pallas import tpu as pltpu
from jax.sharding import PartitionSpec as P

BLK = 128
PAIR = 2 * BLK
WINDOW = 14 * BLK
WORK = 20 * 1024 * WINDOW
CHUNKS = (512, 512)
EARLY = [(0, i) for i in range(4)] + [(1, i) for i in range(4)] + [(2, 0), (2, 1)]
LATE = [(2, 2), (2, 3)] + [(3, i) for i in range(4)]
ANY = pl.BlockSpec(memory_space=pl.ANY)
HBM = pl.BlockSpec(memory_space=pltpu.HBM)
SMEM = pl.BlockSpec(memory_space=pltpu.SMEM)
VMEM = pl.BlockSpec(memory_space=pltpu.VMEM)


def call(kernel, name, outs, ins, args, scratch=(), aliases=None, flops=0):
    shapes = [jax.ShapeDtypeStruct(shape, jnp.bfloat16) for shape, _ in outs]
    return pl.pallas_call(
        kernel,
        out_shape=shapes,
        in_specs=ins,
        out_specs=[spec for _, spec in outs],
        scratch_shapes=scratch,
        input_output_aliases=aliases or {},
        compiler_params=pltpu.CompilerParams(vmem_limit_bytes=16 * 1024 * 1024),
        cost_estimate=pl.CostEstimate(flops=flops, transcendentals=0, bytes_accessed=0),
        name=name,
    )(*args)


def core_index():
    return lax.axis_index("rows") & 1


def join_kernel(own_ref, got_ref, out_ref, wide):
    odd = (lax.axis_index("rows") >> 3) & 1
    wide[pl.ds(pl.multiple_of(odd * 8, 8), 8), :] = own_ref[...].astype(jnp.float32)
    wide[pl.ds(pl.multiple_of(8 - odd * 8, 8), 8), :] = got_ref[...].astype(jnp.float32)
    out_ref[...] = wide[...].astype(out_ref.dtype)


def join(own, got):
    shape = (16, own.shape[1])
    scratch = [pltpu.VMEM(shape, jnp.float32)]
    return call(join_kernel, "join", [(shape, VMEM)], [VMEM] * 2, (own, got), scratch)[0]


def pack_kernel(*refs):
    pieces, (mine_ref, other_ref, wide) = refs[:4], refs[4:]
    device = lax.axis_index("rows")
    ring = (device >> 1) & 3
    width = mine_ref.shape[1]
    for i, piece in enumerate(pieces):
        rows = piece[...].astype(jnp.float32)
        for j in range(2):
            place = pl.multiple_of(j * 32 + ((ring - i) & 3) * 8, 8)
            wide[pl.ds(place, 8), :] = rows[j * 8 : (j + 1) * 8, :]
    for half, out in ((device & 1, mine_ref), (1 - (device & 1), other_ref)):
        columns = pl.ds(pl.multiple_of(half * width, BLK), width)
        out[...] = wide[:, columns].astype(out.dtype)


def pack(pieces):
    width = pieces[0].shape[1]
    outs = [((64, width // 2), VMEM)] * 2
    scratch = [pltpu.VMEM((64, width), jnp.float32)]
    return call(pack_kernel, "pack", outs, [VMEM] * 4, pieces, scratch)


def slab_kernel(mine_ref, got_ref, after_ref, out_ref, wide):
    core = core_index()
    for ref, side in ((mine_ref, core), (got_ref, 1 - core)):
        rows = ref[...].astype(jnp.float32)
        for i in range(8):
            place = pl.multiple_of(i * 16 + side * 8, 8)
            wide[pl.ds(place, 8), :] = rows[i * 8 : (i + 1) * 8, :]
    out_ref[...] = wide[...].astype(out_ref.dtype)


def slab(mine, got, after):
    shape = (128, mine.shape[1])
    scratch = [pltpu.VMEM(shape, jnp.float32)]
    ins = [VMEM, VMEM, ANY]
    return call(slab_kernel, "slab", [(shape, VMEM)], ins, (mine, got, after), scratch)[0]


def split_kernel(x_ref, out_ref, sem):
    width = out_ref.shape[1]
    columns = pl.ds(pl.multiple_of((1 - core_index()) * width, BLK), width)
    copy = pltpu.make_async_copy(x_ref.at[:, columns], out_ref, sem)
    copy.start()
    copy.wait()


def split(x_states):
    shape = (x_states.shape[0], x_states.shape[1] // 2)
    scratch = [pltpu.SemaphoreType.DMA]
    return call(split_kernel, "split", [(shape, VMEM)], [HBM], (x_states,), scratch)[0]


def assemble_kernel(chunks, x_ref, partner_ref, after_ref, *rest):
    outs, sems = rest[:-1], rest[-1]
    core = core_index()
    width = sum(chunks)

    def fill(mine):
        copies, at = [], 0
        for i, n in enumerate(chunks):
            columns = pl.ds(pl.multiple_of(core * width + at, BLK), n)
            up, dn = outs[2 * i], outs[2 * i + 1]
            if mine == 0:
                targets = ((0, 512, dn, 0), (256, 256, up, 0))
            else:
                targets = ((0, 256, dn, 512), (0, 512, up, 256))
            for j, (source, rows, out, place) in enumerate(targets):
                copy = pltpu.make_async_copy(
                    x_ref.at[pl.ds(source, rows), columns],
                    out.at[pl.ds(place, rows)],
                    sems.at[2 * i + j],
                )
                copy.start()
                copies.append(copy)
            at += n
        at = 0
        for i, n in enumerate(chunks):
            up, dn = outs[2 * i], outs[2 * i + 1]
            if mine == 0:
                dn[512:768, :] = partner_ref[0:256, at : at + n]
                up[256:768, :] = partner_ref[:, at : at + n]
            else:
                dn[0:512, :] = partner_ref[:, at : at + n]
                up[0:256, :] = partner_ref[256:512, at : at + n]
            at += n
        for copy in copies:
            copy.wait()

    @pl.when(core == 0)
    def _():
        fill(0)

    @pl.when(core == 1)
    def _():
        fill(1)


def assemble(x_states, partner, after, chunks):
    outs = [((768, n), VMEM) for n in chunks for _ in range(2)]
    scratch = [pltpu.SemaphoreType.DMA((2 * len(chunks),))]
    kernel = functools.partial(assemble_kernel, chunks)
    return call(kernel, "assemble", outs, [HBM, VMEM, ANY], (x_states, partner, after), scratch)


def build_kernel(device_count, col_ref, send_ref, h_ref, after_ref, *out_refs):
    device = lax.axis_index("rows")
    for out_ref in out_refs:
        out_ref[...] = jnp.zeros_like(out_ref)
    block_count = device_count * 4
    for row in range(4):
        band, half = row // 2, row % 2
        for k in range(12):
            column = col_ref[row, k]
            owner = lax.shift_right_logical(column, 2)
            local = column & 3
            offset = ((device - owner + 2) & (device_count - 1)) - 2
            slot = jnp.clip(jnp.where(offset > 0, offset - 1, 1 - offset), 0, 3)
            counts = offset == 0
            for j in range(4):
                counts = counts | (send_ref[slot, j, owner] == local)
            shift = ((column - (device * 4 + row) + 6) & (block_count - 1)) + half
            place = pl.ds(pl.multiple_of(shift * BLK, BLK), BLK)

            @pl.when(counts)
            def _(out_ref=out_refs[band], half=half, row=row, k=k, place=place):
                out_ref[half * BLK : (half + 1) * BLK, place] = h_ref[row, k]


def build(h_blocks, col_blocks, send_list, after, device_count):
    kernel = functools.partial(build_kernel, device_count)
    args = (col_blocks, send_list.transpose(1, 2, 0), h_blocks, after)
    outs = [((PAIR, WINDOW), VMEM)] * 2
    return call(kernel, "build_bands", outs, [SMEM, SMEM, VMEM, ANY], args)


def merge_kernel(*refs):
    out_ref = refs[-1]
    core = core_index()
    for i in range(2):
        out_ref[core * 2 + i] = refs[i][...]
        out_ref[2 - core * 2 + i] = refs[2 + i][...]


def merge(own, partner):
    outs = [((4, PAIR, WINDOW), VMEM)]
    return call(merge_kernel, "merge_bands", outs, [VMEM] * 4, (*own, *partner))[0]


def times_bands(g, columns, bands, left, dn, up, right):
    edge = 768 - g * PAIR

    def dot(start, stop, states):
        return jnp.dot(bands[g, :, start:stop], states, preferred_element_type=jnp.float32)

    total = dot(edge, edge + 768, dn[:, columns])
    total += dot(edge + 768, edge + 1024, up[512:768, columns])
    if g < 3:
        total += dot(0, edge, left[g * PAIR :, columns])
    if g > 0:
        total += dot(edge + 1024, WINDOW, right[: g * PAIR, columns])
    return total


def own_rows(g, columns, dn, up):
    rows = dn[g * PAIR : (g + 1) * PAIR, columns] if g < 3 else up[512:768, columns]
    return rows.astype(jnp.float32)


def first_kernel(columns, center, half, bands, left, dn, up, right, *rest):
    out_up, out_dn = rest[-2:]
    for g in range(4):
        total = times_bands(g, columns, bands, left, dn, up, right)
        value = (total - center[0] * own_rows(g, columns, dn, up)) / half[0]
        value = value.astype(jnp.bfloat16)
        if g < 3:
            out_dn[g * PAIR : (g + 1) * PAIR, :] = value
        if g > 0:
            out_up[(g - 1) * PAIR : g * PAIR, :] = value


def second_kernel(
    columns, center, half, bands, left, dn, up, right, after, xdn, xup, out_mine, out_other, outs
):
    for g in range(4):
        total = times_bands(g, columns, bands, left, dn, up, right)
        value = 2.0 * (total - center[0] * own_rows(g, columns, dn, up)) / half[0]
        value -= own_rows(g, columns, xdn, xup)
        outs[g * PAIR : (g + 1) * PAIR, :] = value.astype(jnp.bfloat16)
    core = core_index()
    out_mine[...] = outs[pl.ds(core * 512, 512), :]
    out_other[...] = outs[pl.ds(512 - core * 512, 512), :]


def first_pass(columns, *args):
    n = columns.stop - columns.start
    outs = [((768, n), VMEM)] * 2
    ins = [SMEM] * 2 + [VMEM] * 5 + [ANY] * (len(args) - 7)
    kernel = functools.partial(first_kernel, columns)
    return call(kernel, "first_pass", outs, ins, args, flops=WORK * n // 20)


def second_pass(columns, *args):
    n = columns.stop - columns.start
    outs = [((512, n), VMEM)] * 2
    ins = [SMEM] * 2 + [VMEM] * 5 + [ANY] + [VMEM] * 2
    scratch = [pltpu.VMEM((1024, n), jnp.bfloat16)]
    kernel = functools.partial(second_kernel, columns)
    return call(kernel, "second_pass", outs, ins, args, scratch, flops=WORK * n)


def tie_kernel(*refs):
    pass


def tie(array, after):
    return call(tie_kernel, "tie", [(array.shape, ANY)], [ANY] * 2, (array, after), (), {0: 0})[0]


def stack_kernel(count, *refs):
    out, at = refs[-1], 0
    for ref in refs[:count]:
        out[at : at + ref.shape[0], :] = ref[...]
        at += ref.shape[0]


def stack(pieces, *after):
    shape = (sum(piece.shape[0] for piece in pieces), pieces[0].shape[1])
    kernel = functools.partial(stack_kernel, len(pieces))
    ins = [VMEM] * len(pieces) + [ANY] * len(after)
    return call(kernel, "stack", [(shape, VMEM)], ins, (*pieces, *after))[0]


def z_step(y):
    return 1 if y < 2 else -1


def x_step(y, z, z_count, forward):
    if forward:
        return -1 if (y == 3 and z == 0) else 1
    return 1 if (y == 0 and z == z_count - 1) else -1


def rotate_kernel(chunks, own_half, *refs):
    count = len(chunks)
    own, got, parts = refs[:count], refs[count : 2 * count], refs[2 * count : 2 * count + 2]
    out_ref, rot, outs, sems = refs[-4:]
    device = lax.axis_index("rows")
    core, y = device & 1, (device >> 1) & 3
    z, x = (device >> 3) & 7, device >> 6
    z_way = jnp.where(y < 2, 1, -1)
    ways = (
        jnp.where((y == 3) & (z == 0), -1, 1),
        jnp.where((y == 0) & (z == 7), 1, -1),
    )
    for part, pieces in zip(parts, (EARLY, LATE)):
        for at, (j, i) in enumerate(pieces):
            from_x = (x - ways[j % 2] * i) & 3
            from_z = ((z >> 1) - z_way * j) & 3
            place = pl.multiple_of(from_x * 512 + from_z * 128, 128)
            rot[pl.ds(place, 128), :] = part[at * 128 : (at + 1) * 128, :]
    width = sum(chunks)
    tile = 256
    half = core if own_half else 1 - core
    stores = []
    for t in range(width // tile):
        columns = slice(t * tile, (t + 1) * tile)
        total, at = 0.0, 0
        for i, n in enumerate(chunks):
            for piece, side in ((own[i], core), (got[i], 1 - core)):
                rows = pl.ds(pl.multiple_of(side * width + at, BLK), n)
                total += jnp.dot(piece[...], rot[rows, columns], preferred_element_type=jnp.float32)
            at += n
        outs[:, columns] = total.astype(jnp.bfloat16)
        target = pl.ds(pl.multiple_of(half * width + t * tile, BLK), tile)
        stores.append(
            pltpu.make_async_copy(outs.at[:, columns], out_ref.at[:, target], sems.at[t])
        )
        stores[-1].start()
    for store in stores:
        store.wait()


def rotate(own, got, parts, chunks, out=None):
    width = sum(chunks)
    kernel = functools.partial(rotate_kernel, chunks, out is None)
    args, ins = [*own, *got, *parts], [VMEM] * (2 * len(chunks) + 2)
    aliases = None
    if out is not None:
        aliases = {len(args): 0}
        args.append(out)
        ins.append(HBM)
    scratch = [
        pltpu.VMEM((2 * width, width), jnp.bfloat16),
        pltpu.VMEM((512, width), jnp.bfloat16),
        pltpu.SemaphoreType.DMA((width // 256,)),
    ]
    return call(kernel, "rotate", [((512, 2 * width), HBM)], ins, args, scratch, aliases)[0]


def local(x_states, h_blocks, col_blocks, send_list, center, half_width, rotation):
    count = lax.axis_size("rows")
    swap = [(i, i ^ 1) for i in range(count)]
    onward = [(i, (i + 2) % count) for i in range(count)]
    backward = [(i, (i - 2) % count) for i in range(count)]

    def move(array, route):
        return lax.ppermute(array, "rows", route)

    def ring(step):
        return [(8 * (i // 8) + (i + 2 * step) % 8, i) for i in range(count)]

    def place(i):
        return i >> 6, (i >> 3) & 7, (i >> 1) & 3

    def along_z(i):
        x, z, y = place(i)
        return x * 64 + (z + 2 * z_step(y)) % 8 * 8 + i % 8

    def along_x(i, forward):
        x, z, y = place(i)
        return (x + x_step(y, z, 8, forward)) % 4 * 64 + i % 64

    z_route = [(i, along_z(i)) for i in range(count)]
    x_routes = [[(i, along_x(i, forward)) for i in range(count)] for forward in (True, False)]

    partner = move(split(x_states), swap)
    rotation = join(rotation, move(rotation, [(i, i ^ 8) for i in range(count)]))
    mine, other = pack([rotation] + [move(rotation, ring(step)) for step in (-1, -2, -3)])
    up, dn = assemble(x_states, partner, mine, (sum(CHUNKS),))
    left, right = move(up, onward), move(dn, backward)
    rows = slab(mine, move(other, swap), up)
    bands = build(h_blocks, col_blocks, send_list, rows, count)
    bands = merge(bands, [move(band, swap) for band in bands])
    slabs = [rows, tie(move(rows, z_route), bands)]
    slabs.append(move(slabs[1], z_route))
    chains = [[stack([rows], bands)], [slabs[1]], [slabs[2]]]

    def on(j, steps):
        for _ in range(steps):
            chains[j].append(move(chains[j][-1], x_routes[j % 2]))

    on(0, 3)
    on(1, 2)

    fixed = (center, half_width, bands)

    starts = [sum(CHUNKS[:i]) for i in range(len(CHUNKS))]
    columns = [slice(start, start + n) for start, n in zip(starts, CHUNKS)]
    every = slice(0, sum(CHUNKS))
    first_up, first_dn = first_pass(every, *fixed, left, dn, up, right, slabs[2], chains[0][3], chains[1][2])
    halo = (move(first_up, onward), first_dn, first_up, move(first_dn, backward))
    after = first_up
    chains[1][2], chains[2][0] = tie(chains[1][2], after), tie(chains[2][0], after)
    chains.append([move(chains[2][0], z_route)])
    on(1, 1)
    on(2, 3)
    on(3, 3)
    own, got = [], []
    for part in columns:
        mine, other = second_pass(part, *fixed, *halo, after, dn, up)
        after = mine
        own.append(mine)
        got.append(move(other, swap))
    parts = [
        stack([chains[j][i] for j, i in EARLY]),
        stack([chains[j][i] for j, i in LATE]),
    ]
    out = rotate(own, got, parts, CHUNKS)
    return rotate(own, got, [move(part, swap) for part in parts], CHUNKS, out)


def solution(mesh):
    placed = (
        P("rows", None),
        P("rows", None, None, None),
        P("rows", None),
        P(),
        P(),
        P(),
        P("rows", None),
    )
    return jax.shard_map(
        local, mesh=mesh, in_specs=placed, out_specs=P("rows", None), check_vma=False
    )
```

time: 152 us -> 136 us (0.89)
  the two profiles are of different devices: /device:TPU:1 before, /device:TPU:225 now
where the time goes in v2:
time: 136 us
  waiting for transfers between devices  82.8 us (61%)
  starting transfers between devices  29.6 us (22%)
  Pallas kernels  19.2 us (14%)
  local copies, waits for them, and re-layouts  2.34 us (2%)
  between operations  1.66 us (1%)
    ppermute x31, waiting for transfers between devices, move(): return lax.ppermute(array, 'rows', route)  82.8 us
    ppermute x31, starting transfers between devices, move(): return lax.ppermute(array, 'rows', route)  29.6 us
    pallas_call x18, Pallas kernels, call(): pl.pallas_call(kernel, out_shape=shapes, in_specs=ins, out_specs=[spec fo...  19.2 us
  transfers between devices with their start and end apart: 31, of which 17 were waited for; matrix products, arithmetic and copies ran while one was open for 0% of the time, Pallas kernels for 7%

profile of v2, /device:TPU:225, one launch (start us, length us, event | category | flops | bytes accessed | tf_op | source)
XLA Modules:
  0.0 135.5 jit_solution(6691471181673979985)
XLA Ops:
  0.0 1.6 %copy-done = bf16[512,2048]{1,0:T(8,128)(2,1)S(1)} copy-done((bf16[512,2048]{1,0:T(8,128)(2,1)S(1)}, bf16[512,2048]{1,0:T(8,128)(2,1)}, u32[]{:S(2)}) %copy-start) | copy-done | bytes 2097176
  1.6 0.2 split.1
  1.8 0.8 collective-permute-start.5
  2.6 0.7 collective-permute-start
  3.3 2.0 %collective-permute-done.got_ref = bf16[8,2048]{1,0:T(8,128)(2,1)S(1)} collective-permute-done((bf16[8,2048]{1,0:T(8,128)(2,1)S(1)}, bf16[8,2048]{1,0:T(8,128)(2,1)S(1)}, u32[]{:S(2)}, u32[]{:S(2)}) %collective-permute-start) | collective-permute-done | bytes 32800 | tf_op jit(solution)/shard_map/ppermute | solution.py:362
  5.4 1.4 %collective-permute-start.1 = (bf16[16,2048]{1,0:T(8,128)(2,1)S(1)}, bf16[16,2048]{1,0:T(8,128)(2,1)S(1)}, u32[]{:S(2)}, u32[]{:S(2)}) collective-permute-start(bf16[16,2048]{1,0:T(8,128)(2,1)S(1)} %join.1.refs_0_), channel_id=1, source_target_pairs={{6,0},{7,1},{0,2},{1,3},{2,4},{3,5},{4,6},{5,7},{14,8},{15,9},{8,1... | collective-permute-start | bytes 196616 | tf_op jit(solution)/shard_map/ppermute | solution.py:362
  6.7 2.6 %collective-permute-start.2 = (bf16[16,2048]{1,0:T(8,128)(2,1)S(1)}, bf16[16,2048]{1,0:T(8,128)(2,1)S(1)}, u32[]{:S(2)}, u32[]{:S(2)}) collective-permute-start(bf16[16,2048]{1,0:T(8,128)(2,1)S(1)} %join.1.refs_0_), channel_id=1, source_target_pairs={{4,0},{5,1},{6,2},{7,3},{0,4},{1,5},{2,6},{3,7},{12,8},{13,9},{14,... | collective-permute-start | bytes 196616 | tf_op jit(solution)/shard_map/ppermute | solution.py:362
  9.4 1.1 collective-permute-start.3
  10.4 1.3 collective-permute-done.2.refs_2_
  11.8 1.5 %collective-permute-done.3.refs_3_ = bf16[16,2048]{1,0:T(8,128)(2,1)S(1)} collective-permute-done((bf16[16,2048]{1,0:T(8,128)(2,1)S(1)}, bf16[16,2048]{1,0:T(8,128)(2,1)S(1)}, u32[]{:S(2)}, u32[]{:S(2)}) %collective-permute-start.3) | collective-permute-done | bytes 65568 | tf_op jit(solution)/shard_map/ppermute | solution.py:362
  13.3 2.6 %collective-permute-start.4 = (bf16[64,1024]{1,0:T(8,128)(2,1)S(1)}, bf16[64,1024]{1,0:T(8,128)(2,1)S(1)}, u32[]{:S(2)}, u32[]{:S(2)}) collective-permute-start(bf16[64,1024]{1,0:T(8,128)(2,1)S(1)} %get-tuple-element.18), channel_id=1, source_target_pairs={{0,1},{1,0},{2,3},{3,2},{4,5},{5,4},{6,7},{7,6},{8,9},{9,8},{10,11... | collective-permute-start | bytes 393224 | tf_op jit(solution)/shard_map/ppermute | solution.py:362
  16.0 0.4 assemble.1
  16.4 0.6 collective-permute-done.4.got_ref
  17.0 0.7 copy-done.2
  17.7 2.1 %build_bands.1 = (bf16[256,1792]{1,0:T(8,128)(2,1)S(1)}, bf16[256,1792]{1,0:T(8,128)(2,1)S(1)}) custom-call(s32[4,12]{1,0:T(4,128)S(1)} %copy-done.5, s32[4,4,256]{2,1,0:T(4,128)S(1)} %bitcast.1, bf16[4,12,128,128]{3,2,1,0:T(8,128)(2,1)S(1)} %copy-done.2, bf16[128,1024]{1,0:T(8,128)(2,1)S(1)} %slab.1.after_ref.refs_0_), custom_call_target="tpu_custom_call" | custom-call | tf_op jit(solution)/shard_map/build_bands/pallas_call | solution.py:25
  19.9 0.1 collective-permute-start.6
  20.0 0.5 collective-permute-start.7
  20.5 3.5 %collective-permute-start.9 = (bf16[768,1024]{1,0:T(8,128)(2,1)S(1)}, bf16[768,1024]{1,0:T(8,128)(2,1)S(1)}, u32[]{:S(2)}, u32[]{:S(2)}) collective-permute-start(bf16[768,1024]{1,0:T(8,128)(2,1)S(1)} %get-tuple-element.22.dn.xdn), channel_id=1, source_target_pairs={{0,254},{1,255},{2,0},{3,1},{4,2},{5,3},{6,4},{7,5},{8,6},{9,7},{1... | collective-permute-start | bytes 4718600 | tf_op jit(solution)/shard_map/ppermute | solution.py:362
  24.1 0.2 merge_bands.1.refs_1_.bands
  24.4 1.3 collective-permute-start.12
  25.7 12.7 %collective-permute-done.10.refs_0_ = bf16[128,1024]{1,0:T(8,128)(2,1)S(1)} collective-permute-done((bf16[128,1024]{1,0:T(8,128)(2,1)S(1)}, bf16[128,1024]{1,0:T(8,128)(2,1)S(1)}, u32[]{:S(2)}, u32[]{:S(2)}) %collective-permute-start.10) | collective-permute-done | bytes 262176 | tf_op jit(solution)/shard_map/ppermute | solution.py:362
  38.4 0.2 collective-permute-start.13
  38.6 0.2 collective-permute-start.11
  38.8 7.6 %collective-permute-done.15.refs_5_ = bf16[128,1024]{1,0:T(8,128)(2,1)S(1)} collective-permute-done((bf16[128,1024]{1,0:T(8,128)(2,1)S(1)}, bf16[128,1024]{1,0:T(8,128)(2,1)S(1)}, u32[]{:S(2)}, u32[]{:S(2)}) %collective-permute-start.15) | collective-permute-done | bytes 262176 | tf_op jit(solution)/shard_map/ppermute | solution.py:362
  46.3 5.6 %collective-permute-done.13.refs_2_ = bf16[128,1024]{1,0:T(8,128)(2,1)S(1)} collective-permute-done((bf16[128,1024]{1,0:T(8,128)(2,1)S(1)}, bf16[128,1024]{1,0:T(8,128)(2,1)S(1)}, u32[]{:S(2)}, u32[]{:S(2)}) %collective-permute-start.13) | collective-permute-done | bytes 262176 | tf_op jit(solution)/shard_map/ppermute | solution.py:362
  53.3 4.3 %collective-permute-done.16.rest_2_.refs_0_ = bf16[128,1024]{1,0:T(8,128)(2,1)S(1)} collective-permute-done((bf16[128,1024]{1,0:T(8,128)(2,1)S(1)}, bf16[128,1024]{1,0:T(8,128)(2,1)S(1)}, u32[]{:S(2)}, u32[]{:S(2)}) %collective-permute-start.16) | collective-permute-done | bytes 262176 | tf_op jit(solution)/shard_map/ppermute | solution.py:362
  57.6 1.0 collective-permute-done.8.left
  58.6 4.6 %collective-permute-done.14.rest_1_.refs_3_ = bf16[128,1024]{1,0:T(8,128)(2,1)S(1)} collective-permute-done((bf16[128,1024]{1,0:T(8,128)(2,1)S(1)}, bf16[128,1024]{1,0:T(8,128)(2,1)S(1)}, u32[]{:S(2)}, u32[]{:S(2)}) %collective-permute-start.14) | collective-permute-done | bytes 262176 | tf_op jit(solution)/shard_map/ppermute | solution.py:362
  63.2 4.0 %first_pass.1 = (bf16[768,1024]{1,0:T(8,128)(2,1)S(1)}, bf16[768,1024]{1,0:T(8,128)(2,1)S(1)}) custom-call(f32[1]{0:T(128)S(6)} %copy.16.center, f32[1]{0:T(128)S(6)} %copy.17.half, bf16[4,256,1792]{2,1,0:T(8,128)(2,1)S(1)} %merge_bands.1.refs_1_.bands, bf16[768,1024]{1,0:T(8,128)(2,1)S(1)} %collective-permute-done.8.left, ...), custom_call_target="tpu_custom_call" | custom-call | flops 1879048192 | tf_op jit(solution)/shard_map/first_pass/pallas_call | solution.py:25
  67.2 0.1 collective-permute-start.17
  67.3 3.6 %collective-permute-start.18 = (bf16[768,1024]{1,0:T(8,128)(2,1)S(1)}, bf16[768,1024]{1,0:T(8,128)(2,1)S(1)}, u32[]{:S(2)}, u32[]{:S(2)}) collective-permute-start(bf16[768,1024]{1,0:T(8,128)(2,1)S(1)} %get-tuple-element.24.dn), channel_id=1, source_target_pairs={{0,254},{1,255},{2,0},{3,1},{4,2},{5,3},{6,4},{7,5},{8,6},{9,7},{1... | collective-permute-start | bytes 4718600 | tf_op jit(solution)/shard_map/ppermute | solution.py:362
  70.9 12.3 %collective-permute-done.26.refs_2_ = bf16[128,1024]{1,0:T(8,128)(2,1)S(1)} collective-permute-done((bf16[128,1024]{1,0:T(8,128)(2,1)S(1)}, bf16[128,1024]{1,0:T(8,128)(2,1)S(1)}, u32[]{:S(2)}, u32[]{:S(2)}) %collective-permute-start.26) | collective-permute-done | bytes 262176 | tf_op jit(solution)/shard_map/ppermute | solution.py:362
  83.1 6.7 %collective-permute-done.27.refs_3_ = bf16[128,1024]{1,0:T(8,128)(2,1)S(1)} collective-permute-done((bf16[128,1024]{1,0:T(8,128)(2,1)S(1)}, bf16[128,1024]{1,0:T(8,128)(2,1)S(1)}, u32[]{:S(2)}, u32[]{:S(2)}) %collective-permute-start.27) | collective-permute-done | bytes 262176 | tf_op jit(solution)/shard_map/ppermute | solution.py:362
  89.8 5.3 %collective-permute-done.24.refs_0_ = bf16[128,1024]{1,0:T(8,128)(2,1)S(1)} collective-permute-done((bf16[128,1024]{1,0:T(8,128)(2,1)S(1)}, bf16[128,1024]{1,0:T(8,128)(2,1)S(1)}, u32[]{:S(2)}, u32[]{:S(2)}) %collective-permute-start.24) | collective-permute-done | bytes 262176 | tf_op jit(solution)/shard_map/ppermute | solution.py:362
  95.2 5.6 %collective-permute-done.28.refs_4_ = bf16[128,1024]{1,0:T(8,128)(2,1)S(1)} collective-permute-done((bf16[128,1024]{1,0:T(8,128)(2,1)S(1)}, bf16[128,1024]{1,0:T(8,128)(2,1)S(1)}, u32[]{:S(2)}, u32[]{:S(2)}) %collective-permute-start.28) | collective-permute-done | bytes 262176 | tf_op jit(solution)/shard_map/ppermute | solution.py:362
  100.8 5.6 %collective-permute-done.21.refs_7_ = bf16[128,1024]{1,0:T(8,128)(2,1)S(1)} collective-permute-done((bf16[128,1024]{1,0:T(8,128)(2,1)S(1)}, bf16[128,1024]{1,0:T(8,128)(2,1)S(1)}, u32[]{:S(2)}, u32[]{:S(2)}) %collective-permute-start.21) | collective-permute-done | bytes 262176 | tf_op jit(solution)/shard_map/ppermute | solution.py:362
  106.4 0.2 stack.4.refs_4_
  106.6 6.7 %collective-permute-start.23 = (bf16[1280,1024]{1,0:T(8,128)(2,1)S(1)}, bf16[1280,1024]{1,0:T(8,128)(2,1)S(1)}, u32[]{:S(2)}, u32[]{:S(2)}) collective-permute-start(bf16[1280,1024]{1,0:T(8,128)(2,1)S(1)} %stack.4.refs_4_), channel_id=1, source_target_pairs={{0,1},{1,0},{2,3},{3,2},{4,5},{5,4},{6,7},{7,6},{8,9},{9,8},{10,11... | collective-permute-start | bytes 7864328 | tf_op jit(solution)/shard_map/ppermute | solution.py:362
  113.2 4.4 %collective-permute-done.29.refs_5_ = bf16[128,1024]{1,0:T(8,128)(2,1)S(1)} collective-permute-done((bf16[128,1024]{1,0:T(8,128)(2,1)S(1)}, bf16[128,1024]{1,0:T(8,128)(2,1)S(1)}, u32[]{:S(2)}, u32[]{:S(2)}) %collective-permute-start.29) | collective-permute-done | bytes 262176 | tf_op jit(solution)/shard_map/ppermute | solution.py:362
  117.6 0.1 stack.5.refs_5_
  117.8 3.6 %collective-permute-start.30 = (bf16[768,1024]{1,0:T(8,128)(2,1)S(1)}, bf16[768,1024]{1,0:T(8,128)(2,1)S(1)}, u32[]{:S(2)}, u32[]{:S(2)}) collective-permute-start(bf16[768,1024]{1,0:T(8,128)(2,1)S(1)} %stack.5.refs_5_), channel_id=1, source_target_pairs={{0,1},{1,0},{2,3},{3,2},{4,5},{5,4},{6,7},{7,6},{8,9},{9,8},{10,11... | collective-permute-start | bytes 4718600 | tf_op jit(solution)/shard_map/ppermute | solution.py:362
  121.3 2.4 %second_pass.2 = (bf16[512,512]{1,0:T(8,128)(2,1)S(1)}, bf16[512,512]{1,0:T(8,128)(2,1)S(1)}) custom-call(f32[1]{0:T(128)S(6)} %copy.16.center, f32[1]{0:T(128)S(6)} %copy.17.half, bf16[4,256,1792]{2,1,0:T(8,128)(2,1)S(1)} %merge_bands.1.refs_1_.bands, bf16[768,1024]{1,0:T(8,128)(2,1)S(1)} %collective-permute-done.17.left, ...), custom_call_target="tpu_custom_call" | custom-call | flops 18790481920 | tf_op jit(solution)/shard_map/second_pass/pallas_call | solution.py:25
  123.7 0.1 collective-permute-start.19
  123.8 2.4 %second_pass.3 = (bf16[512,512]{1,0:T(8,128)(2,1)S(1)}, bf16[512,512]{1,0:T(8,128)(2,1)S(1)}) custom-call(f32[1]{0:T(128)S(6)} %copy.16.center, f32[1]{0:T(128)S(6)} %copy.17.half, bf16[4,256,1792]{2,1,0:T(8,128)(2,1)S(1)} %merge_bands.1.refs_1_.bands, bf16[768,1024]{1,0:T(8,128)(2,1)S(1)} %collective-permute-done.17.left, ...), custom_call_target="tpu_custom_call" | custom-call | flops 18790481920 | tf_op jit(solution)/shard_map/second_pass/pallas_call | solution.py:25
  126.2 0.6 collective-permute-start.20
  126.8 1.5 %collective-permute-done.20.refs_3_ = bf16[512,512]{1,0:T(8,128)(2,1)S(1)} collective-permute-done((bf16[512,512]{1,0:T(8,128)(2,1)S(1)}, bf16[512,512]{1,0:T(8,128)(2,1)S(1)}, u32[]{:S(2)}, u32[]{:S(2)}) %collective-permute-start.20) | collective-permute-done | bytes 524320 | tf_op jit(solution)/shard_map/ppermute | solution.py:362
  128.3 3.5 %rotate.2.refs_6_ = bf16[512,2048]{1,0:T(8,128)(2,1)} custom-call(bf16[512,512]{1,0:T(8,128)(2,1)S(1)} %get-tuple-element.25.after.refs_0_, bf16[512,512]{1,0:T(8,128)(2,1)S(1)} %get-tuple-element.26.refs_1_, bf16[512,512]{1,0:T(8,128)(2,1)S(1)} %collective-permute-done.19.refs_2_, bf16[512,512]{1,0:T(8,128)(2,1)S(1)} %collective-permute-done.20.refs_3_, ...), custom_call_target="tpu_custom_call" | custom-call | tf_op jit(solution)/shard_map/rotate/pallas_call | solution.py:25
  131.8 3.5 %rotate.3 = bf16[512,2048]{1,0:T(8,128)(2,1)} custom-call(bf16[512,512]{1,0:T(8,128)(2,1)S(1)} %get-tuple-element.25.after.refs_0_, bf16[512,512]{1,0:T(8,128)(2,1)S(1)} %get-tuple-element.26.refs_1_, bf16[512,512]{1,0:T(8,128)(2,1)S(1)} %collective-permute-done.19.refs_2_, ...), custom_call_target="tpu_custom_call", output_to_operand_aliasing={{}: (6, {})} | custom-call | tf_op jit(solution)/shard_map/rotate/pallas_call | solution.py:25
  (44 shorter events, 0.3 us)
Async XLA Ops:
  0.0 1.6 %copy-start = (bf16[512,2048]{1,0:T(8,128)(2,1)S(1)}, bf16[512,2048]{1,0:T(8,128)(2,1)}, u32[]{:S(2)}) copy-start(bf16[512,2048]{1,0:T(8,128)(2,1)} %x_ref.3) | copy-start | bytes 6291460
  1.6 1.0 copy-start.3
  1.6 14.4 %copy-start.1 = (bf16[512,2048]{1,0:T(8,128)(2,1)S(1)}, bf16[512,2048]{1,0:T(8,128)(2,1)}, u32[]{:S(2)}) copy-start(bf16[512,2048]{1,0:T(8,128)(2,1)} %x_ref.3) | copy-start | bytes 6291460
  1.8 14.1 %collective-permute-start.5 = (bf16[512,1024]{1,0:T(8,128)(2,1)S(1)}, bf16[512,1024]{1,0:T(8,128)(2,1)S(1)}, u32[]{:S(2)}, u32[]{:S(2)}) collective-permute-start(bf16[512,1024]{1,0:T(8,128)(2,1)S(1)} %split.1), channel_id=1, source_target_pairs={{0,1},{1,0},{2,3},{3,2},{4,5},{5,4},{6,7},{7,6},{8,9},{9,8},{10,11... | collective-permute-start | bytes 3145736 | tf_op jit(solution)/shard_map/ppermute | solution.py:362
  2.6 2.8 %collective-permute-start = (bf16[8,2048]{1,0:T(8,128)(2,1)S(1)}, bf16[8,2048]{1,0:T(8,128)(2,1)S(1)}, u32[]{:S(2)}, u32[]{:S(2)}) collective-permute-start(bf16[8,2048]{1,0:T(8,128)(2,1)S(1)} %copy-done.3), channel_id=1, source_target_pairs={{0,8},{1,9},{2,10},{3,11},{4,12},{5,13},{6,14},{7,15},{8,0},{9,1},... | collective-permute-start | bytes 98312 | tf_op jit(solution)/shard_map/ppermute | solution.py:362
  5.4 5.1 %collective-permute-start.1 = (bf16[16,2048]{1,0:T(8,128)(2,1)S(1)}, bf16[16,2048]{1,0:T(8,128)(2,1)S(1)}, u32[]{:S(2)}, u32[]{:S(2)}) collective-permute-start(bf16[16,2048]{1,0:T(8,128)(2,1)S(1)} %join.1.refs_0_), channel_id=1, source_target_pairs={{6,0},{7,1},{0,2},{1,3},{2,4},{3,5},{4,6},{5,7},{14,8},{15,9},{8,1... | collective-permute-start | bytes 196616 | tf_op jit(solution)/shard_map/ppermute | solution.py:362
  6.7 5.0 %collective-permute-start.2 = (bf16[16,2048]{1,0:T(8,128)(2,1)S(1)}, bf16[16,2048]{1,0:T(8,128)(2,1)S(1)}, u32[]{:S(2)}, u32[]{:S(2)}) collective-permute-start(bf16[16,2048]{1,0:T(8,128)(2,1)S(1)} %join.1.refs_0_), channel_id=1, source_target_pairs={{4,0},{5,1},{6,2},{7,3},{0,4},{1,5},{2,6},{3,7},{12,8},{13,9},{14,... | collective-permute-start | bytes 196616 | tf_op jit(solution)/shard_map/ppermute | solution.py:362
  9.4 3.9 %collective-permute-start.3 = (bf16[16,2048]{1,0:T(8,128)(2,1)S(1)}, bf16[16,2048]{1,0:T(8,128)(2,1)S(1)}, u32[]{:S(2)}, u32[]{:S(2)}) collective-permute-start(bf16[16,2048]{1,0:T(8,128)(2,1)S(1)} %join.1.refs_0_), channel_id=1, source_target_pairs={{2,0},{3,1},{4,2},{5,3},{6,4},{7,5},{0,6},{1,7},{10,8},{11,9},{12,... | collective-permute-start | bytes 196616 | tf_op jit(solution)/shard_map/ppermute | solution.py:362
  13.3 3.6 %collective-permute-start.4 = (bf16[64,1024]{1,0:T(8,128)(2,1)S(1)}, bf16[64,1024]{1,0:T(8,128)(2,1)S(1)}, u32[]{:S(2)}, u32[]{:S(2)}) collective-permute-start(bf16[64,1024]{1,0:T(8,128)(2,1)S(1)} %get-tuple-element.18), channel_id=1, source_target_pairs={{0,1},{1,0},{2,3},{3,2},{4,5},{5,4},{6,7},{7,6},{8,9},{9,8},{10,11... | collective-permute-start | bytes 393224 | tf_op jit(solution)/shard_map/ppermute | solution.py:362
  16.3 1.4 %copy-start.2 = (bf16[4,12,128,128]{3,2,1,0:T(8,128)(2,1)S(1)}, bf16[4,12,128,128]{3,2,1,0:T(8,128)(2,1)}, u32[]{:S(2)}) copy-start(bf16[4,12,128,128]{3,2,1,0:T(8,128)(2,1)} %h_ref.1) | copy-start | bytes 4718596
  16.3 1.4 %copy-start.4 = (s32[256,4,4]{0,2,1:T(4,128)S(1)}, s32[256,4,4]{0,2,1:T(4,128)}, u32[]{:S(2)}) copy-start(s32[256,4,4]{0,2,1:T(4,128)} %param.10) | copy-start | bytes 49156
  16.4 1.4 %copy-start.5 = (s32[4,12]{1,0:T(4,128)S(1)}, s32[4,12]{1,0:T(4,128)}, u32[]{:S(2)}) copy-start(s32[4,12]{1,0:T(4,128)} %col_ref.1) | copy-start | bytes 580
  19.9 4.2 %collective-permute-start.6 = (bf16[256,1792]{1,0:T(8,128)(2,1)S(1)}, bf16[256,1792]{1,0:T(8,128)(2,1)S(1)}, u32[]{:S(2)}, u32[]{:S(2)}) collective-permute-start(bf16[256,1792]{1,0:T(8,128)(2,1)S(1)} %get-tuple-element.20.refs_0_), channel_id=1, source_target_pairs={{0,1},{1,0},{2,3},{3,2},{4,5},{5,4},{6,7},{7,6},{8,9},{9,8},{10,11... | collective-permute-start | bytes 2752520 | tf_op jit(solution)/shard_map/ppermute | solution.py:362
  20.0 4.1 %collective-permute-start.7 = (bf16[256,1792]{1,0:T(8,128)(2,1)S(1)}, bf16[256,1792]{1,0:T(8,128)(2,1)S(1)}, u32[]{:S(2)}, u32[]{:S(2)}) collective-permute-start(bf16[256,1792]{1,0:T(8,128)(2,1)S(1)} %get-tuple-element.21.refs_1_), channel_id=1, source_target_pairs={{0,1},{1,0},{2,3},{3,2},{4,5},{5,4},{6,7},{7,6},{8,9},{9,8},{10,11... | collective-permute-start | bytes 2752520 | tf_op jit(solution)/shard_map/ppermute | solution.py:362
  20.5 38.1 %collective-permute-start.8 = (bf16[768,1024]{1,0:T(8,128)(2,1)S(1)}, bf16[768,1024]{1,0:T(8,128)(2,1)S(1)}, u32[]{:S(2)}, u32[]{:S(2)}) collective-permute-start(bf16[768,1024]{1,0:T(8,128)(2,1)S(1)} %get-tuple-element.19.after_ref.up.xup), channel_id=1, source_target_pairs={{0,2},{1,3},{2,4},{3,5},{4,6},{5,7},{6,8},{7,9},{8,10},{9,11},{10,... | collective-permute-start | bytes 4718600 | tf_op jit(solution)/shard_map/ppermute | solution.py:362
  20.5 38.0 %collective-permute-start.9 = (bf16[768,1024]{1,0:T(8,128)(2,1)S(1)}, bf16[768,1024]{1,0:T(8,128)(2,1)S(1)}, u32[]{:S(2)}, u32[]{:S(2)}) collective-permute-start(bf16[768,1024]{1,0:T(8,128)(2,1)S(1)} %get-tuple-element.22.dn.xdn), channel_id=1, source_target_pairs={{0,254},{1,255},{2,0},{3,1},{4,2},{5,3},{6,4},{7,5},{8,6},{9,7},{1... | collective-permute-start | bytes 4718600 | tf_op jit(solution)/shard_map/ppermute | solution.py:362
  24.1 14.3 %collective-permute-start.10 = (bf16[128,1024]{1,0:T(8,128)(2,1)S(1)}, bf16[128,1024]{1,0:T(8,128)(2,1)S(1)}, u32[]{:S(2)}, u32[]{:S(2)}) collective-permute-start(bf16[128,1024]{1,0:T(8,128)(2,1)S(1)} %slab.1.after_ref.refs_0_), channel_id=1, source_target_pairs={{0,16},{1,17},{2,18},{3,19},{4,52},{5,53},{6,54},{7,55},{8,24},{9,... | collective-permute-start | bytes 786440 | tf_op jit(solution)/shard_map/ppermute | solution.py:362
  24.4 14.0 %collective-permute-start.12 = (bf16[128,1024]{1,0:T(8,128)(2,1)S(1)}, bf16[128,1024]{1,0:T(8,128)(2,1)S(1)}, u32[]{:S(2)}, u32[]{:S(2)}) collective-permute-start(bf16[128,1024]{1,0:T(8,128)(2,1)S(1)} %stack.3.refs_0_), channel_id=1, source_target_pairs={{0,64},{1,65},{2,66},{3,67},{4,68},{5,69},{6,198},{7,199},{8,72},{... | collective-permute-start | bytes 786440 | tf_op jit(solution)/shard_map/ppermute | solution.py:362
  38.4 7.9 %collective-permute-start.15 = (bf16[128,1024]{1,0:T(8,128)(2,1)S(1)}, bf16[128,1024]{1,0:T(8,128)(2,1)S(1)}, u32[]{:S(2)}, u32[]{:S(2)}) collective-permute-start(bf16[128,1024]{1,0:T(8,128)(2,1)S(1)} %tie.3.refs_4_), channel_id=1, source_target_pairs={{0,192},{1,193},{2,194},{3,195},{4,196},{5,197},{6,198},{7,199},{8... | collective-permute-start | bytes 786440 | tf_op jit(solution)/shard_map/ppermute | solution.py:362
  38.4 13.5 %collective-permute-start.13 = (bf16[128,1024]{1,0:T(8,128)(2,1)S(1)}, bf16[128,1024]{1,0:T(8,128)(2,1)S(1)}, u32[]{:S(2)}, u32[]{:S(2)}) collective-permute-start(bf16[128,1024]{1,0:T(8,128)(2,1)S(1)} %collective-permute-done.12.refs_1_), channel_id=1, source_target_pairs={{0,64},{1,65},{2,66},{3,67},{4,68},{5,69},{6,198},{7,199},{8,72},{... | collective-permute-start | bytes 786440 | tf_op jit(solution)/shard_map/ppermute | solution.py:362
  38.6 14.7 %collective-permute-start.11 = (bf16[128,1024]{1,0:T(8,128)(2,1)S(1)}, bf16[128,1024]{1,0:T(8,128)(2,1)S(1)}, u32[]{:S(2)}, u32[]{:S(2)}) collective-permute-start(bf16[128,1024]{1,0:T(8,128)(2,1)S(1)} %tie.3.refs_4_), channel_id=1, source_target_pairs={{0,16},{1,17},{2,18},{3,19},{4,52},{5,53},{6,54},{7,55},{8,24},{9,... | collective-permute-start | bytes 786440 | tf_op jit(solution)/shard_map/ppermute | solution.py:362
  46.3 11.2 %collective-permute-start.16 = (bf16[128,1024]{1,0:T(8,128)(2,1)S(1)}, bf16[128,1024]{1,0:T(8,128)(2,1)S(1)}, u32[]{:S(2)}, u32[]{:S(2)}) collective-permute-start(bf16[128,1024]{1,0:T(8,128)(2,1)S(1)} %collective-permute-done.15.refs_5_), channel_id=1, source_target_pairs={{0,192},{1,193},{2,194},{3,195},{4,196},{5,197},{6,198},{7,199},{8... | collective-permute-start | bytes 786440 | tf_op jit(solution)/shard_map/ppermute | solution.py:362
  51.9 11.2 %collective-permute-start.14 = (bf16[128,1024]{1,0:T(8,128)(2,1)S(1)}, bf16[128,1024]{1,0:T(8,128)(2,1)S(1)}, u32[]{:S(2)}, u32[]{:S(2)}) collective-permute-start(bf16[128,1024]{1,0:T(8,128)(2,1)S(1)} %collective-permute-done.13.refs_2_), channel_id=1, source_target_pairs={{0,64},{1,65},{2,66},{3,67},{4,68},{5,69},{6,198},{7,199},{8,72},{... | collective-permute-start | bytes 786440 | tf_op jit(solution)/shard_map/ppermute | solution.py:362
  67.2 54.1 %collective-permute-start.17 = (bf16[768,1024]{1,0:T(8,128)(2,1)S(1)}, bf16[768,1024]{1,0:T(8,128)(2,1)S(1)}, u32[]{:S(2)}, u32[]{:S(2)}) collective-permute-start(bf16[768,1024]{1,0:T(8,128)(2,1)S(1)} %get-tuple-element.23.up.after.refs_1_), channel_id=1, source_target_pairs={{0,2},{1,3},{2,4},{3,5},{4,6},{5,7},{6,8},{7,9},{8,10},{9,11},{10,... | collective-permute-start | bytes 4718600 | tf_op jit(solution)/shard_map/ppermute | solution.py:362
  67.3 54.0 %collective-permute-start.18 = (bf16[768,1024]{1,0:T(8,128)(2,1)S(1)}, bf16[768,1024]{1,0:T(8,128)(2,1)S(1)}, u32[]{:S(2)}, u32[]{:S(2)}) collective-permute-start(bf16[768,1024]{1,0:T(8,128)(2,1)S(1)} %get-tuple-element.24.dn), channel_id=1, source_target_pairs={{0,254},{1,255},{2,0},{3,1},{4,2},{5,3},{6,4},{7,5},{8,6},{9,7},{1... | collective-permute-start | bytes 4718600 | tf_op jit(solution)/shard_map/ppermute | solution.py:362
  70.8 12.3 %collective-permute-start.26 = (bf16[128,1024]{1,0:T(8,128)(2,1)S(1)}, bf16[128,1024]{1,0:T(8,128)(2,1)S(1)}, u32[]{:S(2)}, u32[]{:S(2)}) collective-permute-start(bf16[128,1024]{1,0:T(8,128)(2,1)S(1)} %tie.5.refs_8_), channel_id=1, source_target_pairs={{0,16},{1,17},{2,18},{3,19},{4,52},{5,53},{6,54},{7,55},{8,24},{9,... | collective-permute-start | bytes 786440 | tf_op jit(solution)/shard_map/ppermute | solution.py:362
  70.9 12.3 %collective-permute-start.22 = (bf16[128,1024]{1,0:T(8,128)(2,1)S(1)}, bf16[128,1024]{1,0:T(8,128)(2,1)S(1)}, u32[]{:S(2)}, u32[]{:S(2)}) collective-permute-start(bf16[128,1024]{1,0:T(8,128)(2,1)S(1)} %tie.5.refs_8_), channel_id=1, source_target_pairs={{0,64},{1,65},{2,66},{3,67},{4,68},{5,69},{6,198},{7,199},{8,72},{... | collective-permute-start | bytes 786440 | tf_op jit(solution)/shard_map/ppermute | solution.py:362
  83.1 6.7 %collective-permute-start.27 = (bf16[128,1024]{1,0:T(8,128)(2,1)S(1)}, bf16[128,1024]{1,0:T(8,128)(2,1)S(1)}, u32[]{:S(2)}, u32[]{:S(2)}) collective-permute-start(bf16[128,1024]{1,0:T(8,128)(2,1)S(1)} %collective-permute-done.26.refs_2_), channel_id=1, source_target_pairs={{0,192},{1,193},{2,194},{3,195},{4,196},{5,197},{6,198},{7,199},{8... | collective-permute-start | bytes 786440 | tf_op jit(solution)/shard_map/ppermute | solution.py:362
  83.1 12.1 %collective-permute-start.24 = (bf16[128,1024]{1,0:T(8,128)(2,1)S(1)}, bf16[128,1024]{1,0:T(8,128)(2,1)S(1)}, u32[]{:S(2)}, u32[]{:S(2)}) collective-permute-start(bf16[128,1024]{1,0:T(8,128)(2,1)S(1)} %collective-permute-done.22.refs_9_), channel_id=1, source_target_pairs={{0,64},{1,65},{2,66},{3,67},{4,68},{5,69},{6,198},{7,199},{8,72},{... | collective-permute-start | bytes 786440 | tf_op jit(solution)/shard_map/ppermute | solution.py:362
  89.8 11.0 %collective-permute-start.28 = (bf16[128,1024]{1,0:T(8,128)(2,1)S(1)}, bf16[128,1024]{1,0:T(8,128)(2,1)S(1)}, u32[]{:S(2)}, u32[]{:S(2)}) collective-permute-start(bf16[128,1024]{1,0:T(8,128)(2,1)S(1)} %collective-permute-done.27.refs_3_), channel_id=1, source_target_pairs={{0,192},{1,193},{2,194},{3,195},{4,196},{5,197},{6,198},{7,199},{8... | collective-permute-start | bytes 786440 | tf_op jit(solution)/shard_map/ppermute | solution.py:362
  89.8 16.6 %collective-permute-start.21 = (bf16[128,1024]{1,0:T(8,128)(2,1)S(1)}, bf16[128,1024]{1,0:T(8,128)(2,1)S(1)}, u32[]{:S(2)}, u32[]{:S(2)}) collective-permute-start(bf16[128,1024]{1,0:T(8,128)(2,1)S(1)} %tie.4.refs_6_), channel_id=1, source_target_pairs={{0,192},{1,193},{2,194},{3,195},{4,196},{5,197},{6,198},{7,199},{8... | collective-permute-start | bytes 786440 | tf_op jit(solution)/shard_map/ppermute | solution.py:362
  95.2 18.1 %collective-permute-start.25 = (bf16[128,1024]{1,0:T(8,128)(2,1)S(1)}, bf16[128,1024]{1,0:T(8,128)(2,1)S(1)}, u32[]{:S(2)}, u32[]{:S(2)}) collective-permute-start(bf16[128,1024]{1,0:T(8,128)(2,1)S(1)} %collective-permute-done.24.refs_0_), channel_id=1, source_target_pairs={{0,64},{1,65},{2,66},{3,67},{4,68},{5,69},{6,198},{7,199},{8,72},{... | collective-permute-start | bytes 786440 | tf_op jit(solution)/shard_map/ppermute | solution.py:362
  100.8 16.9 %collective-permute-start.29 = (bf16[128,1024]{1,0:T(8,128)(2,1)S(1)}, bf16[128,1024]{1,0:T(8,128)(2,1)S(1)}, u32[]{:S(2)}, u32[]{:S(2)}) collective-permute-start(bf16[128,1024]{1,0:T(8,128)(2,1)S(1)} %collective-permute-done.28.refs_4_), channel_id=1, source_target_pairs={{0,192},{1,193},{2,194},{3,195},{4,196},{5,197},{6,198},{7,199},{8... | collective-permute-start | bytes 786440 | tf_op jit(solution)/shard_map/ppermute | solution.py:362
  106.6 25.2 %collective-permute-start.23 = (bf16[1280,1024]{1,0:T(8,128)(2,1)S(1)}, bf16[1280,1024]{1,0:T(8,128)(2,1)S(1)}, u32[]{:S(2)}, u32[]{:S(2)}) collective-permute-start(bf16[1280,1024]{1,0:T(8,128)(2,1)S(1)} %stack.4.refs_4_), channel_id=1, source_target_pairs={{0,1},{1,0},{2,3},{3,2},{4,5},{5,4},{6,7},{7,6},{8,9},{9,8},{10,11... | collective-permute-start | bytes 7864328 | tf_op jit(solution)/shard_map/ppermute | solution.py:362
  117.8 14.1 %collective-permute-start.30 = (bf16[768,1024]{1,0:T(8,128)(2,1)S(1)}, bf16[768,1024]{1,0:T(8,128)(2,1)S(1)}, u32[]{:S(2)}, u32[]{:S(2)}) collective-permute-start(bf16[768,1024]{1,0:T(8,128)(2,1)S(1)} %stack.5.refs_5_), channel_id=1, source_target_pairs={{0,1},{1,0},{2,3},{3,2},{4,5},{5,4},{6,7},{7,6},{8,9},{9,8},{10,11... | collective-permute-start | bytes 4718600 | tf_op jit(solution)/shard_map/ppermute | solution.py:362
  123.7 3.1 %collective-permute-start.19 = (bf16[512,512]{1,0:T(8,128)(2,1)S(1)}, bf16[512,512]{1,0:T(8,128)(2,1)S(1)}, u32[]{:S(2)}, u32[]{:S(2)}) collective-permute-start(bf16[512,512]{1,0:T(8,128)(2,1)S(1)} %get-tuple-element.27), channel_id=1, source_target_pairs={{0,1},{1,0},{2,3},{3,2},{4,5},{5,4},{6,7},{7,6},{8,9},{9,8},{10,11... | collective-permute-start | bytes 1572872 | tf_op jit(solution)/shard_map/ppermute | solution.py:362
  126.2 2.1 %collective-permute-start.20 = (bf16[512,512]{1,0:T(8,128)(2,1)S(1)}, bf16[512,512]{1,0:T(8,128)(2,1)S(1)}, u32[]{:S(2)}, u32[]{:S(2)}) collective-permute-start(bf16[512,512]{1,0:T(8,128)(2,1)S(1)} %get-tuple-element.28), channel_id=1, source_target_pairs={{0,1},{1,0},{2,3},{3,2},{4,5},{5,4},{6,7},{7,6},{8,9},{9,8},{10,11... | collective-permute-start | bytes 1572872 | tf_op jit(solution)/shard_map/ppermute | solution.py:362

commit v3 on v2

--- a/solution.py
+++ b/solution.py
@@ -418,7 +418,7 @@
         got.append(move(other, swap))
     parts = [
         stack([chains[j][i] for j, i in EARLY]),
-        stack([chains[j][i] for j, i in LATE]),
+        stack([chains[j][i] for j, i in LATE], own[-1]),
     ]
     out = rotate(own, got, parts, CHUNKS)
     return rotate(own, got, [move(part, swap) for part in parts], CHUNKS, out)

time: 136 us -> 133 us (0.978)
  waiting for transfers between devices: 82.8 us -> 80.4 us
    ppermute x31, waiting for transfers between devices: 82.8 us -> 80.4 us  [move(): return lax.ppermute(array, 'rows', route)]
  transfers between devices with their start and end apart: 31 -> 31, of which waited for: 17 -> 18; matrix products, arithmetic and copies ran while one was open for 0% -> 0% of each run, Pallas kernels for 7% -> 7%
where the time goes in v3:
time: 133 us
  waiting for transfers between devices  80.4 us (60%)
  starting transfers between devices  29.5 us (22%)
  Pallas kernels  19.2 us (14%)
  local copies, waits for them, and re-layouts  2.34 us (2%)
  between operations  1.67 us (1%)
    ppermute x31, waiting for transfers between devices, move(): return lax.ppermute(array, 'rows', route)  80.4 us
    ppermute x31, starting transfers between devices, move(): return lax.ppermute(array, 'rows', route)  29.5 us
    pallas_call x18, Pallas kernels, call(): pl.pallas_call(kernel, out_shape=shapes, in_specs=ins, out_specs=[spec fo...  19.2 us
  transfers between devices with their start and end apart: 31, of which 18 were waited for; matrix products, arithmetic and copies ran while one was open for 0% of the time, Pallas kernels for 7%

profile of v3, /device:TPU:225, one launch (start us, length us, event | category | flops | bytes accessed | tf_op | source)
XLA Modules:
  0.0 133.1 jit_solution(9327812244304245471)
XLA Ops:
  0.0 1.6 %copy-done = bf16[512,2048]{1,0:T(8,128)(2,1)S(1)} copy-done((bf16[512,2048]{1,0:T(8,128)(2,1)S(1)}, bf16[512,2048]{1,0:T(8,128)(2,1)}, u32[]{:S(2)}) %copy-start) | copy-done | bytes 2097176
  1.6 0.2 split.1
  1.8 0.8 collective-permute-start.5
  2.6 0.7 collective-permute-start
  3.3 2.0 %collective-permute-done.got_ref = bf16[8,2048]{1,0:T(8,128)(2,1)S(1)} collective-permute-done((bf16[8,2048]{1,0:T(8,128)(2,1)S(1)}, bf16[8,2048]{1,0:T(8,128)(2,1)S(1)}, u32[]{:S(2)}, u32[]{:S(2)}) %collective-permute-start) | collective-permute-done | bytes 32800 | tf_op jit(solution)/shard_map/ppermute | solution.py:362
  5.4 1.4 %collective-permute-start.1 = (bf16[16,2048]{1,0:T(8,128)(2,1)S(1)}, bf16[16,2048]{1,0:T(8,128)(2,1)S(1)}, u32[]{:S(2)}, u32[]{:S(2)}) collective-permute-start(bf16[16,2048]{1,0:T(8,128)(2,1)S(1)} %join.1.refs_0_), channel_id=1, source_target_pairs={{6,0},{7,1},{0,2},{1,3},{2,4},{3,5},{4,6},{5,7},{14,8},{15,9},{8,1... | collective-permute-start | bytes 196616 | tf_op jit(solution)/shard_map/ppermute | solution.py:362
  6.7 2.6 %collective-permute-start.2 = (bf16[16,2048]{1,0:T(8,128)(2,1)S(1)}, bf16[16,2048]{1,0:T(8,128)(2,1)S(1)}, u32[]{:S(2)}, u32[]{:S(2)}) collective-permute-start(bf16[16,2048]{1,0:T(8,128)(2,1)S(1)} %join.1.refs_0_), channel_id=1, source_target_pairs={{4,0},{5,1},{6,2},{7,3},{0,4},{1,5},{2,6},{3,7},{12,8},{13,9},{14,... | collective-permute-start | bytes 196616 | tf_op jit(solution)/shard_map/ppermute | solution.py:362
  9.4 1.1 collective-permute-start.3
  10.4 1.3 %collective-permute-done.2.refs_2_ = bf16[16,2048]{1,0:T(8,128)(2,1)S(1)} collective-permute-done((bf16[16,2048]{1,0:T(8,128)(2,1)S(1)}, bf16[16,2048]{1,0:T(8,128)(2,1)S(1)}, u32[]{:S(2)}, u32[]{:S(2)}) %collective-permute-start.2) | collective-permute-done | bytes 65568 | tf_op jit(solution)/shard_map/ppermute | solution.py:362
  11.8 1.5 %collective-permute-done.3.refs_3_ = bf16[16,2048]{1,0:T(8,128)(2,1)S(1)} collective-permute-done((bf16[16,2048]{1,0:T(8,128)(2,1)S(1)}, bf16[16,2048]{1,0:T(8,128)(2,1)S(1)}, u32[]{:S(2)}, u32[]{:S(2)}) %collective-permute-start.3) | collective-permute-done | bytes 65568 | tf_op jit(solution)/shard_map/ppermute | solution.py:362
  13.3 2.6 %collective-permute-start.4 = (bf16[64,1024]{1,0:T(8,128)(2,1)S(1)}, bf16[64,1024]{1,0:T(8,128)(2,1)S(1)}, u32[]{:S(2)}, u32[]{:S(2)}) collective-permute-start(bf16[64,1024]{1,0:T(8,128)(2,1)S(1)} %get-tuple-element.18), channel_id=1, source_target_pairs={{0,1},{1,0},{2,3},{3,2},{4,5},{5,4},{6,7},{7,6},{8,9},{9,8},{10,11... | collective-permute-start | bytes 393224 | tf_op jit(solution)/shard_map/ppermute | solution.py:362
  16.0 0.4 assemble.1
  16.4 0.6 collective-permute-done.4.got_ref
  17.0 0.7 copy-done.2
  17.7 2.1 %build_bands.1 = (bf16[256,1792]{1,0:T(8,128)(2,1)S(1)}, bf16[256,1792]{1,0:T(8,128)(2,1)S(1)}) custom-call(s32[4,12]{1,0:T(4,128)S(1)} %copy-done.5, s32[4,4,256]{2,1,0:T(4,128)S(1)} %bitcast.1, bf16[4,12,128,128]{3,2,1,0:T(8,128)(2,1)S(1)} %copy-done.2, bf16[128,1024]{1,0:T(8,128)(2,1)S(1)} %slab.1.after_ref.refs_0_), custom_call_target="tpu_custom_call" | custom-call | tf_op jit(solution)/shard_map/build_bands/pallas_call | solution.py:25
  19.9 0.1 collective-permute-start.6
  20.0 0.5 collective-permute-start.7
  20.5 3.5 %collective-permute-start.9 = (bf16[768,1024]{1,0:T(8,128)(2,1)S(1)}, bf16[768,1024]{1,0:T(8,128)(2,1)S(1)}, u32[]{:S(2)}, u32[]{:S(2)}) collective-permute-start(bf16[768,1024]{1,0:T(8,128)(2,1)S(1)} %get-tuple-element.22.dn.xdn), channel_id=1, source_target_pairs={{0,254},{1,255},{2,0},{3,1},{4,2},{5,3},{6,4},{7,5},{8,6},{9,7},{1... | collective-permute-start | bytes 4718600 | tf_op jit(solution)/shard_map/ppermute | solution.py:362
  24.1 0.2 merge_bands.1.refs_1_.bands
  24.4 1.3 collective-permute-start.12
  25.7 12.7 %collective-permute-done.10.refs_0_ = bf16[128,1024]{1,0:T(8,128)(2,1)S(1)} collective-permute-done((bf16[128,1024]{1,0:T(8,128)(2,1)S(1)}, bf16[128,1024]{1,0:T(8,128)(2,1)S(1)}, u32[]{:S(2)}, u32[]{:S(2)}) %collective-permute-start.10) | collective-permute-done | bytes 262176 | tf_op jit(solution)/shard_map/ppermute | solution.py:362
  38.4 0.2 collective-permute-start.13
  38.6 0.2 collective-permute-start.11
  38.8 7.6 %collective-permute-done.15.refs_5_ = bf16[128,1024]{1,0:T(8,128)(2,1)S(1)} collective-permute-done((bf16[128,1024]{1,0:T(8,128)(2,1)S(1)}, bf16[128,1024]{1,0:T(8,128)(2,1)S(1)}, u32[]{:S(2)}, u32[]{:S(2)}) %collective-permute-start.15) | collective-permute-done | bytes 262176 | tf_op jit(solution)/shard_map/ppermute | solution.py:362
  46.3 5.6 %collective-permute-done.13.refs_2_ = bf16[128,1024]{1,0:T(8,128)(2,1)S(1)} collective-permute-done((bf16[128,1024]{1,0:T(8,128)(2,1)S(1)}, bf16[128,1024]{1,0:T(8,128)(2,1)S(1)}, u32[]{:S(2)}, u32[]{:S(2)}) %collective-permute-start.13) | collective-permute-done | bytes 262176 | tf_op jit(solution)/shard_map/ppermute | solution.py:362
  53.3 4.3 %collective-permute-done.16.rest_2_.refs_0_ = bf16[128,1024]{1,0:T(8,128)(2,1)S(1)} collective-permute-done((bf16[128,1024]{1,0:T(8,128)(2,1)S(1)}, bf16[128,1024]{1,0:T(8,128)(2,1)S(1)}, u32[]{:S(2)}, u32[]{:S(2)}) %collective-permute-start.16) | collective-permute-done | bytes 262176 | tf_op jit(solution)/shard_map/ppermute | solution.py:362
  57.6 1.0 collective-permute-done.8.left
  58.6 4.6 %collective-permute-done.14.rest_1_.refs_3_ = bf16[128,1024]{1,0:T(8,128)(2,1)S(1)} collective-permute-done((bf16[128,1024]{1,0:T(8,128)(2,1)S(1)}, bf16[128,1024]{1,0:T(8,128)(2,1)S(1)}, u32[]{:S(2)}, u32[]{:S(2)}) %collective-permute-start.14) | collective-permute-done | bytes 262176 | tf_op jit(solution)/shard_map/ppermute | solution.py:362
  63.2 4.0 %first_pass.1 = (bf16[768,1024]{1,0:T(8,128)(2,1)S(1)}, bf16[768,1024]{1,0:T(8,128)(2,1)S(1)}) custom-call(f32[1]{0:T(128)S(6)} %copy.16.center, f32[1]{0:T(128)S(6)} %copy.17.half, bf16[4,256,1792]{2,1,0:T(8,128)(2,1)S(1)} %merge_bands.1.refs_1_.bands, bf16[768,1024]{1,0:T(8,128)(2,1)S(1)} %collective-permute-done.8.left, ...), custom_call_target="tpu_custom_call" | custom-call | flops 1879048192 | tf_op jit(solution)/shard_map/first_pass/pallas_call | solution.py:25
  67.3 3.6 %collective-permute-start.18 = (bf16[768,1024]{1,0:T(8,128)(2,1)S(1)}, bf16[768,1024]{1,0:T(8,128)(2,1)S(1)}, u32[]{:S(2)}, u32[]{:S(2)}) collective-permute-start(bf16[768,1024]{1,0:T(8,128)(2,1)S(1)} %get-tuple-element.24.dn), channel_id=1, source_target_pairs={{0,254},{1,255},{2,0},{3,1},{4,2},{5,3},{6,4},{7,5},{8,6},{9,7},{1... | collective-permute-start | bytes 4718600 | tf_op jit(solution)/shard_map/ppermute | solution.py:362
  70.9 12.3 %collective-permute-done.26.refs_2_ = bf16[128,1024]{1,0:T(8,128)(2,1)S(1)} collective-permute-done((bf16[128,1024]{1,0:T(8,128)(2,1)S(1)}, bf16[128,1024]{1,0:T(8,128)(2,1)S(1)}, u32[]{:S(2)}, u32[]{:S(2)}) %collective-permute-start.26) | collective-permute-done | bytes 262176 | tf_op jit(solution)/shard_map/ppermute | solution.py:362
  83.2 6.6 %collective-permute-done.27.refs_3_ = bf16[128,1024]{1,0:T(8,128)(2,1)S(1)} collective-permute-done((bf16[128,1024]{1,0:T(8,128)(2,1)S(1)}, bf16[128,1024]{1,0:T(8,128)(2,1)S(1)}, u32[]{:S(2)}, u32[]{:S(2)}) %collective-permute-start.27) | collective-permute-done | bytes 262176 | tf_op jit(solution)/shard_map/ppermute | solution.py:362
  89.8 5.3 %collective-permute-done.21.refs_7_ = bf16[128,1024]{1,0:T(8,128)(2,1)S(1)} collective-permute-done((bf16[128,1024]{1,0:T(8,128)(2,1)S(1)}, bf16[128,1024]{1,0:T(8,128)(2,1)S(1)}, u32[]{:S(2)}, u32[]{:S(2)}) %collective-permute-start.21) | collective-permute-done | bytes 262176 | tf_op jit(solution)/shard_map/ppermute | solution.py:362
  95.2 0.2 stack.4.refs_4_
  95.4 6.7 %collective-permute-start.23 = (bf16[1280,1024]{1,0:T(8,128)(2,1)S(1)}, bf16[1280,1024]{1,0:T(8,128)(2,1)S(1)}, u32[]{:S(2)}, u32[]{:S(2)}) collective-permute-start(bf16[1280,1024]{1,0:T(8,128)(2,1)S(1)} %stack.4.refs_4_), channel_id=1, source_target_pairs={{0,1},{1,0},{2,3},{3,2},{4,5},{5,4},{6,7},{7,6},{8,9},{9,8},{10,11... | collective-permute-start | bytes 7864328 | tf_op jit(solution)/shard_map/ppermute | solution.py:362
  102.0 4.4 %collective-permute-done.28.refs_4_ = bf16[128,1024]{1,0:T(8,128)(2,1)S(1)} collective-permute-done((bf16[128,1024]{1,0:T(8,128)(2,1)S(1)}, bf16[128,1024]{1,0:T(8,128)(2,1)S(1)}, u32[]{:S(2)}, u32[]{:S(2)}) %collective-permute-start.28) | collective-permute-done | bytes 262176 | tf_op jit(solution)/shard_map/ppermute | solution.py:362
  106.4 2.4 %second_pass.2 = (bf16[512,512]{1,0:T(8,128)(2,1)S(1)}, bf16[512,512]{1,0:T(8,128)(2,1)S(1)}) custom-call(f32[1]{0:T(128)S(6)} %copy.16.center, f32[1]{0:T(128)S(6)} %copy.17.half, bf16[4,256,1792]{2,1,0:T(8,128)(2,1)S(1)} %merge_bands.1.refs_1_.bands, bf16[768,1024]{1,0:T(8,128)(2,1)S(1)} %collective-permute-done.17.left, ...), custom_call_target="tpu_custom_call" | custom-call | flops 18790481920 | tf_op jit(solution)/shard_map/second_pass/pallas_call | solution.py:25
  108.8 2.4 %second_pass.3 = (bf16[512,512]{1,0:T(8,128)(2,1)S(1)}, bf16[512,512]{1,0:T(8,128)(2,1)S(1)}) custom-call(f32[1]{0:T(128)S(6)} %copy.16.center, f32[1]{0:T(128)S(6)} %copy.17.half, bf16[4,256,1792]{2,1,0:T(8,128)(2,1)S(1)} %merge_bands.1.refs_1_.bands, bf16[768,1024]{1,0:T(8,128)(2,1)S(1)} %collective-permute-done.17.left, ...), custom_call_target="tpu_custom_call" | custom-call | flops 18790481920 | tf_op jit(solution)/shard_map/second_pass/pallas_call | solution.py:25
  111.2 0.8 collective-permute-done.25.refs_1_
  112.0 5.6 %collective-permute-done.29.refs_5_ = bf16[128,1024]{1,0:T(8,128)(2,1)S(1)} collective-permute-done((bf16[128,1024]{1,0:T(8,128)(2,1)S(1)}, bf16[128,1024]{1,0:T(8,128)(2,1)S(1)}, u32[]{:S(2)}, u32[]{:S(2)}) %collective-permute-start.29) | collective-permute-done | bytes 262176 | tf_op jit(solution)/shard_map/ppermute | solution.py:362
  117.6 0.1 stack.5.refs_5_
  117.8 3.6 %collective-permute-start.30 = (bf16[768,1024]{1,0:T(8,128)(2,1)S(1)}, bf16[768,1024]{1,0:T(8,128)(2,1)S(1)}, u32[]{:S(2)}, u32[]{:S(2)}) collective-permute-start(bf16[768,1024]{1,0:T(8,128)(2,1)S(1)} %stack.5.refs_5_), channel_id=1, source_target_pairs={{0,1},{1,0},{2,3},{3,2},{4,5},{5,4},{6,7},{7,6},{8,9},{9,8},{10,11... | collective-permute-start | bytes 4718600 | tf_op jit(solution)/shard_map/ppermute | solution.py:362
  121.3 0.1 collective-permute-start.19
  121.4 0.4 collective-permute-start.20
  121.8 3.3 %collective-permute-done.19.refs_2_ = bf16[512,512]{1,0:T(8,128)(2,1)S(1)} collective-permute-done((bf16[512,512]{1,0:T(8,128)(2,1)S(1)}, bf16[512,512]{1,0:T(8,128)(2,1)S(1)}, u32[]{:S(2)}, u32[]{:S(2)}) %collective-permute-start.19) | collective-permute-done | bytes 524320 | tf_op jit(solution)/shard_map/ppermute | solution.py:362
  125.1 0.7 collective-permute-done.20.refs_3_
  125.9 3.5 %rotate.2.refs_6_ = bf16[512,2048]{1,0:T(8,128)(2,1)} custom-call(bf16[512,512]{1,0:T(8,128)(2,1)S(1)} %get-tuple-element.25.after.refs_0_, bf16[512,512]{1,0:T(8,128)(2,1)S(1)} %get-tuple-element.26.refs_6_.refs_1_, bf16[512,512]{1,0:T(8,128)(2,1)S(1)} %collective-permute-done.19.refs_2_, bf16[512,512]{1,0:T(8,128)(2,1)S(1)} %collective-permute-done.20.refs_3_, ...), custom_call_target="tpu_custom_call" | custom-call | tf_op jit(solution)/shard_map/rotate/pallas_call | solution.py:25
  129.4 3.5 %rotate.3 = bf16[512,2048]{1,0:T(8,128)(2,1)} custom-call(bf16[512,512]{1,0:T(8,128)(2,1)S(1)} %get-tuple-element.25.after.refs_0_, bf16[512,512]{1,0:T(8,128)(2,1)S(1)} %get-tuple-element.26.refs_6_.refs_1_, bf16[512,512]{1,0:T(8,128)(2,1)S(1)} %collective-permute-done.19.refs_2_, ...), custom_call_target="tpu_custom_call", output_to_operand_aliasing={{}: (6, {})} | custom-call | tf_op jit(solution)/shard_map/rotate/pallas_call | solution.py:25
  (44 shorter events, 0.5 us)
Async XLA Ops:
  0.0 1.6 %copy-start = (bf16[512,2048]{1,0:T(8,128)(2,1)S(1)}, bf16[512,2048]{1,0:T(8,128)(2,1)}, u32[]{:S(2)}) copy-start(bf16[512,2048]{1,0:T(8,128)(2,1)} %x_ref.3) | copy-start | bytes 6291460
  1.6 1.0 copy-start.3
  1.6 14.4 %copy-start.1 = (bf16[512,2048]{1,0:T(8,128)(2,1)S(1)}, bf16[512,2048]{1,0:T(8,128)(2,1)}, u32[]{:S(2)}) copy-start(bf16[512,2048]{1,0:T(8,128)(2,1)} %x_ref.3) | copy-start | bytes 6291460
  1.8 14.1 %collective-permute-start.5 = (bf16[512,1024]{1,0:T(8,128)(2,1)S(1)}, bf16[512,1024]{1,0:T(8,128)(2,1)S(1)}, u32[]{:S(2)}, u32[]{:S(2)}) collective-permute-start(bf16[512,1024]{1,0:T(8,128)(2,1)S(1)} %split.1), channel_id=1, source_target_pairs={{0,1},{1,0},{2,3},{3,2},{4,5},{5,4},{6,7},{7,6},{8,9},{9,8},{10,11... | collective-permute-start | bytes 3145736 | tf_op jit(solution)/shard_map/ppermute | solution.py:362
  2.6 2.8 %collective-permute-start = (bf16[8,2048]{1,0:T(8,128)(2,1)S(1)}, bf16[8,2048]{1,0:T(8,128)(2,1)S(1)}, u32[]{:S(2)}, u32[]{:S(2)}) collective-permute-start(bf16[8,2048]{1,0:T(8,128)(2,1)S(1)} %copy-done.3), channel_id=1, source_target_pairs={{0,8},{1,9},{2,10},{3,11},{4,12},{5,13},{6,14},{7,15},{8,0},{9,1},... | collective-permute-start | bytes 98312 | tf_op jit(solution)/shard_map/ppermute | solution.py:362
  5.4 5.1 %collective-permute-start.1 = (bf16[16,2048]{1,0:T(8,128)(2,1)S(1)}, bf16[16,2048]{1,0:T(8,128)(2,1)S(1)}, u32[]{:S(2)}, u32[]{:S(2)}) collective-permute-start(bf16[16,2048]{1,0:T(8,128)(2,1)S(1)} %join.1.refs_0_), channel_id=1, source_target_pairs={{6,0},{7,1},{0,2},{1,3},{2,4},{3,5},{4,6},{5,7},{14,8},{15,9},{8,1... | collective-permute-start | bytes 196616 | tf_op jit(solution)/shard_map/ppermute | solution.py:362
  6.7 5.0 %collective-permute-start.2 = (bf16[16,2048]{1,0:T(8,128)(2,1)S(1)}, bf16[16,2048]{1,0:T(8,128)(2,1)S(1)}, u32[]{:S(2)}, u32[]{:S(2)}) collective-permute-start(bf16[16,2048]{1,0:T(8,128)(2,1)S(1)} %join.1.refs_0_), channel_id=1, source_target_pairs={{4,0},{5,1},{6,2},{7,3},{0,4},{1,5},{2,6},{3,7},{12,8},{13,9},{14,... | collective-permute-start | bytes 196616 | tf_op jit(solution)/shard_map/ppermute | solution.py:362
  9.4 3.9 %collective-permute-start.3 = (bf16[16,2048]{1,0:T(8,128)(2,1)S(1)}, bf16[16,2048]{1,0:T(8,128)(2,1)S(1)}, u32[]{:S(2)}, u32[]{:S(2)}) collective-permute-start(bf16[16,2048]{1,0:T(8,128)(2,1)S(1)} %join.1.refs_0_), channel_id=1, source_target_pairs={{2,0},{3,1},{4,2},{5,3},{6,4},{7,5},{0,6},{1,7},{10,8},{11,9},{12,... | collective-permute-start | bytes 196616 | tf_op jit(solution)/shard_map/ppermute | solution.py:362
  13.3 3.6 %collective-permute-start.4 = (bf16[64,1024]{1,0:T(8,128)(2,1)S(1)}, bf16[64,1024]{1,0:T(8,128)(2,1)S(1)}, u32[]{:S(2)}, u32[]{:S(2)}) collective-permute-start(bf16[64,1024]{1,0:T(8,128)(2,1)S(1)} %get-tuple-element.18), channel_id=1, source_target_pairs={{0,1},{1,0},{2,3},{3,2},{4,5},{5,4},{6,7},{7,6},{8,9},{9,8},{10,11... | collective-permute-start | bytes 393224 | tf_op jit(solution)/shard_map/ppermute | solution.py:362
  16.3 1.4 %copy-start.2 = (bf16[4,12,128,128]{3,2,1,0:T(8,128)(2,1)S(1)}, bf16[4,12,128,128]{3,2,1,0:T(8,128)(2,1)}, u32[]{:S(2)}) copy-start(bf16[4,12,128,128]{3,2,1,0:T(8,128)(2,1)} %h_ref.1) | copy-start | bytes 4718596
  16.3 1.4 %copy-start.4 = (s32[256,4,4]{0,2,1:T(4,128)S(1)}, s32[256,4,4]{0,2,1:T(4,128)}, u32[]{:S(2)}) copy-start(s32[256,4,4]{0,2,1:T(4,128)} %param.10) | copy-start | bytes 49156
  16.4 1.4 %copy-start.5 = (s32[4,12]{1,0:T(4,128)S(1)}, s32[4,12]{1,0:T(4,128)}, u32[]{:S(2)}) copy-start(s32[4,12]{1,0:T(4,128)} %col_ref.1) | copy-start | bytes 580
  19.9 4.2 %collective-permute-start.6 = (bf16[256,1792]{1,0:T(8,128)(2,1)S(1)}, bf16[256,1792]{1,0:T(8,128)(2,1)S(1)}, u32[]{:S(2)}, u32[]{:S(2)}) collective-permute-start(bf16[256,1792]{1,0:T(8,128)(2,1)S(1)} %get-tuple-element.20.refs_0_), channel_id=1, source_target_pairs={{0,1},{1,0},{2,3},{3,2},{4,5},{5,4},{6,7},{7,6},{8,9},{9,8},{10,11... | collective-permute-start | bytes 2752520 | tf_op jit(solution)/shard_map/ppermute | solution.py:362
  20.0 4.1 %collective-permute-start.7 = (bf16[256,1792]{1,0:T(8,128)(2,1)S(1)}, bf16[256,1792]{1,0:T(8,128)(2,1)S(1)}, u32[]{:S(2)}, u32[]{:S(2)}) collective-permute-start(bf16[256,1792]{1,0:T(8,128)(2,1)S(1)} %get-tuple-element.21.refs_1_), channel_id=1, source_target_pairs={{0,1},{1,0},{2,3},{3,2},{4,5},{5,4},{6,7},{7,6},{8,9},{9,8},{10,11... | collective-permute-start | bytes 2752520 | tf_op jit(solution)/shard_map/ppermute | solution.py:362
  20.5 38.1 %collective-permute-start.8 = (bf16[768,1024]{1,0:T(8,128)(2,1)S(1)}, bf16[768,1024]{1,0:T(8,128)(2,1)S(1)}, u32[]{:S(2)}, u32[]{:S(2)}) collective-permute-start(bf16[768,1024]{1,0:T(8,128)(2,1)S(1)} %get-tuple-element.19.after_ref.up.xup), channel_id=1, source_target_pairs={{0,2},{1,3},{2,4},{3,5},{4,6},{5,7},{6,8},{7,9},{8,10},{9,11},{10,... | collective-permute-start | bytes 4718600 | tf_op jit(solution)/shard_map/ppermute | solution.py:362
  20.5 38.0 %collective-permute-start.9 = (bf16[768,1024]{1,0:T(8,128)(2,1)S(1)}, bf16[768,1024]{1,0:T(8,128)(2,1)S(1)}, u32[]{:S(2)}, u32[]{:S(2)}) collective-permute-start(bf16[768,1024]{1,0:T(8,128)(2,1)S(1)} %get-tuple-element.22.dn.xdn), channel_id=1, source_target_pairs={{0,254},{1,255},{2,0},{3,1},{4,2},{5,3},{6,4},{7,5},{8,6},{9,7},{1... | collective-permute-start | bytes 4718600 | tf_op jit(solution)/shard_map/ppermute | solution.py:362
  24.1 14.3 %collective-permute-start.10 = (bf16[128,1024]{1,0:T(8,128)(2,1)S(1)}, bf16[128,1024]{1,0:T(8,128)(2,1)S(1)}, u32[]{:S(2)}, u32[]{:S(2)}) collective-permute-start(bf16[128,1024]{1,0:T(8,128)(2,1)S(1)} %slab.1.after_ref.refs_0_), channel_id=1, source_target_pairs={{0,16},{1,17},{2,18},{3,19},{4,52},{5,53},{6,54},{7,55},{8,24},{9,... | collective-permute-start | bytes 786440 | tf_op jit(solution)/shard_map/ppermute | solution.py:362
  24.4 14.0 %collective-permute-start.12 = (bf16[128,1024]{1,0:T(8,128)(2,1)S(1)}, bf16[128,1024]{1,0:T(8,128)(2,1)S(1)}, u32[]{:S(2)}, u32[]{:S(2)}) collective-permute-start(bf16[128,1024]{1,0:T(8,128)(2,1)S(1)} %stack.3.refs_0_), channel_id=1, source_target_pairs={{0,64},{1,65},{2,66},{3,67},{4,68},{5,69},{6,198},{7,199},{8,72},{... | collective-permute-start | bytes 786440 | tf_op jit(solution)/shard_map/ppermute | solution.py:362
  38.4 7.9 %collective-permute-start.15 = (bf16[128,1024]{1,0:T(8,128)(2,1)S(1)}, bf16[128,1024]{1,0:T(8,128)(2,1)S(1)}, u32[]{:S(2)}, u32[]{:S(2)}) collective-permute-start(bf16[128,1024]{1,0:T(8,128)(2,1)S(1)} %tie.3.refs_4_), channel_id=1, source_target_pairs={{0,192},{1,193},{2,194},{3,195},{4,196},{5,197},{6,198},{7,199},{8... | collective-permute-start | bytes 786440 | tf_op jit(solution)/shard_map/ppermute | solution.py:362
  38.4 13.5 %collective-permute-start.13 = (bf16[128,1024]{1,0:T(8,128)(2,1)S(1)}, bf16[128,1024]{1,0:T(8,128)(2,1)S(1)}, u32[]{:S(2)}, u32[]{:S(2)}) collective-permute-start(bf16[128,1024]{1,0:T(8,128)(2,1)S(1)} %collective-permute-done.12.refs_1_), channel_id=1, source_target_pairs={{0,64},{1,65},{2,66},{3,67},{4,68},{5,69},{6,198},{7,199},{8,72},{... | collective-permute-start | bytes 786440 | tf_op jit(solution)/shard_map/ppermute | solution.py:362
  38.6 14.7 %collective-permute-start.11 = (bf16[128,1024]{1,0:T(8,128)(2,1)S(1)}, bf16[128,1024]{1,0:T(8,128)(2,1)S(1)}, u32[]{:S(2)}, u32[]{:S(2)}) collective-permute-start(bf16[128,1024]{1,0:T(8,128)(2,1)S(1)} %tie.3.refs_4_), channel_id=1, source_target_pairs={{0,16},{1,17},{2,18},{3,19},{4,52},{5,53},{6,54},{7,55},{8,24},{9,... | collective-permute-start | bytes 786440 | tf_op jit(solution)/shard_map/ppermute | solution.py:362
  46.3 11.2 %collective-permute-start.16 = (bf16[128,1024]{1,0:T(8,128)(2,1)S(1)}, bf16[128,1024]{1,0:T(8,128)(2,1)S(1)}, u32[]{:S(2)}, u32[]{:S(2)}) collective-permute-start(bf16[128,1024]{1,0:T(8,128)(2,1)S(1)} %collective-permute-done.15.refs_5_), channel_id=1, source_target_pairs={{0,192},{1,193},{2,194},{3,195},{4,196},{5,197},{6,198},{7,199},{8... | collective-permute-start | bytes 786440 | tf_op jit(solution)/shard_map/ppermute | solution.py:362
  51.9 11.2 %collective-permute-start.14 = (bf16[128,1024]{1,0:T(8,128)(2,1)S(1)}, bf16[128,1024]{1,0:T(8,128)(2,1)S(1)}, u32[]{:S(2)}, u32[]{:S(2)}) collective-permute-start(bf16[128,1024]{1,0:T(8,128)(2,1)S(1)} %collective-permute-done.13.refs_2_), channel_id=1, source_target_pairs={{0,64},{1,65},{2,66},{3,67},{4,68},{5,69},{6,198},{7,199},{8,72},{... | collective-permute-start | bytes 786440 | tf_op jit(solution)/shard_map/ppermute | solution.py:362
  67.2 39.2 %collective-permute-start.17 = (bf16[768,1024]{1,0:T(8,128)(2,1)S(1)}, bf16[768,1024]{1,0:T(8,128)(2,1)S(1)}, u32[]{:S(2)}, u32[]{:S(2)}) collective-permute-start(bf16[768,1024]{1,0:T(8,128)(2,1)S(1)} %get-tuple-element.23.up.after.refs_1_), channel_id=1, source_target_pairs={{0,2},{1,3},{2,4},{3,5},{4,6},{5,7},{6,8},{7,9},{8,10},{9,11},{10,... | collective-permute-start | bytes 4718600 | tf_op jit(solution)/shard_map/ppermute | solution.py:362
  67.3 39.1 %collective-permute-start.18 = (bf16[768,1024]{1,0:T(8,128)(2,1)S(1)}, bf16[768,1024]{1,0:T(8,128)(2,1)S(1)}, u32[]{:S(2)}, u32[]{:S(2)}) collective-permute-start(bf16[768,1024]{1,0:T(8,128)(2,1)S(1)} %get-tuple-element.24.dn), channel_id=1, source_target_pairs={{0,254},{1,255},{2,0},{3,1},{4,2},{5,3},{6,4},{7,5},{8,6},{9,7},{1... | collective-permute-start | bytes 4718600 | tf_op jit(solution)/shard_map/ppermute | solution.py:362
  70.8 12.3 %collective-permute-start.26 = (bf16[128,1024]{1,0:T(8,128)(2,1)S(1)}, bf16[128,1024]{1,0:T(8,128)(2,1)S(1)}, u32[]{:S(2)}, u32[]{:S(2)}) collective-permute-start(bf16[128,1024]{1,0:T(8,128)(2,1)S(1)} %tie.5.refs_8_), channel_id=1, source_target_pairs={{0,16},{1,17},{2,18},{3,19},{4,52},{5,53},{6,54},{7,55},{8,24},{9,... | collective-permute-start | bytes 786440 | tf_op jit(solution)/shard_map/ppermute | solution.py:362
  70.9 12.3 %collective-permute-start.22 = (bf16[128,1024]{1,0:T(8,128)(2,1)S(1)}, bf16[128,1024]{1,0:T(8,128)(2,1)S(1)}, u32[]{:S(2)}, u32[]{:S(2)}) collective-permute-start(bf16[128,1024]{1,0:T(8,128)(2,1)S(1)} %tie.5.refs_8_), channel_id=1, source_target_pairs={{0,64},{1,65},{2,66},{3,67},{4,68},{5,69},{6,198},{7,199},{8,72},{... | collective-permute-start | bytes 786440 | tf_op jit(solution)/shard_map/ppermute | solution.py:362
  83.1 6.7 %collective-permute-start.27 = (bf16[128,1024]{1,0:T(8,128)(2,1)S(1)}, bf16[128,1024]{1,0:T(8,128)(2,1)S(1)}, u32[]{:S(2)}, u32[]{:S(2)}) collective-permute-start(bf16[128,1024]{1,0:T(8,128)(2,1)S(1)} %collective-permute-done.26.refs_2_), channel_id=1, source_target_pairs={{0,192},{1,193},{2,194},{3,195},{4,196},{5,197},{6,198},{7,199},{8... | collective-permute-start | bytes 786440 | tf_op jit(solution)/shard_map/ppermute | solution.py:362
  83.1 12.1 %collective-permute-start.21 = (bf16[128,1024]{1,0:T(8,128)(2,1)S(1)}, bf16[128,1024]{1,0:T(8,128)(2,1)S(1)}, u32[]{:S(2)}, u32[]{:S(2)}) collective-permute-start(bf16[128,1024]{1,0:T(8,128)(2,1)S(1)} %tie.4.refs_6_), channel_id=1, source_target_pairs={{0,192},{1,193},{2,194},{3,195},{4,196},{5,197},{6,198},{7,199},{8... | collective-permute-start | bytes 786440 | tf_op jit(solution)/shard_map/ppermute | solution.py:362
  83.1 18.9 %collective-permute-start.24 = (bf16[128,1024]{1,0:T(8,128)(2,1)S(1)}, bf16[128,1024]{1,0:T(8,128)(2,1)S(1)}, u32[]{:S(2)}, u32[]{:S(2)}) collective-permute-start(bf16[128,1024]{1,0:T(8,128)(2,1)S(1)} %collective-permute-done.22.refs_9_), channel_id=1, source_target_pairs={{0,64},{1,65},{2,66},{3,67},{4,68},{5,69},{6,198},{7,199},{8,72},{... | collective-permute-start | bytes 786440 | tf_op jit(solution)/shard_map/ppermute | solution.py:362
  89.8 16.6 %collective-permute-start.28 = (bf16[128,1024]{1,0:T(8,128)(2,1)S(1)}, bf16[128,1024]{1,0:T(8,128)(2,1)S(1)}, u32[]{:S(2)}, u32[]{:S(2)}) collective-permute-start(bf16[128,1024]{1,0:T(8,128)(2,1)S(1)} %collective-permute-done.27.refs_3_), channel_id=1, source_target_pairs={{0,192},{1,193},{2,194},{3,195},{4,196},{5,197},{6,198},{7,199},{8... | collective-permute-start | bytes 786440 | tf_op jit(solution)/shard_map/ppermute | solution.py:362
  95.4 34.0 %collective-permute-start.23 = (bf16[1280,1024]{1,0:T(8,128)(2,1)S(1)}, bf16[1280,1024]{1,0:T(8,128)(2,1)S(1)}, u32[]{:S(2)}, u32[]{:S(2)}) collective-permute-start(bf16[1280,1024]{1,0:T(8,128)(2,1)S(1)} %stack.4.refs_4_), channel_id=1, source_target_pairs={{0,1},{1,0},{2,3},{3,2},{4,5},{5,4},{6,7},{7,6},{8,9},{9,8},{10,11... | collective-permute-start | bytes 7864328 | tf_op jit(solution)/shard_map/ppermute | solution.py:362
  102.0 10.0 %collective-permute-start.25 = (bf16[128,1024]{1,0:T(8,128)(2,1)S(1)}, bf16[128,1024]{1,0:T(8,128)(2,1)S(1)}, u32[]{:S(2)}, u32[]{:S(2)}) collective-permute-start(bf16[128,1024]{1,0:T(8,128)(2,1)S(1)} %collective-permute-done.24.refs_0_), channel_id=1, source_target_pairs={{0,64},{1,65},{2,66},{3,67},{4,68},{5,69},{6,198},{7,199},{8,72},{... | collective-permute-start | bytes 786440 | tf_op jit(solution)/shard_map/ppermute | solution.py:362
  106.4 11.2 %collective-permute-start.29 = (bf16[128,1024]{1,0:T(8,128)(2,1)S(1)}, bf16[128,1024]{1,0:T(8,128)(2,1)S(1)}, u32[]{:S(2)}, u32[]{:S(2)}) collective-permute-start(bf16[128,1024]{1,0:T(8,128)(2,1)S(1)} %collective-permute-done.28.refs_4_), channel_id=1, source_target_pairs={{0,192},{1,193},{2,194},{3,195},{4,196},{5,197},{6,198},{7,199},{8... | collective-permute-start | bytes 786440 | tf_op jit(solution)/shard_map/ppermute | solution.py:362
  117.8 11.6 %collective-permute-start.30 = (bf16[768,1024]{1,0:T(8,128)(2,1)S(1)}, bf16[768,1024]{1,0:T(8,128)(2,1)S(1)}, u32[]{:S(2)}, u32[]{:S(2)}) collective-permute-start(bf16[768,1024]{1,0:T(8,128)(2,1)S(1)} %stack.5.refs_5_), channel_id=1, source_target_pairs={{0,1},{1,0},{2,3},{3,2},{4,5},{5,4},{6,7},{7,6},{8,9},{9,8},{10,11... | collective-permute-start | bytes 4718600 | tf_op jit(solution)/shard_map/ppermute | solution.py:362
  121.3 3.8 %collective-permute-start.19 = (bf16[512,512]{1,0:T(8,128)(2,1)S(1)}, bf16[512,512]{1,0:T(8,128)(2,1)S(1)}, u32[]{:S(2)}, u32[]{:S(2)}) collective-permute-start(bf16[512,512]{1,0:T(8,128)(2,1)S(1)} %get-tuple-element.27), channel_id=1, source_target_pairs={{0,1},{1,0},{2,3},{3,2},{4,5},{5,4},{6,7},{7,6},{8,9},{9,8},{10,11... | collective-permute-start | bytes 1572872 | tf_op jit(solution)/shard_map/ppermute | solution.py:362
  121.4 4.4 %collective-permute-start.20 = (bf16[512,512]{1,0:T(8,128)(2,1)S(1)}, bf16[512,512]{1,0:T(8,128)(2,1)S(1)}, u32[]{:S(2)}, u32[]{:S(2)}) collective-permute-start(bf16[512,512]{1,0:T(8,128)(2,1)S(1)} %get-tuple-element.28), channel_id=1, source_target_pairs={{0,1},{1,0},{2,3},{3,2},{4,5},{5,4},{6,7},{7,6},{8,9},{9,8},{10,11... | collective-permute-start | bytes 1572872 | tf_op jit(solution)/shard_map/ppermute | solution.py:362

commit v4 on v3

--- a/solution.py
+++ b/solution.py
@@ -12,8 +12,8 @@
 WINDOW = 14 * BLK
 WORK = 20 * 1024 * WINDOW
 CHUNKS = (512, 512)
-EARLY = [(0, i) for i in range(4)] + [(1, i) for i in range(4)] + [(2, 0), (2, 1)]
-LATE = [(2, 2), (2, 3)] + [(3, i) for i in range(4)]
+EARLY = [(0, i) for i in range(4)] + [(1, i) for i in range(4)] + [(2, i) for i in range(3)] + [(3, 0), (3, 1)]
+LATE = [(2, 3), (3, 2), (3, 3)]
 ANY = pl.BlockSpec(memory_space=pl.ANY)
 HBM = pl.BlockSpec(memory_space=pltpu.HBM)
 SMEM = pl.BlockSpec(memory_space=pltpu.SMEM)

time: 133 us -> 134 us (level)
  waiting for transfers between devices: 80.4 us -> 83.6 us
  starting transfers between devices: 29.5 us -> 26.9 us
    ppermute x31, waiting for transfers between devices: 80.4 us -> 83.6 us  [move(): return lax.ppermute(array, 'rows', route)]
    ppermute x31, starting transfers between devices: 29.5 us -> 26.9 us  [move(): return lax.ppermute(array, 'rows', route)]
where the time goes in v4:
time: 134 us
  waiting for transfers between devices  83.6 us (62%)
  starting transfers between devices  26.9 us (20%)
  Pallas kernels  19.2 us (14%)
  local copies, waits for them, and re-layouts  2.34 us (2%)
  between operations  1.69 us (1%)
    ppermute x31, waiting for transfers between devices, move(): return lax.ppermute(array, 'rows', route)  83.6 us
    ppermute x31, starting transfers between devices, move(): return lax.ppermute(array, 'rows', route)  26.9 us
    pallas_call x18, Pallas kernels, call(): pl.pallas_call(kernel, out_shape=shapes, in_specs=ins, out_specs=[spec fo...  19.2 us
  transfers between devices with their start and end apart: 31, of which 18 were waited for; matrix products, arithmetic and copies ran while one was open for 0% of the time, Pallas kernels for 7%

profile of v4, /device:TPU:225, one launch (start us, length us, event | category | flops | bytes accessed | tf_op | source)
XLA Modules:
  0.0 133.7 jit_solution(3914908763158443037)
XLA Ops:
  0.0 1.6 %copy-done = bf16[512,2048]{1,0:T(8,128)(2,1)S(1)} copy-done((bf16[512,2048]{1,0:T(8,128)(2,1)S(1)}, bf16[512,2048]{1,0:T(8,128)(2,1)}, u32[]{:S(2)}) %copy-start) | copy-done | bytes 2097176
  1.6 0.2 split.1
  1.8 0.8 collective-permute-start.5
  2.6 0.7 collective-permute-start
  3.3 2.0 %collective-permute-done.got_ref = bf16[8,2048]{1,0:T(8,128)(2,1)S(1)} collective-permute-done((bf16[8,2048]{1,0:T(8,128)(2,1)S(1)}, bf16[8,2048]{1,0:T(8,128)(2,1)S(1)}, u32[]{:S(2)}, u32[]{:S(2)}) %collective-permute-start) | collective-permute-done | bytes 32800 | tf_op jit(solution)/shard_map/ppermute | solution.py:362
  5.4 1.4 %collective-permute-start.1 = (bf16[16,2048]{1,0:T(8,128)(2,1)S(1)}, bf16[16,2048]{1,0:T(8,128)(2,1)S(1)}, u32[]{:S(2)}, u32[]{:S(2)}) collective-permute-start(bf16[16,2048]{1,0:T(8,128)(2,1)S(1)} %join.1.refs_0_), channel_id=1, source_target_pairs={{6,0},{7,1},{0,2},{1,3},{2,4},{3,5},{4,6},{5,7},{14,8},{15,9},{8,1... | collective-permute-start | bytes 196616 | tf_op jit(solution)/shard_map/ppermute | solution.py:362
  6.7 2.6 %collective-permute-start.2 = (bf16[16,2048]{1,0:T(8,128)(2,1)S(1)}, bf16[16,2048]{1,0:T(8,128)(2,1)S(1)}, u32[]{:S(2)}, u32[]{:S(2)}) collective-permute-start(bf16[16,2048]{1,0:T(8,128)(2,1)S(1)} %join.1.refs_0_), channel_id=1, source_target_pairs={{4,0},{5,1},{6,2},{7,3},{0,4},{1,5},{2,6},{3,7},{12,8},{13,9},{14,... | collective-permute-start | bytes 196616 | tf_op jit(solution)/shard_map/ppermute | solution.py:362
  9.4 1.1 collective-permute-start.3
  10.4 1.3 %collective-permute-done.2.refs_2_ = bf16[16,2048]{1,0:T(8,128)(2,1)S(1)} collective-permute-done((bf16[16,2048]{1,0:T(8,128)(2,1)S(1)}, bf16[16,2048]{1,0:T(8,128)(2,1)S(1)}, u32[]{:S(2)}, u32[]{:S(2)}) %collective-permute-start.2) | collective-permute-done | bytes 65568 | tf_op jit(solution)/shard_map/ppermute | solution.py:362
  11.8 1.5 %collective-permute-done.3.refs_3_ = bf16[16,2048]{1,0:T(8,128)(2,1)S(1)} collective-permute-done((bf16[16,2048]{1,0:T(8,128)(2,1)S(1)}, bf16[16,2048]{1,0:T(8,128)(2,1)S(1)}, u32[]{:S(2)}, u32[]{:S(2)}) %collective-permute-start.3) | collective-permute-done | bytes 65568 | tf_op jit(solution)/shard_map/ppermute | solution.py:362
  13.3 2.6 %collective-permute-start.4 = (bf16[64,1024]{1,0:T(8,128)(2,1)S(1)}, bf16[64,1024]{1,0:T(8,128)(2,1)S(1)}, u32[]{:S(2)}, u32[]{:S(2)}) collective-permute-start(bf16[64,1024]{1,0:T(8,128)(2,1)S(1)} %get-tuple-element.18), channel_id=1, source_target_pairs={{0,1},{1,0},{2,3},{3,2},{4,5},{5,4},{6,7},{7,6},{8,9},{9,8},{10,11... | collective-permute-start | bytes 393224 | tf_op jit(solution)/shard_map/ppermute | solution.py:362
  16.0 0.4 assemble.1
  16.4 0.6 collective-permute-done.4.got_ref
  17.0 0.7 copy-done.2
  17.7 2.1 %build_bands.1 = (bf16[256,1792]{1,0:T(8,128)(2,1)S(1)}, bf16[256,1792]{1,0:T(8,128)(2,1)S(1)}) custom-call(s32[4,12]{1,0:T(4,128)S(1)} %copy-done.5, s32[4,4,256]{2,1,0:T(4,128)S(1)} %bitcast.1, bf16[4,12,128,128]{3,2,1,0:T(8,128)(2,1)S(1)} %copy-done.2, bf16[128,1024]{1,0:T(8,128)(2,1)S(1)} %slab.1.after_ref.refs_0_), custom_call_target="tpu_custom_call" | custom-call | tf_op jit(solution)/shard_map/build_bands/pallas_call | solution.py:25
  19.9 0.1 collective-permute-start.6
  20.0 0.5 collective-permute-start.7
  20.5 3.5 %collective-permute-start.9 = (bf16[768,1024]{1,0:T(8,128)(2,1)S(1)}, bf16[768,1024]{1,0:T(8,128)(2,1)S(1)}, u32[]{:S(2)}, u32[]{:S(2)}) collective-permute-start(bf16[768,1024]{1,0:T(8,128)(2,1)S(1)} %get-tuple-element.22.dn.xdn), channel_id=1, source_target_pairs={{0,254},{1,255},{2,0},{3,1},{4,2},{5,3},{6,4},{7,5},{8,6},{9,7},{1... | collective-permute-start | bytes 4718600 | tf_op jit(solution)/shard_map/ppermute | solution.py:362
  24.1 0.2 merge_bands.1.refs_1_.bands
  24.4 1.3 collective-permute-start.12
  25.7 12.7 %collective-permute-done.10.refs_0_ = bf16[128,1024]{1,0:T(8,128)(2,1)S(1)} collective-permute-done((bf16[128,1024]{1,0:T(8,128)(2,1)S(1)}, bf16[128,1024]{1,0:T(8,128)(2,1)S(1)}, u32[]{:S(2)}, u32[]{:S(2)}) %collective-permute-start.10) | collective-permute-done | bytes 262176 | tf_op jit(solution)/shard_map/ppermute | solution.py:362
  38.4 0.2 collective-permute-start.13
  38.6 0.2 collective-permute-start.11
  38.8 7.6 %collective-permute-done.15.refs_5_ = bf16[128,1024]{1,0:T(8,128)(2,1)S(1)} collective-permute-done((bf16[128,1024]{1,0:T(8,128)(2,1)S(1)}, bf16[128,1024]{1,0:T(8,128)(2,1)S(1)}, u32[]{:S(2)}, u32[]{:S(2)}) %collective-permute-start.15) | collective-permute-done | bytes 262176 | tf_op jit(solution)/shard_map/ppermute | solution.py:362
  46.3 5.6 %collective-permute-done.13.refs_2_ = bf16[128,1024]{1,0:T(8,128)(2,1)S(1)} collective-permute-done((bf16[128,1024]{1,0:T(8,128)(2,1)S(1)}, bf16[128,1024]{1,0:T(8,128)(2,1)S(1)}, u32[]{:S(2)}, u32[]{:S(2)}) %collective-permute-start.13) | collective-permute-done | bytes 262176 | tf_op jit(solution)/shard_map/ppermute | solution.py:362
  53.3 4.3 %collective-permute-done.16.rest_2_.refs_0_ = bf16[128,1024]{1,0:T(8,128)(2,1)S(1)} collective-permute-done((bf16[128,1024]{1,0:T(8,128)(2,1)S(1)}, bf16[128,1024]{1,0:T(8,128)(2,1)S(1)}, u32[]{:S(2)}, u32[]{:S(2)}) %collective-permute-start.16) | collective-permute-done | bytes 262176 | tf_op jit(solution)/shard_map/ppermute | solution.py:362
  57.6 1.0 collective-permute-done.8.left
  58.6 4.6 %collective-permute-done.14.rest_1_.refs_3_ = bf16[128,1024]{1,0:T(8,128)(2,1)S(1)} collective-permute-done((bf16[128,1024]{1,0:T(8,128)(2,1)S(1)}, bf16[128,1024]{1,0:T(8,128)(2,1)S(1)}, u32[]{:S(2)}, u32[]{:S(2)}) %collective-permute-start.14) | collective-permute-done | bytes 262176 | tf_op jit(solution)/shard_map/ppermute | solution.py:362
  63.2 4.0 %first_pass.1 = (bf16[768,1024]{1,0:T(8,128)(2,1)S(1)}, bf16[768,1024]{1,0:T(8,128)(2,1)S(1)}) custom-call(f32[1]{0:T(128)S(6)} %copy.16.center, f32[1]{0:T(128)S(6)} %copy.17.half, bf16[4,256,1792]{2,1,0:T(8,128)(2,1)S(1)} %merge_bands.1.refs_1_.bands, bf16[768,1024]{1,0:T(8,128)(2,1)S(1)} %collective-permute-done.8.left, ...), custom_call_target="tpu_custom_call" | custom-call | flops 1879048192 | tf_op jit(solution)/shard_map/first_pass/pallas_call | solution.py:25
  67.2 0.1 collective-permute-start.17
  67.3 3.6 %collective-permute-start.18 = (bf16[768,1024]{1,0:T(8,128)(2,1)S(1)}, bf16[768,1024]{1,0:T(8,128)(2,1)S(1)}, u32[]{:S(2)}, u32[]{:S(2)}) collective-permute-start(bf16[768,1024]{1,0:T(8,128)(2,1)S(1)} %get-tuple-element.24.dn), channel_id=1, source_target_pairs={{0,254},{1,255},{2,0},{3,1},{4,2},{5,3},{6,4},{7,5},{8,6},{9,7},{1... | collective-permute-start | bytes 4718600 | tf_op jit(solution)/shard_map/ppermute | solution.py:362
  70.9 12.3 %collective-permute-done.24.refs_11_ = bf16[128,1024]{1,0:T(8,128)(2,1)S(1)} collective-permute-done((bf16[128,1024]{1,0:T(8,128)(2,1)S(1)}, bf16[128,1024]{1,0:T(8,128)(2,1)S(1)}, u32[]{:S(2)}, u32[]{:S(2)}) %collective-permute-start.24) | collective-permute-done | bytes 262176 | tf_op jit(solution)/shard_map/ppermute | solution.py:362
  83.2 6.6 %collective-permute-done.25.refs_12_ = bf16[128,1024]{1,0:T(8,128)(2,1)S(1)} collective-permute-done((bf16[128,1024]{1,0:T(8,128)(2,1)S(1)}, bf16[128,1024]{1,0:T(8,128)(2,1)S(1)}, u32[]{:S(2)}, u32[]{:S(2)}) %collective-permute-start.25) | collective-permute-done | bytes 262176 | tf_op jit(solution)/shard_map/ppermute | solution.py:362
  89.8 5.3 %collective-permute-done.21.refs_7_ = bf16[128,1024]{1,0:T(8,128)(2,1)S(1)} collective-permute-done((bf16[128,1024]{1,0:T(8,128)(2,1)S(1)}, bf16[128,1024]{1,0:T(8,128)(2,1)S(1)}, u32[]{:S(2)}, u32[]{:S(2)}) %collective-permute-start.21) | collective-permute-done | bytes 262176 | tf_op jit(solution)/shard_map/ppermute | solution.py:362
  95.2 5.6 %collective-permute-done.23.refs_10_ = bf16[128,1024]{1,0:T(8,128)(2,1)S(1)} collective-permute-done((bf16[128,1024]{1,0:T(8,128)(2,1)S(1)}, bf16[128,1024]{1,0:T(8,128)(2,1)S(1)}, u32[]{:S(2)}, u32[]{:S(2)}) %collective-permute-start.23) | collective-permute-done | bytes 262176 | tf_op jit(solution)/shard_map/ppermute | solution.py:362
  100.8 0.2 stack.4.refs_4_
  101.0 6.4 %collective-permute-start.26 = (bf16[1664,1024]{1,0:T(8,128)(2,1)S(1)}, bf16[1664,1024]{1,0:T(8,128)(2,1)S(1)}, u32[]{:S(2)}, u32[]{:S(2)}) collective-permute-start(bf16[1664,1024]{1,0:T(8,128)(2,1)S(1)} %stack.4.refs_4_), channel_id=1, source_target_pairs={{0,1},{1,0},{2,3},{3,2},{4,5},{5,4},{6,7},{7,6},{8,9},{9,8},{10,11... | collective-permute-start | bytes 10223624 | tf_op jit(solution)/shard_map/ppermute | solution.py:362
  107.4 2.4 %second_pass.2 = (bf16[512,512]{1,0:T(8,128)(2,1)S(1)}, bf16[512,512]{1,0:T(8,128)(2,1)S(1)}) custom-call(f32[1]{0:T(128)S(6)} %copy.16.center, f32[1]{0:T(128)S(6)} %copy.17.half, bf16[4,256,1792]{2,1,0:T(8,128)(2,1)S(1)} %merge_bands.1.refs_1_.bands, bf16[768,1024]{1,0:T(8,128)(2,1)S(1)} %collective-permute-done.17.left, ...), custom_call_target="tpu_custom_call" | custom-call | flops 18790481920 | tf_op jit(solution)/shard_map/second_pass/pallas_call | solution.py:25
  109.8 2.4 %second_pass.3 = (bf16[512,512]{1,0:T(8,128)(2,1)S(1)}, bf16[512,512]{1,0:T(8,128)(2,1)S(1)}) custom-call(f32[1]{0:T(128)S(6)} %copy.16.center, f32[1]{0:T(128)S(6)} %copy.17.half, bf16[4,256,1792]{2,1,0:T(8,128)(2,1)S(1)} %merge_bands.1.refs_1_.bands, bf16[768,1024]{1,0:T(8,128)(2,1)S(1)} %collective-permute-done.17.left, ...), custom_call_target="tpu_custom_call" | custom-call | flops 18790481920 | tf_op jit(solution)/shard_map/second_pass/pallas_call | solution.py:25
  112.2 4.0 %collective-permute-done.27.refs_0_ = bf16[128,1024]{1,0:T(8,128)(2,1)S(1)} collective-permute-done((bf16[128,1024]{1,0:T(8,128)(2,1)S(1)}, bf16[128,1024]{1,0:T(8,128)(2,1)S(1)}, u32[]{:S(2)}, u32[]{:S(2)}) %collective-permute-start.27) | collective-permute-done | bytes 262176 | tf_op jit(solution)/shard_map/ppermute | solution.py:362
  116.2 5.6 %collective-permute-done.29.refs_2_ = bf16[128,1024]{1,0:T(8,128)(2,1)S(1)} collective-permute-done((bf16[128,1024]{1,0:T(8,128)(2,1)S(1)}, bf16[128,1024]{1,0:T(8,128)(2,1)S(1)}, u32[]{:S(2)}, u32[]{:S(2)}) %collective-permute-start.29) | collective-permute-done | bytes 262176 | tf_op jit(solution)/shard_map/ppermute | solution.py:362
  121.9 1.2 collective-permute-start.30
  123.1 0.1 collective-permute-start.19
  123.2 0.4 collective-permute-start.20
  123.6 2.2 %collective-permute-done.19.refs_2_ = bf16[512,512]{1,0:T(8,128)(2,1)S(1)} collective-permute-done((bf16[512,512]{1,0:T(8,128)(2,1)S(1)}, bf16[512,512]{1,0:T(8,128)(2,1)S(1)}, u32[]{:S(2)}, u32[]{:S(2)}) %collective-permute-start.19) | collective-permute-done | bytes 524320 | tf_op jit(solution)/shard_map/ppermute | solution.py:362
  125.8 0.7 collective-permute-done.20.refs_3_
  126.5 3.5 %rotate.2.refs_6_ = bf16[512,2048]{1,0:T(8,128)(2,1)} custom-call(bf16[512,512]{1,0:T(8,128)(2,1)S(1)} %get-tuple-element.25.after.refs_0_, bf16[512,512]{1,0:T(8,128)(2,1)S(1)} %get-tuple-element.26.refs_3_.refs_1_, bf16[512,512]{1,0:T(8,128)(2,1)S(1)} %collective-permute-done.19.refs_2_, bf16[512,512]{1,0:T(8,128)(2,1)S(1)} %collective-permute-done.20.refs_3_, ...), custom_call_target="tpu_custom_call" | custom-call | tf_op jit(solution)/shard_map/rotate/pallas_call | solution.py:25
  130.0 3.5 %rotate.3 = bf16[512,2048]{1,0:T(8,128)(2,1)} custom-call(bf16[512,512]{1,0:T(8,128)(2,1)S(1)} %get-tuple-element.25.after.refs_0_, bf16[512,512]{1,0:T(8,128)(2,1)S(1)} %get-tuple-element.26.refs_3_.refs_1_, bf16[512,512]{1,0:T(8,128)(2,1)S(1)} %collective-permute-done.19.refs_2_, ...), custom_call_target="tpu_custom_call", output_to_operand_aliasing={{}: (6, {})} | custom-call | tf_op jit(solution)/shard_map/rotate/pallas_call | solution.py:25
  (44 shorter events, 0.5 us)
Async XLA Ops:
  0.0 1.6 %copy-start = (bf16[512,2048]{1,0:T(8,128)(2,1)S(1)}, bf16[512,2048]{1,0:T(8,128)(2,1)}, u32[]{:S(2)}) copy-start(bf16[512,2048]{1,0:T(8,128)(2,1)} %x_ref.3) | copy-start | bytes 6291460
  1.6 1.0 copy-start.3
  1.6 14.4 %copy-start.1 = (bf16[512,2048]{1,0:T(8,128)(2,1)S(1)}, bf16[512,2048]{1,0:T(8,128)(2,1)}, u32[]{:S(2)}) copy-start(bf16[512,2048]{1,0:T(8,128)(2,1)} %x_ref.3) | copy-start | bytes 6291460
  1.8 14.1 %collective-permute-start.5 = (bf16[512,1024]{1,0:T(8,128)(2,1)S(1)}, bf16[512,1024]{1,0:T(8,128)(2,1)S(1)}, u32[]{:S(2)}, u32[]{:S(2)}) collective-permute-start(bf16[512,1024]{1,0:T(8,128)(2,1)S(1)} %split.1), channel_id=1, source_target_pairs={{0,1},{1,0},{2,3},{3,2},{4,5},{5,4},{6,7},{7,6},{8,9},{9,8},{10,11... | collective-permute-start | bytes 3145736 | tf_op jit(solution)/shard_map/ppermute | solution.py:362
  2.6 2.8 %collective-permute-start = (bf16[8,2048]{1,0:T(8,128)(2,1)S(1)}, bf16[8,2048]{1,0:T(8,128)(2,1)S(1)}, u32[]{:S(2)}, u32[]{:S(2)}) collective-permute-start(bf16[8,2048]{1,0:T(8,128)(2,1)S(1)} %copy-done.3), channel_id=1, source_target_pairs={{0,8},{1,9},{2,10},{3,11},{4,12},{5,13},{6,14},{7,15},{8,0},{9,1},... | collective-permute-start | bytes 98312 | tf_op jit(solution)/shard_map/ppermute | solution.py:362
  5.4 5.1 %collective-permute-start.1 = (bf16[16,2048]{1,0:T(8,128)(2,1)S(1)}, bf16[16,2048]{1,0:T(8,128)(2,1)S(1)}, u32[]{:S(2)}, u32[]{:S(2)}) collective-permute-start(bf16[16,2048]{1,0:T(8,128)(2,1)S(1)} %join.1.refs_0_), channel_id=1, source_target_pairs={{6,0},{7,1},{0,2},{1,3},{2,4},{3,5},{4,6},{5,7},{14,8},{15,9},{8,1... | collective-permute-start | bytes 196616 | tf_op jit(solution)/shard_map/ppermute | solution.py:362
  6.7 5.0 %collective-permute-start.2 = (bf16[16,2048]{1,0:T(8,128)(2,1)S(1)}, bf16[16,2048]{1,0:T(8,128)(2,1)S(1)}, u32[]{:S(2)}, u32[]{:S(2)}) collective-permute-start(bf16[16,2048]{1,0:T(8,128)(2,1)S(1)} %join.1.refs_0_), channel_id=1, source_target_pairs={{4,0},{5,1},{6,2},{7,3},{0,4},{1,5},{2,6},{3,7},{12,8},{13,9},{14,... | collective-permute-start | bytes 196616 | tf_op jit(solution)/shard_map/ppermute | solution.py:362
  9.4 3.9 %collective-permute-start.3 = (bf16[16,2048]{1,0:T(8,128)(2,1)S(1)}, bf16[16,2048]{1,0:T(8,128)(2,1)S(1)}, u32[]{:S(2)}, u32[]{:S(2)}) collective-permute-start(bf16[16,2048]{1,0:T(8,128)(2,1)S(1)} %join.1.refs_0_), channel_id=1, source_target_pairs={{2,0},{3,1},{4,2},{5,3},{6,4},{7,5},{0,6},{1,7},{10,8},{11,9},{12,... | collective-permute-start | bytes 196616 | tf_op jit(solution)/shard_map/ppermute | solution.py:362
  13.3 3.6 %collective-permute-start.4 = (bf16[64,1024]{1,0:T(8,128)(2,1)S(1)}, bf16[64,1024]{1,0:T(8,128)(2,1)S(1)}, u32[]{:S(2)}, u32[]{:S(2)}) collective-permute-start(bf16[64,1024]{1,0:T(8,128)(2,1)S(1)} %get-tuple-element.18), channel_id=1, source_target_pairs={{0,1},{1,0},{2,3},{3,2},{4,5},{5,4},{6,7},{7,6},{8,9},{9,8},{10,11... | collective-permute-start | bytes 393224 | tf_op jit(solution)/shard_map/ppermute | solution.py:362
  16.3 1.4 %copy-start.2 = (bf16[4,12,128,128]{3,2,1,0:T(8,128)(2,1)S(1)}, bf16[4,12,128,128]{3,2,1,0:T(8,128)(2,1)}, u32[]{:S(2)}) copy-start(bf16[4,12,128,128]{3,2,1,0:T(8,128)(2,1)} %h_ref.1) | copy-start | bytes 4718596
  16.3 1.4 %copy-start.4 = (s32[256,4,4]{0,2,1:T(4,128)S(1)}, s32[256,4,4]{0,2,1:T(4,128)}, u32[]{:S(2)}) copy-start(s32[256,4,4]{0,2,1:T(4,128)} %param.10) | copy-start | bytes 49156
  16.4 1.4 %copy-start.5 = (s32[4,12]{1,0:T(4,128)S(1)}, s32[4,12]{1,0:T(4,128)}, u32[]{:S(2)}) copy-start(s32[4,12]{1,0:T(4,128)} %col_ref.1) | copy-start | bytes 580
  19.9 4.2 %collective-permute-start.6 = (bf16[256,1792]{1,0:T(8,128)(2,1)S(1)}, bf16[256,1792]{1,0:T(8,128)(2,1)S(1)}, u32[]{:S(2)}, u32[]{:S(2)}) collective-permute-start(bf16[256,1792]{1,0:T(8,128)(2,1)S(1)} %get-tuple-element.20.refs_0_), channel_id=1, source_target_pairs={{0,1},{1,0},{2,3},{3,2},{4,5},{5,4},{6,7},{7,6},{8,9},{9,8},{10,11... | collective-permute-start | bytes 2752520 | tf_op jit(solution)/shard_map/ppermute | solution.py:362
  20.0 4.1 %collective-permute-start.7 = (bf16[256,1792]{1,0:T(8,128)(2,1)S(1)}, bf16[256,1792]{1,0:T(8,128)(2,1)S(1)}, u32[]{:S(2)}, u32[]{:S(2)}) collective-permute-start(bf16[256,1792]{1,0:T(8,128)(2,1)S(1)} %get-tuple-element.21.refs_1_), channel_id=1, source_target_pairs={{0,1},{1,0},{2,3},{3,2},{4,5},{5,4},{6,7},{7,6},{8,9},{9,8},{10,11... | collective-permute-start | bytes 2752520 | tf_op jit(solution)/shard_map/ppermute | solution.py:362
  20.5 38.1 %collective-permute-start.8 = (bf16[768,1024]{1,0:T(8,128)(2,1)S(1)}, bf16[768,1024]{1,0:T(8,128)(2,1)S(1)}, u32[]{:S(2)}, u32[]{:S(2)}) collective-permute-start(bf16[768,1024]{1,0:T(8,128)(2,1)S(1)} %get-tuple-element.19.after_ref.up.xup), channel_id=1, source_target_pairs={{0,2},{1,3},{2,4},{3,5},{4,6},{5,7},{6,8},{7,9},{8,10},{9,11},{10,... | collective-permute-start | bytes 4718600 | tf_op jit(solution)/shard_map/ppermute | solution.py:362
  20.5 38.0 %collective-permute-start.9 = (bf16[768,1024]{1,0:T(8,128)(2,1)S(1)}, bf16[768,1024]{1,0:T(8,128)(2,1)S(1)}, u32[]{:S(2)}, u32[]{:S(2)}) collective-permute-start(bf16[768,1024]{1,0:T(8,128)(2,1)S(1)} %get-tuple-element.22.dn.xdn), channel_id=1, source_target_pairs={{0,254},{1,255},{2,0},{3,1},{4,2},{5,3},{6,4},{7,5},{8,6},{9,7},{1... | collective-permute-start | bytes 4718600 | tf_op jit(solution)/shard_map/ppermute | solution.py:362
  24.1 14.3 %collective-permute-start.10 = (bf16[128,1024]{1,0:T(8,128)(2,1)S(1)}, bf16[128,1024]{1,0:T(8,128)(2,1)S(1)}, u32[]{:S(2)}, u32[]{:S(2)}) collective-permute-start(bf16[128,1024]{1,0:T(8,128)(2,1)S(1)} %slab.1.after_ref.refs_0_), channel_id=1, source_target_pairs={{0,16},{1,17},{2,18},{3,19},{4,52},{5,53},{6,54},{7,55},{8,24},{9,... | collective-permute-start | bytes 786440 | tf_op jit(solution)/shard_map/ppermute | solution.py:362
  24.4 14.0 %collective-permute-start.12 = (bf16[128,1024]{1,0:T(8,128)(2,1)S(1)}, bf16[128,1024]{1,0:T(8,128)(2,1)S(1)}, u32[]{:S(2)}, u32[]{:S(2)}) collective-permute-start(bf16[128,1024]{1,0:T(8,128)(2,1)S(1)} %stack.3.refs_0_), channel_id=1, source_target_pairs={{0,64},{1,65},{2,66},{3,67},{4,68},{5,69},{6,198},{7,199},{8,72},{... | collective-permute-start | bytes 786440 | tf_op jit(solution)/shard_map/ppermute | solution.py:362
  38.4 7.9 %collective-permute-start.15 = (bf16[128,1024]{1,0:T(8,128)(2,1)S(1)}, bf16[128,1024]{1,0:T(8,128)(2,1)S(1)}, u32[]{:S(2)}, u32[]{:S(2)}) collective-permute-start(bf16[128,1024]{1,0:T(8,128)(2,1)S(1)} %tie.3.refs_4_), channel_id=1, source_target_pairs={{0,192},{1,193},{2,194},{3,195},{4,196},{5,197},{6,198},{7,199},{8... | collective-permute-start | bytes 786440 | tf_op jit(solution)/shard_map/ppermute | solution.py:362
  38.4 13.5 %collective-permute-start.13 = (bf16[128,1024]{1,0:T(8,128)(2,1)S(1)}, bf16[128,1024]{1,0:T(8,128)(2,1)S(1)}, u32[]{:S(2)}, u32[]{:S(2)}) collective-permute-start(bf16[128,1024]{1,0:T(8,128)(2,1)S(1)} %collective-permute-done.12.refs_1_), channel_id=1, source_target_pairs={{0,64},{1,65},{2,66},{3,67},{4,68},{5,69},{6,198},{7,199},{8,72},{... | collective-permute-start | bytes 786440 | tf_op jit(solution)/shard_map/ppermute | solution.py:362
  38.6 14.7 %collective-permute-start.11 = (bf16[128,1024]{1,0:T(8,128)(2,1)S(1)}, bf16[128,1024]{1,0:T(8,128)(2,1)S(1)}, u32[]{:S(2)}, u32[]{:S(2)}) collective-permute-start(bf16[128,1024]{1,0:T(8,128)(2,1)S(1)} %tie.3.refs_4_), channel_id=1, source_target_pairs={{0,16},{1,17},{2,18},{3,19},{4,52},{5,53},{6,54},{7,55},{8,24},{9,... | collective-permute-start | bytes 786440 | tf_op jit(solution)/shard_map/ppermute | solution.py:362
  46.3 11.2 %collective-permute-start.16 = (bf16[128,1024]{1,0:T(8,128)(2,1)S(1)}, bf16[128,1024]{1,0:T(8,128)(2,1)S(1)}, u32[]{:S(2)}, u32[]{:S(2)}) collective-permute-start(bf16[128,1024]{1,0:T(8,128)(2,1)S(1)} %collective-permute-done.15.refs_5_), channel_id=1, source_target_pairs={{0,192},{1,193},{2,194},{3,195},{4,196},{5,197},{6,198},{7,199},{8... | collective-permute-start | bytes 786440 | tf_op jit(solution)/shard_map/ppermute | solution.py:362
  51.9 11.2 %collective-permute-start.14 = (bf16[128,1024]{1,0:T(8,128)(2,1)S(1)}, bf16[128,1024]{1,0:T(8,128)(2,1)S(1)}, u32[]{:S(2)}, u32[]{:S(2)}) collective-permute-start(bf16[128,1024]{1,0:T(8,128)(2,1)S(1)} %collective-permute-done.13.refs_2_), channel_id=1, source_target_pairs={{0,64},{1,65},{2,66},{3,67},{4,68},{5,69},{6,198},{7,199},{8,72},{... | collective-permute-start | bytes 786440 | tf_op jit(solution)/shard_map/ppermute | solution.py:362
  67.2 40.2 %collective-permute-start.17 = (bf16[768,1024]{1,0:T(8,128)(2,1)S(1)}, bf16[768,1024]{1,0:T(8,128)(2,1)S(1)}, u32[]{:S(2)}, u32[]{:S(2)}) collective-permute-start(bf16[768,1024]{1,0:T(8,128)(2,1)S(1)} %get-tuple-element.23.up.after.refs_1_), channel_id=1, source_target_pairs={{0,2},{1,3},{2,4},{3,5},{4,6},{5,7},{6,8},{7,9},{8,10},{9,11},{10,... | collective-permute-start | bytes 4718600 | tf_op jit(solution)/shard_map/ppermute | solution.py:362
  67.3 40.1 %collective-permute-start.18 = (bf16[768,1024]{1,0:T(8,128)(2,1)S(1)}, bf16[768,1024]{1,0:T(8,128)(2,1)S(1)}, u32[]{:S(2)}, u32[]{:S(2)}) collective-permute-start(bf16[768,1024]{1,0:T(8,128)(2,1)S(1)} %get-tuple-element.24.dn), channel_id=1, source_target_pairs={{0,254},{1,255},{2,0},{3,1},{4,2},{5,3},{6,4},{7,5},{8,6},{9,7},{1... | collective-permute-start | bytes 4718600 | tf_op jit(solution)/shard_map/ppermute | solution.py:362
  70.8 12.3 %collective-permute-start.24 = (bf16[128,1024]{1,0:T(8,128)(2,1)S(1)}, bf16[128,1024]{1,0:T(8,128)(2,1)S(1)}, u32[]{:S(2)}, u32[]{:S(2)}) collective-permute-start(bf16[128,1024]{1,0:T(8,128)(2,1)S(1)} %tie.5.refs_8_), channel_id=1, source_target_pairs={{0,16},{1,17},{2,18},{3,19},{4,52},{5,53},{6,54},{7,55},{8,24},{9,... | collective-permute-start | bytes 786440 | tf_op jit(solution)/shard_map/ppermute | solution.py:362
  70.9 12.3 %collective-permute-start.22 = (bf16[128,1024]{1,0:T(8,128)(2,1)S(1)}, bf16[128,1024]{1,0:T(8,128)(2,1)S(1)}, u32[]{:S(2)}, u32[]{:S(2)}) collective-permute-start(bf16[128,1024]{1,0:T(8,128)(2,1)S(1)} %tie.5.refs_8_), channel_id=1, source_target_pairs={{0,64},{1,65},{2,66},{3,67},{4,68},{5,69},{6,198},{7,199},{8,72},{... | collective-permute-start | bytes 786440 | tf_op jit(solution)/shard_map/ppermute | solution.py:362
  83.1 6.7 %collective-permute-start.25 = (bf16[128,1024]{1,0:T(8,128)(2,1)S(1)}, bf16[128,1024]{1,0:T(8,128)(2,1)S(1)}, u32[]{:S(2)}, u32[]{:S(2)}) collective-permute-start(bf16[128,1024]{1,0:T(8,128)(2,1)S(1)} %collective-permute-done.24.refs_11_), channel_id=1, source_target_pairs={{0,192},{1,193},{2,194},{3,195},{4,196},{5,197},{6,198},{7,199},{8... | collective-permute-start | bytes 786440 | tf_op jit(solution)/shard_map/ppermute | solution.py:362
  83.1 12.1 %collective-permute-start.21 = (bf16[128,1024]{1,0:T(8,128)(2,1)S(1)}, bf16[128,1024]{1,0:T(8,128)(2,1)S(1)}, u32[]{:S(2)}, u32[]{:S(2)}) collective-permute-start(bf16[128,1024]{1,0:T(8,128)(2,1)S(1)} %tie.4.refs_6_), channel_id=1, source_target_pairs={{0,192},{1,193},{2,194},{3,195},{4,196},{5,197},{6,198},{7,199},{8... | collective-permute-start | bytes 786440 | tf_op jit(solution)/shard_map/ppermute | solution.py:362
  83.1 17.7 %collective-permute-start.23 = (bf16[128,1024]{1,0:T(8,128)(2,1)S(1)}, bf16[128,1024]{1,0:T(8,128)(2,1)S(1)}, u32[]{:S(2)}, u32[]{:S(2)}) collective-permute-start(bf16[128,1024]{1,0:T(8,128)(2,1)S(1)} %collective-permute-done.22.refs_9_), channel_id=1, source_target_pairs={{0,64},{1,65},{2,66},{3,67},{4,68},{5,69},{6,198},{7,199},{8,72},{... | collective-permute-start | bytes 786440 | tf_op jit(solution)/shard_map/ppermute | solution.py:362
  89.8 17.6 %collective-permute-start.28 = (bf16[128,1024]{1,0:T(8,128)(2,1)S(1)}, bf16[128,1024]{1,0:T(8,128)(2,1)S(1)}, u32[]{:S(2)}, u32[]{:S(2)}) collective-permute-start(bf16[128,1024]{1,0:T(8,128)(2,1)S(1)} %collective-permute-done.25.refs_12_), channel_id=1, source_target_pairs={{0,192},{1,193},{2,194},{3,195},{4,196},{5,197},{6,198},{7,199},{8... | collective-permute-start | bytes 786440 | tf_op jit(solution)/shard_map/ppermute | solution.py:362
  101.0 29.0 %collective-permute-start.26 = (bf16[1664,1024]{1,0:T(8,128)(2,1)S(1)}, bf16[1664,1024]{1,0:T(8,128)(2,1)S(1)}, u32[]{:S(2)}, u32[]{:S(2)}) collective-permute-start(bf16[1664,1024]{1,0:T(8,128)(2,1)S(1)} %stack.4.refs_4_), channel_id=1, source_target_pairs={{0,1},{1,0},{2,3},{3,2},{4,5},{5,4},{6,7},{7,6},{8,9},{9,8},{10,11... | collective-permute-start | bytes 10223624 | tf_op jit(solution)/shard_map/ppermute | solution.py:362
  107.4 8.8 %collective-permute-start.27 = (bf16[128,1024]{1,0:T(8,128)(2,1)S(1)}, bf16[128,1024]{1,0:T(8,128)(2,1)S(1)}, u32[]{:S(2)}, u32[]{:S(2)}) collective-permute-start(bf16[128,1024]{1,0:T(8,128)(2,1)S(1)} %collective-permute-done.23.refs_10_), channel_id=1, source_target_pairs={{0,64},{1,65},{2,66},{3,67},{4,68},{5,69},{6,198},{7,199},{8,72},{... | collective-permute-start | bytes 786440 | tf_op jit(solution)/shard_map/ppermute | solution.py:362
  107.4 14.4 %collective-permute-start.29 = (bf16[128,1024]{1,0:T(8,128)(2,1)S(1)}, bf16[128,1024]{1,0:T(8,128)(2,1)S(1)}, u32[]{:S(2)}, u32[]{:S(2)}) collective-permute-start(bf16[128,1024]{1,0:T(8,128)(2,1)S(1)} %collective-permute-done.28.refs_1_), channel_id=1, source_target_pairs={{0,192},{1,193},{2,194},{3,195},{4,196},{5,197},{6,198},{7,199},{8... | collective-permute-start | bytes 786440 | tf_op jit(solution)/shard_map/ppermute | solution.py:362
  121.9 8.1 %collective-permute-start.30 = (bf16[384,1024]{1,0:T(8,128)(2,1)S(1)}, bf16[384,1024]{1,0:T(8,128)(2,1)S(1)}, u32[]{:S(2)}, u32[]{:S(2)}) collective-permute-start(bf16[384,1024]{1,0:T(8,128)(2,1)S(1)} %stack.5.refs_5_), channel_id=1, source_target_pairs={{0,1},{1,0},{2,3},{3,2},{4,5},{5,4},{6,7},{7,6},{8,9},{9,8},{10,11... | collective-permute-start | bytes 2359304 | tf_op jit(solution)/shard_map/ppermute | solution.py:362
  123.1 2.7 %collective-permute-start.19 = (bf16[512,512]{1,0:T(8,128)(2,1)S(1)}, bf16[512,512]{1,0:T(8,128)(2,1)S(1)}, u32[]{:S(2)}, u32[]{:S(2)}) collective-permute-start(bf16[512,512]{1,0:T(8,128)(2,1)S(1)} %get-tuple-element.27), channel_id=1, source_target_pairs={{0,1},{1,0},{2,3},{3,2},{4,5},{5,4},{6,7},{7,6},{8,9},{9,8},{10,11... | collective-permute-start | bytes 1572872 | tf_op jit(solution)/shard_map/ppermute | solution.py:362
  123.2 3.3 %collective-permute-start.20 = (bf16[512,512]{1,0:T(8,128)(2,1)S(1)}, bf16[512,512]{1,0:T(8,128)(2,1)S(1)}, u32[]{:S(2)}, u32[]{:S(2)}) collective-permute-start(bf16[512,512]{1,0:T(8,128)(2,1)S(1)} %get-tuple-element.28), channel_id=1, source_target_pairs={{0,1},{1,0},{2,3},{3,2},{4,5},{5,4},{6,7},{7,6},{8,9},{9,8},{10,11... | collective-permute-start | bytes 1572872 | tf_op jit(solution)/shard_map/ppermute | solution.py:362
